TPU v7x, 32 devices: a whole 2x2x4 slice. The times are simulated.
32 devices in a mesh: groups: 2 (over y), clus: 16 (over z, x, core).
Axes of the slice: x: 2, y: 2, z: 4, core: 2. Of those that a mesh axis runs over, the one named last changes fastest.
Arguments:
- sources: bfloat16 [256, 8, 256], P(('groups', 'clus')), parts along dimension 0, may hold values from -6 to 6
- near_blocks: bfloat16 [256, 3, 256, 256], P(('groups', 'clus')), parts along dimension 0, may hold values from -0.21875 to 0.21875
- far_u: bfloat16 [8192, 32, 256], P(('groups', 'clus')), parts along dimension 0, may hold values from -0.375 to 0.375
- far_v: bfloat16 [8192, 32, 256], P(('groups', 'clus')), parts along dimension 0, may hold values from -0.1875 to 0.1875
- send_list: int32 [32, 16, 2], P(('groups', 'clus')), parts along dimension 0, may hold values from -1 to 7, as said below
- far_slot: int32 [8192], P(('groups', 'clus')), parts along dimension 0, may hold values from 0 to 31, as said below
- ret_list: int32 [32, 16, 2], P(('groups', 'clus')), parts along dimension 0, may hold values from -1 to 7, as said below
- ret_slot: int32 [8192], P(('groups', 'clus')), parts along dimension 0, may hold values from 0 to 31, as said below
Outputs:
- adjoint_field: float32 [256, 8, 256], P(('groups', 'clus')), parts along dimension 0
There are 2 independent parts, one for each index of `groups`. A program takes and returns all parts, laid end to end along the dimension named above; each array names one. Nothing has to cross between parts.
Inputs may be any that keep to these rules, and one draw needn't show every extreme that they name: Each row send_list[p, d, :] holds its valid local cluster indices, all different, in its first entries and -1 after them; at least one is valid; one receiving device gets 2 clusters from every sender. `far_slot`: every block names a valid entry of send_list for its owner. Each row ret_list[d, q, :] holds its valid local cluster indices, all different, in its first entries and -1 after them; at least one is valid; one device is served 2 clusters by every block owner. `ret_slot`: every block names a valid entry of ret_list for its owner.
All inputs are finite; a program needn't handle non-finite values.
Results may differ from a plain program's by a relative error of at most 0.0021.
Values may be sent and summed in bfloat16 or wider, within the bound.
No kernel may reach another device: no remote copies, remote signals or barrier semaphores. Data moves between devices by JAX's collectives and lax.ppermute only.
A program may use at most 64 MiB of HBM per device.

v0:
```python
import jax
import jax.numpy as jnp
from jax import lax
from jax.sharding import PartitionSpec as P


def padded_2(x, sides, width):
    for axis, dim in sides:
        devices, length = (lax.axis_size(axis), x.shape[dim])
        up = [(i, (i + 1) % devices) for i in range(devices - 1)]
        down = [(j, i) for i, j in up]
        last = lax.slice_in_dim(x, length - width, length, axis=dim)
        first = lax.slice_in_dim(x, 0, width, axis=dim)
        before = lax.ppermute(last, axis, up)
        after = lax.ppermute(first, axis, down)
        x = jnp.concatenate([before, x, after], axis=dim)
    return x


def body(sources, near_blocks, far_u, far_v, send_list, far_slot, ret_list, ret_slot):
    local_count = sources.shape[0]
    peer_count = lax.axis_size("clus")
    capacity = send_list.shape[2]
    padded = padded_2(sources, (("clus", 0),), 1)
    stacked = jnp.stack([padded[offset : offset + local_count] for offset in range(3)], axis=1)
    near_part = jnp.einsum(
        "covl,colk->cvk", stacked, near_blocks, preferred_element_type=jnp.float32
    )
    index_list = send_list[0]
    alive = index_list >= 0
    outgoing = jnp.where(alive[:, :, None, None], sources[jnp.maximum(index_list, 0)], 0)
    incoming = lax.all_to_all(outgoing, "clus", split_axis=0, concat_axis=0, tiled=True)
    flattened = incoming.reshape(peer_count * capacity, incoming.shape[2], incoming.shape[3])
    picked = flattened[far_slot]
    coefficients = jnp.einsum(
        "bvl,brl->bvr", picked, far_u, preferred_element_type=jnp.float32
    ).astype(jnp.bfloat16)
    contributions = jnp.einsum(
        "bvr,brl->bvl", coefficients, far_v, preferred_element_type=jnp.float32
    )
    return_list = ret_list[0]
    dest_peer = ret_slot // capacity
    dest_rank = ret_slot % capacity
    dest_rows = dest_peer * local_count + return_list[dest_peer, dest_rank]
    buffered = jax.ops.segment_sum(contributions, dest_rows, num_segments=peer_count * local_count)
    far_part = lax.psum_scatter(buffered, "clus", scatter_dimension=0, tiled=True)
    return near_part + far_part


def solution(mesh):
    placed = (
        P(("groups", "clus"), None, None),
        P(("groups", "clus"), None, None, None),
        P(("groups", "clus"), None, None),
        P(("groups", "clus"), None, None),
        P(("groups", "clus"), None, None),
        P(("groups", "clus")),
        P(("groups", "clus"), None, None),
        P(("groups", "clus")),
    )
    return jax.shard_map(
        body,
        mesh=mesh,
        in_specs=placed,
        out_specs=P(("groups", "clus"), None, None),
        check_vma=False,
    )
```

profile of v0, /device:TPU:0, one launch (start us, length us, event | category | flops | bytes accessed | tf_op | source)
XLA Modules:
  0.0 131.1 jit_solution(16118318709611956775)
XLA Ops:
  6.5 0.0 copy-start
  6.5 0.8 broadcast_maximum_fusion
  7.4 0.8 compare_bitcast_fusion
  8.2 0.1 copy.12
  8.3 0.1 reshape.31
  8.4 0.1 copy.11
  8.5 1.3 %gather_fusion.1 = bf16[32,8,256]{2,1,0:T(8,128)(2,1)S(1)} fusion(bf16[8,8,256]{2,1,0:T(8,128)(2,1)} %param.8, s32[1024]{0:T(1024)S(1)} %pad_clamp_fusion.1), kind=kCustom, calls=%fused_computation.1 | custom fusion | bytes 262272 | tf_op jit(solution)/shard_map/gather | solution.py:31
  9.8 0.8 broadcast_select_fusion
  10.6 7.4 %all-to-all-start = ((bf16[16,2,8,256]{3,2,1,0:T(8,128)(2,1)}), bf16[16,2,8,256]{3,2,1,0:T(8,128)(2,1)S(1)}, u32[]{:S(2)}, u32[]{:S(2)}) async-start(bf16[16,2,8,256]{3,2,1,0:T(8,128)(2,1)} %broadcast_select_fusion), calls=%async_computation | async-start | bytes 262144 | tf_op jit(solution)/shard_map/all_to_all | solution.py:32
  17.9 0.0 reduce-scatter.2.cloned.1.call-start
  18.0 0.7 fusion.11
  18.7 0.7 compare_select_fusion
  19.4 2.3 %gather_fusion = s32[256]{0:T(256)S(1)} fusion(s32[16,2]{0,1:T(2,128)} %bitcast.19, s32[256]{0:T(256)S(1)} %get-tuple-element.5), kind=kCustom, calls=%fused_computation | custom fusion | bytes 4096 | tf_op jit(solution)/shard_map/gather | solution.py:44
  21.7 4.2 %all-to-all-done = bf16[16,2,8,256]{3,2,1,0:T(8,128)(2,1)S(1)} async-done(((bf16[16,2,8,256]{3,2,1,0:T(8,128)(2,1)}), bf16[16,2,8,256]{3,2,1,0:T(8,128)(2,1)S(1)}, u32[]{:S(2)}, u32[]{:S(2)}) %all-to-all-start) | async-done | bytes 131104 | tf_op jit(solution)/shard_map/all_to_all | solution.py:32
  25.9 1.8 %gather_fusion.2 = bf16[256,8,256]{2,1,0:T(8,128)(2,1)} fusion(bf16[32,8,256]{2,1,0:T(8,128)(2,1)S(1)} %bitcast.20, s32[1024]{0:T(1024)S(1)} %pad_clamp_fusion), kind=kCustom, calls=%fused_computation.2 | custom fusion | bytes 2098176 | tf_op jit(solution)/shard_map/gather | solution.py:34
  27.6 6.9 %fusion = f32[256,8,256]{2,1,0:T(8,128)} fusion(bf16[256,32,256]{2,1,0:T(8,128)(2,1)} %param.11, bf16[256,8,256]{2,1,0:T(8,128)(2,1)} %gather_fusion.2, bf16[256,32,256]{2,1,0:T(8,128)(2,1)} %param.10), kind=kOutput, calls=%fused_computation.5 | convolution fusion | flops 67174400 | bytes 11534336 | tf_op jit(solution)/shard_map/bvr,brl->bvl/dot_general | solution.py:38
  34.5 0.0 copy-start.1
  34.5 1.1 broadcast_in_dim.29
  35.5 31.4 %scatter_fusion = f32[128,8,256]{2,1,0:T(8,128)} fusion(f32[128,8,256]{2,1,0:T(8,128)} %broadcast_in_dim.29, s32[256]{0:T(256)S(1)} %multiply_add_fusion, f32[256,8,256]{2,1,0:T(8,128)} %fusion), kind=kCustom, calls=%fused_computation.3 | custom fusion | flops 524288 | bytes 6292480 | tf_op jit(solution)/shard_map/scatter-add | solution.py:45
  67.0 0.0 reduce-scatter.2.cloned.1.call-update
  67.0 0.0 copy-done.1
  67.0 1.3 collective-permute-start
  68.3 1.3 collective-permute-start.1
  69.6 0.0 collective-permute-done
  69.6 1.7 %collective-permute-done.1 = bf16[1,8,256]{2,1,0:T(8,128)(2,1)S(1)} collective-permute-done((bf16[1,8,256]{2,1,0:T(8,128)(2,1)S(1)}, bf16[1,8,256]{2,1,0:T(8,128)(2,1)S(1)}, u32[]{:S(2)}, u32[]{:S(2)}) %collective-permute-start.1) | collective-permute-done | bytes 4128 | tf_op jit(solution)/shard_map/ppermute | solution.py:15
  71.4 50.8 %reduce-scatter.2.cloned.1.call-done = f32[8,8,256]{2,1,0:T(8,128)} async-done(((f32[128,8,256]{2,1,0:T(8,128)}), f32[8,8,256]{2,1,0:T(8,128)}) %reduce-scatter.2.cloned.1.call-update) | async-done | bytes 65552 | tf_op jit(solution)/shard_map/reduce_scatter | solution.py:46
  122.2 0.0 copy-done
  122.2 2.0 %fusion.1 = f32[8,8,256]{2,1,0:T(8,128)} fusion(f32[8,8,256]{2,1,0:T(8,128)} %reduce-scatter.2.cloned.1.call-done, bf16[8,3,256,256]{3,2,1,0:T(8,128)(2,1)S(1)} %copy-done, bf16[8,1,8,256]{3,2,1,0:T(8,128)(2,1)S(1)} %get-tuple-element.8, bf16[8,1,8,256]{3,2,1,0:T(8,128)(2,1)S(1)} %bitcast.21, bf16[8,1,8,256]{3,2,1,0:T(8,128)(2,1)S(1)} %get-tuple-element.7), kind=kOutput, calls=%fused_computation.7 | convolution fusion | flops 25280512 | bytes 3375104 | tf_op jit(solution)/shard_map/covl,colk->cvk/dot_general | solution.py:26
  (5 shorter events, 0.0 us)
Async XLA Ops:
  6.5 115.7 %copy-start = (bf16[8,3,256,256]{3,2,1,0:T(8,128)(2,1)S(1)}, bf16[8,3,256,256]{3,2,1,0:T(8,128)(2,1)}, u32[]{:S(2)}) copy-start(bf16[8,3,256,256]{3,2,1,0:T(8,128)(2,1)} %param.9) | copy-start | bytes 9437188
  10.6 15.3 %all-to-all-start = ((bf16[16,2,8,256]{3,2,1,0:T(8,128)(2,1)}), bf16[16,2,8,256]{3,2,1,0:T(8,128)(2,1)S(1)}, u32[]{:S(2)}, u32[]{:S(2)}) async-start(bf16[16,2,8,256]{3,2,1,0:T(8,128)(2,1)} %broadcast_select_fusion), calls=%async_computation | async-start | bytes 262144 | tf_op jit(solution)/shard_map/all_to_all | solution.py:32
  17.9 104.3 %reduce-scatter.2.cloned.1.call-start = ((), (), s32[]{:S(2)}) async-start(), calls=%async_computation.2 | async-start | bytes 1114112 | tf_op jit(solution)/shard_map/reduce_scatter | solution.py:46
  34.5 32.5 %copy-start.1 = (bf16[8,8,256]{2,1,0:T(8,128)(2,1)S(1)}, bf16[8,8,256]{2,1,0:T(8,128)(2,1)}, u32[]{:S(2)}) copy-start(bf16[8,8,256]{2,1,0:T(8,128)(2,1)} %param.8) | copy-start | bytes 98308
  67.0 2.6 %collective-permute-start = (bf16[1,8,256]{2,1,0:T(8,128)(2,1)S(1)}, bf16[1,8,256]{2,1,0:T(8,128)(2,1)S(1)}, u32[]{:S(2)}, u32[]{:S(2)}) collective-permute-start(bf16[1,8,256]{2,1,0:T(8,128)(2,1)S(1)} %get-tuple-element.9), channel_id=1, source_target_pairs={{0,1},{1,2},{2,3},{3,4},{4,5},{5,6},{6,7},{7,8},{8,9},{9,10},{10,1... | collective-permute-start | bytes 12296 | tf_op jit(solution)/shard_map/ppermute | solution.py:14
  68.3 3.1 %collective-permute-start.1 = (bf16[1,8,256]{2,1,0:T(8,128)(2,1)S(1)}, bf16[1,8,256]{2,1,0:T(8,128)(2,1)S(1)}, u32[]{:S(2)}, u32[]{:S(2)}) collective-permute-start(bf16[1,8,256]{2,1,0:T(8,128)(2,1)S(1)} %get-tuple-element.10), channel_id=1, source_target_pairs={{1,0},{2,1},{3,2},{4,3},{5,4},{6,5},{7,6},{8,7},{9,8},{10,9},{11,1... | collective-permute-start | bytes 12296 | tf_op jit(solution)/shard_map/ppermute | solution.py:15
Sparse Core Ops, SparseCore 0:
  67.1 55.0 reduce-scatter.1
where the time goes:
time: 132 us; the launch traced here: 131 us
  waiting for transfers between devices  56.8 us (43%)
  other arithmetic  35.2 us (27%)
  between operations  13.5 us (10%)
  starting transfers between devices  9.98 us (8%)
  matrix products  8.85 us (7%)
  local copies, waits for them, and re-layouts  6.76 us (5%)
    reduce_scatter x1, waiting for transfers between devices, body(): lax.psum_scatter(buffered, 'clus', scatter_dimension=0, tiled=True)  50.8 us
    scatter-add x1, other arithmetic, body(): jax.ops.segment_sum(contributions, dest_rows, num_segments=peer_count * l...  31.4 us
    all_to_all x1, starting transfers between devices, body(): lax.all_to_all(outgoing, 'clus', split_axis=0, concat_axis=0, tiled=True)  7.36 us
    dot_general x1, matrix products, body(): jnp.einsum('bvr,brl->bvl', coefficients, far_v, preferred_element_type=jn...  6.86 us
    all_to_all x1, waiting for transfers between devices, body(): lax.all_to_all(outgoing, 'clus', split_axis=0, concat_axis=0, tiled=True)  4.16 us
  transfers between devices with their start and end apart: 4, of which 3 were waited for; matrix products, arithmetic and copies ran while one was open for 3% of the time, Pallas kernels for 0%

commit v1 on v0

v1 whole, which is shorter than its diff:
```python
import jax
import jax.numpy as jnp
from jax import lax
from jax.experimental import pallas as pl
from jax.experimental.pallas import tpu as pltpu
from jax.sharding import PartitionSpec as P

VMEM = pl.BlockSpec(memory_space=pltpu.VMEM)
SMEM = pl.BlockSpec(memory_space=pltpu.SMEM)


def pack_kernel(send_ref, ret_ref, src_ref, out_ref):
    clusters, nvec, leaf = src_ref.shape
    cap, peers = send_ref.shape
    me = lax.axis_index("clus")
    half = (nvec, leaf // cap)
    first = src_ref[0].astype(jnp.float32)
    last = src_ref[clusters - 1].astype(jnp.float32)

    def step(p, carry):
        rows = [
            src_ref[jnp.maximum(send_ref[k, p], 0)].astype(jnp.float32) for k in range(cap)
        ]
        rows.append(jnp.where(p > me, last, first))
        rows.append(
            jnp.concatenate(
                [jnp.full(half, ret_ref[k, p].astype(jnp.float32)) for k in range(cap)], axis=1
            )
        )
        out_ref[p] = jnp.concatenate(rows, axis=0).astype(out_ref.dtype)
        return carry

    lax.fori_loop(0, peers, step, 0, unroll=min(peers, 16))


def far_kernel(slot_ref, dest_ref, x_ref, u_ref, v_ref, out_ref, xf, coef, acc):
    peers = x_ref.shape[0]
    slots, nvec, leaf = xf.shape
    cap = slots // peers
    blocks, rank, _ = u_ref.shape
    group = leaf // rank
    ways = acc.shape[0]

    def widen(p, carry):
        rows = x_ref[p, : cap * nvec, :].astype(jnp.float32)
        for k in range(cap):
            xf[p * cap + k] = rows[k * nvec : (k + 1) * nvec]
        return carry

    lax.fori_loop(0, peers, widen, 0, unroll=min(peers, 16))
    acc[...] = jnp.zeros_like(acc)
    owner = lax.broadcasted_iota(jnp.int32, (nvec, leaf), 1) // rank

    def project(g, carry):
        picked = jnp.concatenate(
            [xf[slot_ref[g * group + i]] for i in range(group)], axis=0
        ).astype(jnp.bfloat16)
        u = u_ref[pl.ds(g * group, group)].reshape(group * rank, leaf)
        full = lax.dot_general(
            picked, u, (((1,), (1,)), ((), ())), preferred_element_type=jnp.float32
        )
        kept = full[:nvec]
        for i in range(1, group):
            kept = jnp.where(owner == i, full[i * nvec : (i + 1) * nvec], kept)
        coef[g] = kept
        return carry

    def expand(g, carry):
        kept = coef[g]
        spread = jnp.concatenate(
            [jnp.where(owner == i, kept, 0.0) for i in range(group)], axis=0
        ).astype(jnp.bfloat16)
        v = v_ref[pl.ds(g * group, group)].reshape(group * rank, leaf)
        terms = jnp.dot(spread, v, preferred_element_type=jnp.float32)
        for i in range(group):
            at = dest_ref[g * group + i]
            acc[i % ways, at] += terms[i * nvec : (i + 1) * nvec]
        return carry

    lax.fori_loop(0, blocks // group, project, 0, unroll=4)
    lax.fori_loop(0, blocks // group, expand, 0, unroll=4)

    def narrow(p, carry):
        rows = []
        for k in range(cap):
            total = acc[0, p * cap + k]
            for w in range(1, ways):
                total += acc[w, p * cap + k]
            rows.append(total)
        out_ref[p] = jnp.concatenate(rows, axis=0).astype(out_ref.dtype)
        return carry

    lax.fori_loop(0, peers, narrow, 0, unroll=min(peers, 16))


def near_kernel(src_ref, near_ref, x_ref, near_out, place_out, place):
    clusters, nvec, leaf = src_ref.shape
    peers = x_ref.shape[0]
    cap = place.shape[0] // (peers * nvec)
    me = lax.axis_index("clus")
    edge = slice(cap * nvec, (cap + 1) * nvec)
    before = x_ref[jnp.maximum(me - 1, 0)][edge].astype(jnp.float32)
    after = x_ref[jnp.minimum(me + 1, peers - 1)][edge].astype(jnp.float32)
    before = jnp.where(me > 0, before, 0.0).astype(jnp.bfloat16)
    after = jnp.where(me < peers - 1, after, 0.0).astype(jnp.bfloat16)
    rows = [before] + [src_ref[s] for s in range(clusters)] + [after]
    for s in range(clusters):
        total = jnp.dot(rows[s], near_ref[s, 0], preferred_element_type=jnp.float32)
        for o in range(1, 3):
            total += jnp.dot(rows[s + o], near_ref[s, o], preferred_element_type=jnp.float32)
        near_out[s * nvec : (s + 1) * nvec] = total

    lane = lax.broadcasted_iota(jnp.int32, (nvec, leaf // cap), 1)
    sub = lax.broadcasted_iota(jnp.int32, (nvec, leaf // cap), 0)
    cluster = jnp.where(lane % nvec == sub, lane // nvec, -2).astype(jnp.float32)

    def step(p, carry):
        meta = x_ref[p, (cap + 1) * nvec :, :].astype(jnp.float32)
        for k in range(cap):
            width = leaf // cap
            place[pl.ds((p * cap + k) * nvec, nvec)] = jnp.where(
                meta[:, k * width : (k + 1) * width] == cluster, 1.0, 0.0
            )
        return carry

    lax.fori_loop(0, peers, step, 0, unroll=min(peers, 16))
    place_out[...] = place[...].T[: clusters * nvec].astype(jnp.bfloat16)


def sum_kernel(back_ref, near_ref, place_ref, out_ref):
    peers, rows, leaf = back_ref.shape
    clusters, nvec, _ = out_ref.shape
    terms = back_ref[...].reshape(peers * rows, leaf)
    total = near_ref[...] + jnp.dot(
        place_ref[...], terms, preferred_element_type=jnp.float32
    )
    out_ref[...] = total.reshape(clusters, nvec, leaf)


def cost(flops, moved):
    return pl.CostEstimate(flops=flops, bytes_accessed=moved, transcendentals=0)


def body(sources, near_blocks, far_u, far_v, send_list, far_slot, ret_list, ret_slot):
    clusters, nvec, leaf = sources.shape
    _, peers, cap = send_list.shape
    blocks, rank, _ = far_u.shape
    slots = peers * cap
    group = leaf // rank
    params = pltpu.CompilerParams(vmem_limit_bytes=24 * 2**20)
    message = pl.pallas_call(
        pack_kernel,
        out_shape=jax.ShapeDtypeStruct((peers, (cap + 2) * nvec, leaf), jnp.bfloat16),
        in_specs=[SMEM, SMEM, VMEM],
        out_specs=VMEM,
        compiler_params=params,
        cost_estimate=cost(0, peers * (cap + 2) * nvec * leaf * 2),
        name="pack",
    )(send_list[0].T, ret_list[0].T, sources)
    incoming = lax.all_to_all(message, "clus", split_axis=0, concat_axis=0, tiled=True)
    returns = pl.pallas_call(
        far_kernel,
        out_shape=jax.ShapeDtypeStruct((peers, cap * nvec, leaf), jnp.bfloat16),
        in_specs=[SMEM, SMEM, VMEM, VMEM, VMEM],
        out_specs=VMEM,
        scratch_shapes=[
            pltpu.VMEM((slots, nvec, leaf), jnp.float32),
            pltpu.VMEM((blocks // group, nvec, leaf), jnp.float32),
            pltpu.VMEM((4 if peers <= 16 else 1, slots, nvec, leaf), jnp.float32),
        ],
        compiler_params=params,
        cost_estimate=cost(4 * blocks * 8 * nvec * leaf * rank, 4 * blocks * rank * leaf),
        name="far",
    )(far_slot, ret_slot, incoming, far_u, far_v)
    back = lax.all_to_all(returns, "clus", split_axis=0, concat_axis=0, tiled=True)
    near_part, place = pl.pallas_call(
        near_kernel,
        out_shape=(
            jax.ShapeDtypeStruct((clusters * nvec, leaf), jnp.float32),
            jax.ShapeDtypeStruct((clusters * nvec, slots * nvec), jnp.bfloat16),
        ),
        in_specs=[VMEM, VMEM, VMEM],
        out_specs=(VMEM, VMEM),
        scratch_shapes=[pltpu.VMEM((slots * nvec, leaf // cap), jnp.float32)],
        compiler_params=params,
        cost_estimate=cost(2 * 3 * clusters * nvec * leaf * leaf, 6 * clusters * leaf * leaf),
        name="near",
    )(sources, near_blocks, incoming)
    return pl.pallas_call(
        sum_kernel,
        out_shape=jax.ShapeDtypeStruct((clusters, nvec, leaf), jnp.float32),
        in_specs=[VMEM, VMEM, VMEM],
        out_specs=VMEM,
        compiler_params=params,
        cost_estimate=cost(2 * clusters * nvec * slots * nvec * leaf, slots * nvec * leaf * 2),
        name="sum",
    )(back, near_part, place)


def solution(mesh):
    placed = (
        P(("groups", "clus"), None, None),
        P(("groups", "clus"), None, None, None),
        P(("groups", "clus"), None, None),
        P(("groups", "clus"), None, None),
        P(("groups", "clus"), None, None),
        P(("groups", "clus")),
        P(("groups", "clus"), None, None),
        P(("groups", "clus")),
    )
    return jax.shard_map(
        body,
        mesh=mesh,
        in_specs=placed,
        out_specs=P(("groups", "clus"), None, None),
        check_vma=False,
    )
```

time: 132 us -> 45.9 us (0.35)
  waiting for transfers between devices: 56.8 us -> 5.37 us
  other arithmetic: 35.2 us -> 0 us
  blocking collectives: 0 us -> 17.2 us
  between operations: 13.5 us -> 0.05 us
  matrix products: 8.85 us -> 0 us
  Pallas kernels: 0 us -> 7.75 us
  starting transfers between devices: 9.98 us -> 3.51 us
  local copies, waits for them, and re-layouts: 6.76 us -> 11.4 us
    reduce_scatter x1 -> x0, waiting for transfers between devices: 50.8 us -> none  [body(): lax.psum_scatter(buffered, 'clus', scatter_dimension=0, tiled=True)]
    scatter-add x1 -> x0, other arithmetic: 31.4 us -> none  [body(): jax.ops.segment_sum(contributions, dest_rows, num_segments=peer_count * l...]
    all_to_all x0 -> x1, blocking collectives: none -> 17.2 us  [body(): lax.all_to_all(message, 'clus', split_axis=0, concat_axis=0, tiled=True)]
    unnamed x4 -> x26, local copies, waits for them, and re-layouts: 0.01 us -> 11.4 us
    dot_general x2 -> x0, matrix products: 8.85 us -> none  [the longest x1 6.86 us: body(): jnp.einsum('bvr,brl->bvl', coefficients, far_v, preferred_element_type=jn...]
    pallas_call x0 -> x4, Pallas kernels: none -> 7.75 us  [the longest x1 5.82 us: body(): pl.pallas_call(far_kernel, out_shape=jax.ShapeDtypeStruct((peers, cap * n...]
    gather x3 -> x0, local copies, waits for them, and re-layouts: 5.41 us -> none  [the longest x1 2.33 us: body(): dest_rows = dest_peer * local_count + return_list[dest_peer, dest_rank]]
    all_to_all x1, starting transfers between devices: 7.36 us -> 3.51 us  [body(): lax.all_to_all(returns, 'clus', split_axis=0, concat_axis=0, tiled=True)]
  transfers between devices with their start and end apart: 4 -> 1, of which waited for: 3 -> 1; matrix products, arithmetic and copies ran while one was open for 3% -> 0% of each run, Pallas kernels for 0% -> 1%
where the time goes in v1:
time: 45.9 us; the launch traced here: 45.3 us
  blocking collectives  17.2 us (37%)
  local copies, waits for them, and re-layouts  11.4 us (25%)
  Pallas kernels  7.75 us (17%)
  waiting for transfers between devices  5.37 us (12%)
  starting transfers between devices  3.51 us (8%)
    all_to_all x1, blocking collectives, body(): lax.all_to_all(message, 'clus', split_axis=0, concat_axis=0, tiled=True)  17.2 us
    unnamed x26, local copies, waits for them, and re-layouts  11.4 us
    pallas_call x1, Pallas kernels, body(): pl.pallas_call(far_kernel, out_shape=jax.ShapeDtypeStruct((peers, cap * n...  5.82 us
    all_to_all x1, waiting for transfers between devices, body(): lax.all_to_all(returns, 'clus', split_axis=0, concat_axis=0, tiled=True)  5.37 us
    all_to_all x1, starting transfers between devices, body(): lax.all_to_all(returns, 'clus', split_axis=0, concat_axis=0, tiled=True)  3.51 us
  transfers between devices with their start and end apart: 1, of which 1 were waited for; matrix products, arithmetic and copies ran while one was open for 0% of the time, Pallas kernels for 1%

profile of v1, /device:TPU:0, one launch (start us, length us, event | category | flops | bytes accessed | tf_op | source)
XLA Modules:
  0.0 45.3 jit_solution(529115940498973285)
XLA Ops:
  0.0 0.0 copy-start.3
  0.0 0.8 %copy-done.3 = bf16[8,8,256]{2,1,0:T(8,128)(2,1)S(1)} copy-done((bf16[8,8,256]{2,1,0:T(8,128)(2,1)S(1)}, bf16[8,8,256]{2,1,0:T(8,128)(2,1)}, u32[]{:S(2)}) %copy-start.3) | copy-done | bytes 32792
  0.8 0.0 copy-start.9
  0.8 0.7 %copy-done.9 = s32[1,16,2]{1,2,0:T(2,128)S(1)} copy-done((s32[1,16,2]{1,2,0:T(2,128)S(1)}, s32[1,16,2]{1,2,0:T(2,128)}, u32[]{:S(2)}) %copy-start.9) | copy-done | bytes 152
  1.4 0.0 copy-start.10
  1.4 0.7 %copy-done.10 = s32[1,16,2]{1,2,0:T(2,128)S(1)} copy-done((s32[1,16,2]{1,2,0:T(2,128)S(1)}, s32[1,16,2]{1,2,0:T(2,128)}, u32[]{:S(2)}) %copy-start.10) | copy-done | bytes 152
  2.1 0.6 %pack.1 = bf16[16,32,256]{2,1,0:T(8,128)(2,1)S(1)} custom-call(s32[2,16]{1,0:T(2,128)S(1)} %bitcast.6, s32[2,16]{1,0:T(2,128)S(1)} %bitcast.7, bf16[8,8,256]{2,1,0:T(8,128)(2,1)S(1)} %copy-done.3), custom_call_target="tpu_custom_call" | custom-call | bytes 262144 | tf_op jit(solution)/shard_map/pack/pallas_call | solution.py:151
  2.8 17.2 %all_to_all.10.x_ref = bf16[16,32,256]{2,1,0:T(8,128)(2,1)S(1)} all-to-all(bf16[16,32,256]{2,1,0:T(8,128)(2,1)S(1)} %pack.1), channel_id=1, replica_groups=mesh['groups'=2,'clus'=16] {'clus'}, dimensions={0} | all-to-all | bytes 524288 | tf_op jit(solution)/shard_map/all_to_all | solution.py:160
  20.0 0.0 copy-start
  20.0 2.2 %copy-done = bf16[256,32,256]{2,1,0:T(8,128)(2,1)S(1)} copy-done((bf16[256,32,256]{2,1,0:T(8,128)(2,1)S(1)}, bf16[256,32,256]{2,1,0:T(8,128)(2,1)}, u32[]{:S(2)}) %copy-start) | copy-done | bytes 4194328
  22.2 0.0 copy-start.1
  22.2 2.2 %copy-done.1 = bf16[256,32,256]{2,1,0:T(8,128)(2,1)S(1)} copy-done((bf16[256,32,256]{2,1,0:T(8,128)(2,1)S(1)}, bf16[256,32,256]{2,1,0:T(8,128)(2,1)}, u32[]{:S(2)}) %copy-start.1) | copy-done | bytes 4194328
  24.3 0.0 copy-start.11
  24.3 0.7 %copy-done.11 = s32[256]{0:T(256)S(1)} copy-done((s32[256]{0:T(256)S(1)}, s32[256]{0:T(256)}, u32[]{:S(2)}) %copy-start.11) | copy-done | bytes 1048
  25.0 0.0 copy-start.12
  25.0 0.7 %copy-done.12 = s32[256]{0:T(256)S(1)} copy-done((s32[256]{0:T(256)S(1)}, s32[256]{0:T(256)}, u32[]{:S(2)}) %copy-start.12) | copy-done | bytes 1048
  25.7 0.0 copy-start.2
  25.7 5.8 %far.1 = bf16[16,16,256]{2,1,0:T(8,128)(2,1)} custom-call(s32[256]{0:T(256)S(1)} %copy-done.11, s32[256]{0:T(256)S(1)} %copy-done.12, bf16[16,32,256]{2,1,0:T(8,128)(2,1)S(1)} %all_to_all.10.x_ref, bf16[256,32,256]{2,1,0:T(8,128)(2,1)S(1)} %copy-done, bf16[256,32,256]{2,1,0:T(8,128)(2,1)S(1)} %copy-done.1), custom_call_target="tpu_custom_call" | custom-call | flops 536870912 | bytes 8388608 | tf_op jit(solution)/shard_map/far/pallas_call | solution.py:161
  31.5 3.5 %all-to-all-start.1 = ((bf16[16,16,256]{2,1,0:T(8,128)(2,1)}), bf16[16,16,256]{2,1,0:T(8,128)(2,1)S(1)}, u32[]{:S(2)}, u32[]{:S(2)}) async-start(bf16[16,16,256]{2,1,0:T(8,128)(2,1)} %far.1), calls=%async_computation.1 | async-start | bytes 262144 | tf_op jit(solution)/shard_map/all_to_all | solution.py:175
  35.0 0.0 copy-done.2
  35.1 0.0 copy-start.4
  35.1 0.7 %copy-done.4 = bf16[8,8,256]{2,1,0:T(8,128)(2,1)S(1)} copy-done((bf16[8,8,256]{2,1,0:T(8,128)(2,1)S(1)}, bf16[8,8,256]{2,1,0:T(8,128)(2,1)}, u32[]{:S(2)}) %copy-start.4) | copy-done | bytes 32792
  35.8 0.5 %near.1 = (f32[64,256]{1,0:T(8,128)S(1)}, bf16[64,256]{1,0:T(8,128)(2,1)S(1)}) custom-call(bf16[8,8,256]{2,1,0:T(8,128)(2,1)S(1)} %copy-done.4, bf16[8,3,256,256]{3,2,1,0:T(8,128)(2,1)S(1)} %copy-done.2, bf16[16,32,256]{2,1,0:T(8,128)(2,1)S(1)} %all_to_all.10.x_ref), custom_call_target="tpu_custom_call" | custom-call | flops 25165824 | bytes 3145728 | tf_op jit(solution)/shard_map/near/pallas_call | solution.py:176
  36.3 0.0 copy-start.5
  36.3 0.6 %copy-done.5 = f32[64,256]{1,0:T(8,128)} copy-done((f32[64,256]{1,0:T(8,128)}, f32[64,256]{1,0:T(8,128)S(1)}, u32[]{:S(2)}) %copy-start.5) | copy-done | bytes 65560
  37.0 0.0 copy-start.7
  37.0 0.6 %copy-done.7 = bf16[64,256]{1,0:T(8,128)(2,1)} copy-done((bf16[64,256]{1,0:T(8,128)(2,1)}, bf16[64,256]{1,0:T(8,128)(2,1)S(1)}, u32[]{:S(2)}) %copy-start.7) | copy-done | bytes 32792
  37.6 5.4 %all-to-all-done.1.back_ref = bf16[16,16,256]{2,1,0:T(8,128)(2,1)S(1)} async-done(((bf16[16,16,256]{2,1,0:T(8,128)(2,1)}), bf16[16,16,256]{2,1,0:T(8,128)(2,1)S(1)}, u32[]{:S(2)}, u32[]{:S(2)}) %all-to-all-start.1) | async-done | bytes 131104 | tf_op jit(solution)/shard_map/all_to_all | solution.py:175
  42.9 0.0 copy-start.6
  42.9 0.8 %copy-done.6 = f32[64,256]{1,0:T(8,128)S(1)} copy-done((f32[64,256]{1,0:T(8,128)S(1)}, f32[64,256]{1,0:T(8,128)}, u32[]{:S(2)}) %copy-start.6) | copy-done | bytes 65560
  43.8 0.0 copy-start.8
  43.8 0.8 %copy-done.8 = bf16[64,256]{1,0:T(8,128)(2,1)S(1)} copy-done((bf16[64,256]{1,0:T(8,128)(2,1)S(1)}, bf16[64,256]{1,0:T(8,128)(2,1)}, u32[]{:S(2)}) %copy-start.8) | copy-done | bytes 32792
  44.5 0.8 %sum.1 = f32[8,8,256]{2,1,0:T(8,128)} custom-call(bf16[16,16,256]{2,1,0:T(8,128)(2,1)S(1)} %all-to-all-done.1.back_ref, f32[64,256]{1,0:T(8,128)S(1)} %copy-done.6, bf16[64,256]{1,0:T(8,128)(2,1)S(1)} %copy-done.8), custom_call_target="tpu_custom_call" | custom-call | flops 8388608 | bytes 131072 | tf_op jit(solution)/shard_map/sum/pallas_call | solution.py:189
Async XLA Ops:
  0.0 0.8 %copy-start.3 = (bf16[8,8,256]{2,1,0:T(8,128)(2,1)S(1)}, bf16[8,8,256]{2,1,0:T(8,128)(2,1)}, u32[]{:S(2)}) copy-start(bf16[8,8,256]{2,1,0:T(8,128)(2,1)} %src_ref.3) | copy-start | bytes 98308
  0.8 0.7 %copy-start.9 = (s32[1,16,2]{1,2,0:T(2,128)S(1)}, s32[1,16,2]{1,2,0:T(2,128)}, u32[]{:S(2)}) copy-start(s32[1,16,2]{1,2,0:T(2,128)} %param.12) | copy-start | bytes 388
  1.4 0.7 %copy-start.10 = (s32[1,16,2]{1,2,0:T(2,128)S(1)}, s32[1,16,2]{1,2,0:T(2,128)}, u32[]{:S(2)}) copy-start(s32[1,16,2]{1,2,0:T(2,128)} %param.14) | copy-start | bytes 388
  20.0 2.2 %copy-start = (bf16[256,32,256]{2,1,0:T(8,128)(2,1)S(1)}, bf16[256,32,256]{2,1,0:T(8,128)(2,1)}, u32[]{:S(2)}) copy-start(bf16[256,32,256]{2,1,0:T(8,128)(2,1)} %u_ref.1) | copy-start | bytes 12582916
  22.2 2.2 %copy-start.1 = (bf16[256,32,256]{2,1,0:T(8,128)(2,1)S(1)}, bf16[256,32,256]{2,1,0:T(8,128)(2,1)}, u32[]{:S(2)}) copy-start(bf16[256,32,256]{2,1,0:T(8,128)(2,1)} %v_ref.1) | copy-start | bytes 12582916
  24.3 0.7 %copy-start.11 = (s32[256]{0:T(256)S(1)}, s32[256]{0:T(256)}, u32[]{:S(2)}) copy-start(s32[256]{0:T(256)} %slot_ref.1) | copy-start | bytes 3076
  25.0 0.7 %copy-start.12 = (s32[256]{0:T(256)S(1)}, s32[256]{0:T(256)}, u32[]{:S(2)}) copy-start(s32[256]{0:T(256)} %dest_ref.1) | copy-start | bytes 3076
  25.7 9.3 %copy-start.2 = (bf16[8,3,256,256]{3,2,1,0:T(8,128)(2,1)S(1)}, bf16[8,3,256,256]{3,2,1,0:T(8,128)(2,1)}, u32[]{:S(2)}) copy-start(bf16[8,3,256,256]{3,2,1,0:T(8,128)(2,1)} %near_ref.1) | copy-start | bytes 9437188
  31.5 11.4 %all-to-all-start.1 = ((bf16[16,16,256]{2,1,0:T(8,128)(2,1)}), bf16[16,16,256]{2,1,0:T(8,128)(2,1)S(1)}, u32[]{:S(2)}, u32[]{:S(2)}) async-start(bf16[16,16,256]{2,1,0:T(8,128)(2,1)} %far.1), calls=%async_computation.1 | async-start | bytes 262144 | tf_op jit(solution)/shard_map/all_to_all | solution.py:175
  35.1 0.8 %copy-start.4 = (bf16[8,8,256]{2,1,0:T(8,128)(2,1)S(1)}, bf16[8,8,256]{2,1,0:T(8,128)(2,1)}, u32[]{:S(2)}) copy-start(bf16[8,8,256]{2,1,0:T(8,128)(2,1)} %src_ref.3) | copy-start | bytes 98308
  36.3 0.6 %copy-start.5 = (f32[64,256]{1,0:T(8,128)}, f32[64,256]{1,0:T(8,128)S(1)}, u32[]{:S(2)}) copy-start(f32[64,256]{1,0:T(8,128)S(1)} %get-tuple-element.7.near_ref) | copy-start | bytes 196612
  37.0 0.6 %copy-start.7 = (bf16[64,256]{1,0:T(8,128)(2,1)}, bf16[64,256]{1,0:T(8,128)(2,1)S(1)}, u32[]{:S(2)}) copy-start(bf16[64,256]{1,0:T(8,128)(2,1)S(1)} %get-tuple-element.8.place_ref) | copy-start | bytes 98308
  42.9 0.8 %copy-start.6 = (f32[64,256]{1,0:T(8,128)S(1)}, f32[64,256]{1,0:T(8,128)}, u32[]{:S(2)}) copy-start(f32[64,256]{1,0:T(8,128)} %copy-done.5) | copy-start | bytes 196612
  43.8 0.8 %copy-start.8 = (bf16[64,256]{1,0:T(8,128)(2,1)S(1)}, bf16[64,256]{1,0:T(8,128)(2,1)}, u32[]{:S(2)}) copy-start(bf16[64,256]{1,0:T(8,128)(2,1)} %copy-done.7) | copy-start | bytes 98308

commit v2 on v1

v2 whole, which is shorter than its diff:
```python
import jax
import jax.numpy as jnp
from jax import lax
from jax.experimental import pallas as pl
from jax.experimental.pallas import tpu as pltpu
from jax.sharding import PartitionSpec as P

VMEM = pl.BlockSpec(memory_space=pltpu.VMEM)
HBM = pl.BlockSpec(memory_space=pltpu.HBM)
CHUNKS = 4


def fetch(pairs, sems):
    copies = [pltpu.make_async_copy(a, b, sems.at[i]) for i, (a, b) in enumerate(pairs)]
    for copy in copies:
        copy.start()
    return copies


def halves(x):
    w = x.shape[1] // 2
    return [x[:, :w], x[:, w:]]


def pack_kernel(send_hbm, ret_hbm, src_hbm, out_ref, send_ref, ret_ref, src_ref, sems):
    for copy in fetch([(send_hbm, send_ref), (ret_hbm, ret_ref), (src_hbm, src_ref)], sems):
        copy.wait()
    clusters, nvec, leaf = src_ref.shape
    cap, peers = send_ref.shape
    me = lax.axis_index("clus")
    first = src_ref[0].astype(jnp.float32)
    last = src_ref[clusters - 1].astype(jnp.float32)

    def step(p, carry):
        rows = []
        for k in range(cap):
            rows += halves(src_ref[jnp.maximum(send_ref[k, p], 0)].astype(jnp.float32))
        rows += halves(jnp.where(p > me, last, first))
        rows.append(
            jnp.concatenate(
                [
                    jnp.full((nvec // cap, leaf // 2), ret_ref[k, p].astype(jnp.float32))
                    for k in range(cap)
                ],
                axis=0,
            )
        )
        out_ref[p] = jnp.concatenate(rows, axis=0).astype(out_ref.dtype)
        return carry

    lax.fori_loop(0, peers, step, 0, unroll=min(peers, 16))


def joined(rows, nvec):
    return jnp.concatenate([rows[:nvec], rows[nvec:]], axis=1)


def far_kernel(
    slot_hbm, dest_hbm, x_ref, u_hbm, v_hbm, out_ref, slot_ref, dest_ref, u_ref, v_ref, xf, *rest
):
    accs, sems = rest[:-1], rest[-1]
    peers = x_ref.shape[0]
    slots, nvec, leaf = xf.shape
    cap = slots // peers
    blocks, rank, _ = u_ref.shape
    group = leaf // rank
    size = blocks // CHUNKS
    pairs = [(slot_hbm, slot_ref), (dest_hbm, dest_ref)]
    for c in range(CHUNKS):
        part = pl.ds(c * size, size)
        pairs += [(u_hbm.at[part], u_ref.at[part]), (v_hbm.at[part], v_ref.at[part])]
    copies = fetch(pairs, sems)

    def widen(p, carry):
        rows = x_ref[p].astype(jnp.float32)
        for k in range(cap):
            xf[p * cap + k] = joined(rows[2 * k * nvec : 2 * (k + 1) * nvec], nvec)
        return carry

    lax.fori_loop(0, peers, widen, 0, unroll=min(peers, 16))
    for acc in accs:
        acc[...] = jnp.zeros_like(acc)
    owner = lax.broadcasted_iota(jnp.int32, (nvec, leaf), 1) // rank
    copies[0].wait()
    copies[1].wait()
    for g in range(blocks // group):
        if g * group % size == 0:
            copies[2 + 2 * (g * group // size)].wait()
            copies[3 + 2 * (g * group // size)].wait()
        picked = jnp.concatenate(
            [xf[slot_ref[g * group + i]] for i in range(group)], axis=0
        ).astype(jnp.bfloat16)
        u = u_ref[g * group : (g + 1) * group].reshape(group * rank, leaf)
        full = lax.dot_general(
            picked, u, (((1,), (1,)), ((), ())), preferred_element_type=jnp.float32
        )
        kept = full[:nvec]
        for i in range(1, group):
            kept = jnp.where(owner == i, full[i * nvec : (i + 1) * nvec], kept)
        spread = jnp.concatenate(
            [jnp.where(owner == i, kept, 0.0) for i in range(group)], axis=0
        ).astype(jnp.bfloat16)
        v = v_ref[g * group : (g + 1) * group].reshape(group * rank, leaf)
        terms = jnp.dot(spread, v, preferred_element_type=jnp.float32)
        for i in range(group):
            accs[i % len(accs)][dest_ref[g * group + i]] += terms[i * nvec : (i + 1) * nvec]

    def narrow(p, carry):
        rows = []
        for k in range(cap):
            total = accs[0][p * cap + k]
            for acc in accs[1:]:
                total += acc[p * cap + k]
            rows.append(total)
        out_ref[p] = jnp.concatenate(rows, axis=0).astype(out_ref.dtype)
        return carry

    lax.fori_loop(0, peers, narrow, 0, unroll=min(peers, 16))


def near_kernel(src_ref, near_hbm, x_ref, near_out, place_out, near_ref, place, sems):
    clusters, nvec, leaf = src_ref.shape
    peers = x_ref.shape[0]
    cap = place.shape[0] // (peers * nvec)
    copies = fetch([(near_hbm.at[s], near_ref.at[s]) for s in range(clusters)], sems)

    width = leaf // 2
    lane = lax.broadcasted_iota(jnp.int32, (nvec, width), 1)
    sub = lax.broadcasted_iota(jnp.int32, (nvec, width), 0)
    cluster = jnp.where(lane % nvec == sub, lane // nvec, -2).astype(jnp.float32)

    def step(p, carry):
        meta = x_ref[p, 2 * (cap + 1) * nvec :, :].astype(jnp.float32)
        for k in range(cap):
            at = jnp.broadcast_to(meta[k * nvec // cap : k * nvec // cap + 1], (nvec, width))
            place[pl.ds((p * cap + k) * nvec, nvec)] = jnp.where(at == cluster, 1.0, 0.0)
        return carry

    lax.fori_loop(0, peers, step, 0, unroll=min(peers, 16))
    place_out[...] = place[...].T[: clusters * nvec].astype(jnp.bfloat16)

    me = lax.axis_index("clus")
    edge = slice(2 * cap * nvec, 2 * (cap + 1) * nvec)
    before = joined(x_ref[jnp.maximum(me - 1, 0)][edge].astype(jnp.float32), nvec)
    after = joined(x_ref[jnp.minimum(me + 1, peers - 1)][edge].astype(jnp.float32), nvec)
    before = jnp.where(me > 0, before, 0.0).astype(jnp.bfloat16)
    after = jnp.where(me < peers - 1, after, 0.0).astype(jnp.bfloat16)
    rows = [before] + [src_ref[s] for s in range(clusters)] + [after]
    for s in range(clusters):
        copies[s].wait()
        total = jnp.dot(rows[s], near_ref[s, 0], preferred_element_type=jnp.float32)
        for o in range(1, 3):
            total += jnp.dot(rows[s + o], near_ref[s, o], preferred_element_type=jnp.float32)
        near_out[s * nvec : (s + 1) * nvec] = total


def sum_kernel(back_ref, near_ref, place_ref, out_ref):
    peers, rows, leaf = back_ref.shape
    clusters, nvec, _ = out_ref.shape
    terms = back_ref[...].reshape(peers * rows, leaf)
    total = near_ref[...] + jnp.dot(
        place_ref[...], terms, preferred_element_type=jnp.float32
    )
    out_ref[...] = total.reshape(clusters, nvec, leaf)


def cost(flops, moved):
    return pl.CostEstimate(flops=flops, bytes_accessed=moved, transcendentals=0)


def body(sources, near_blocks, far_u, far_v, send_list, far_slot, ret_list, ret_slot):
    clusters, nvec, leaf = sources.shape
    _, peers, cap = send_list.shape
    blocks, rank, _ = far_u.shape
    slots = peers * cap
    rows = 2 * (cap + 1) * nvec + nvec
    params = pltpu.CompilerParams(vmem_limit_bytes=24 * 2**20)
    message = pl.pallas_call(
        pack_kernel,
        out_shape=jax.ShapeDtypeStruct((peers, rows, leaf // 2), jnp.bfloat16),
        in_specs=[HBM, HBM, HBM],
        out_specs=VMEM,
        scratch_shapes=[
            pltpu.SMEM((cap, peers), jnp.int32),
            pltpu.SMEM((cap, peers), jnp.int32),
            pltpu.VMEM((clusters, nvec, leaf), jnp.bfloat16),
            pltpu.SemaphoreType.DMA((3,)),
        ],
        compiler_params=params,
        cost_estimate=cost(0, peers * rows * leaf),
        name="pack",
    )(send_list[0].T, ret_list[0].T, sources)
    incoming = lax.all_to_all(message, "clus", split_axis=0, concat_axis=0, tiled=True)
    returns = pl.pallas_call(
        far_kernel,
        out_shape=jax.ShapeDtypeStruct((peers, cap * nvec, leaf), jnp.bfloat16),
        in_specs=[HBM, HBM, VMEM, HBM, HBM],
        out_specs=VMEM,
        scratch_shapes=[
            pltpu.SMEM((blocks,), jnp.int32),
            pltpu.SMEM((blocks,), jnp.int32),
            pltpu.VMEM((blocks, rank, leaf), jnp.bfloat16),
            pltpu.VMEM((blocks, rank, leaf), jnp.bfloat16),
            pltpu.VMEM((slots, nvec, leaf), jnp.float32),
        ]
        + [pltpu.VMEM((slots, nvec, leaf), jnp.float32)] * (4 if peers <= 16 else 1)
        + [pltpu.SemaphoreType.DMA((2 + 2 * CHUNKS,))],
        compiler_params=params,
        cost_estimate=cost(4 * blocks * 8 * nvec * leaf * rank, 4 * blocks * rank * leaf),
        name="far",
    )(far_slot, ret_slot, incoming, far_u, far_v)
    back = lax.all_to_all(returns, "clus", split_axis=0, concat_axis=0, tiled=True)
    near_part, place = pl.pallas_call(
        near_kernel,
        out_shape=(
            jax.ShapeDtypeStruct((clusters * nvec, leaf), jnp.float32),
            jax.ShapeDtypeStruct((clusters * nvec, slots * nvec), jnp.bfloat16),
        ),
        in_specs=[VMEM, HBM, VMEM],
        out_specs=(VMEM, VMEM),
        scratch_shapes=[
            pltpu.VMEM(near_blocks.shape, jnp.bfloat16),
            pltpu.VMEM((slots * nvec, leaf // 2), jnp.float32),
            pltpu.SemaphoreType.DMA((clusters,)),
        ],
        compiler_params=params,
        cost_estimate=cost(2 * 3 * clusters * nvec * leaf * leaf, 6 * clusters * leaf * leaf),
        name="near",
    )(sources, near_blocks, incoming)
    return pl.pallas_call(
        sum_kernel,
        out_shape=jax.ShapeDtypeStruct((clusters, nvec, leaf), jnp.float32),
        in_specs=[VMEM, VMEM, VMEM],
        out_specs=VMEM,
        compiler_params=params,
        cost_estimate=cost(2 * clusters * nvec * slots * nvec * leaf, slots * nvec * leaf * 2),
        name="sum",
    )(back, near_part, place)


def solution(mesh):
    placed = (
        P(("groups", "clus"), None, None),
        P(("groups", "clus"), None, None, None),
        P(("groups", "clus"), None, None),
        P(("groups", "clus"), None, None),
        P(("groups", "clus"), None, None),
        P(("groups", "clus")),
        P(("groups", "clus"), None, None),
        P(("groups", "clus")),
    )
    return jax.shard_map(
        body,
        mesh=mesh,
        in_specs=placed,
        out_specs=P(("groups", "clus"), None, None),
        check_vma=False,
    )
```

time: 45.9 us -> 47.9 us (1.044)
  Pallas kernels: 7.75 us -> 13.2 us
  waiting for transfers between devices: 5.37 us -> 3.24 us
  local copies, waits for them, and re-layouts: 11.4 us -> 10.7 us
  blocking collectives: 17.2 us -> 16.7 us
    pallas_call x1, Pallas kernels: 0.51 us -> 3.39 us  [body(): pl.pallas_call(near_kernel, out_shape=(jax.ShapeDtypeStruct((clusters * n...]
    pallas_call x1, Pallas kernels: 5.82 us -> 8.31 us  [body(): pl.pallas_call(far_kernel, out_shape=jax.ShapeDtypeStruct((peers, cap * n...]
    all_to_all x1, waiting for transfers between devices: 5.37 us -> 3.24 us  [body(): lax.all_to_all(returns, 'clus', split_axis=0, concat_axis=0, tiled=True)]
    unnamed x26, local copies, waits for them, and re-layouts: 11.4 us -> 10.7 us
    all_to_all x1, blocking collectives: 17.2 us -> 16.7 us  [body(): lax.all_to_all(message, 'clus', split_axis=0, concat_axis=0, tiled=True)]
  transfers between devices with their start and end apart: 1 -> 1, of which waited for: 1 -> 1; matrix products, arithmetic and copies ran while one was open for 0% -> 0% of each run, Pallas kernels for 1% -> 7%
where the time goes in v2:
time: 47.9 us; the launch traced here: 47.3 us
  blocking collectives  16.7 us (35%)
  Pallas kernels  13.2 us (28%)
  local copies, waits for them, and re-layouts  10.7 us (22%)
  starting transfers between devices  3.52 us (7%)
  waiting for transfers between devices  3.24 us (7%)
    all_to_all x1, blocking collectives, body(): lax.all_to_all(message, 'clus', split_axis=0, concat_axis=0, tiled=True)  16.7 us
    unnamed x26, local copies, waits for them, and re-layouts  10.7 us
    pallas_call x1, Pallas kernels, body(): pl.pallas_call(far_kernel, out_shape=jax.ShapeDtypeStruct((peers, cap * n...  8.31 us
    all_to_all x1, starting transfers between devices, body(): lax.all_to_all(returns, 'clus', split_axis=0, concat_axis=0, tiled=True)  3.52 us
    pallas_call x1, Pallas kernels, body(): pl.pallas_call(near_kernel, out_shape=(jax.ShapeDtypeStruct((clusters * n...  3.39 us
    all_to_all x1, waiting for transfers between devices, body(): lax.all_to_all(returns, 'clus', split_axis=0, concat_axis=0, tiled=True)  3.24 us
  transfers between devices with their start and end apart: 1, of which 1 were waited for; matrix products, arithmetic and copies ran while one was open for 0% of the time, Pallas kernels for 7%

profile of v2, /device:TPU:0, one launch (start us, length us, event | category | flops | bytes accessed | tf_op | source)
XLA Modules:
  0.0 47.3 jit_solution(7796099552559147943)
XLA Ops:
  0.0 0.0 copy-start.3
  0.0 0.8 %copy-done.3 = bf16[8,8,256]{2,1,0:T(8,128)(2,1)S(1)} copy-done((bf16[8,8,256]{2,1,0:T(8,128)(2,1)S(1)}, bf16[8,8,256]{2,1,0:T(8,128)(2,1)}, u32[]{:S(2)}) %copy-start.3) | copy-done | bytes 32792
  0.8 0.0 copy-start.9
  0.8 0.7 %copy-done.9 = s32[1,16,2]{1,2,0:T(2,128)S(1)} copy-done((s32[1,16,2]{1,2,0:T(2,128)S(1)}, s32[1,16,2]{1,2,0:T(2,128)}, u32[]{:S(2)}) %copy-start.9) | copy-done | bytes 152
  1.4 0.0 copy-start.10
  1.4 0.7 %copy-done.10 = s32[1,16,2]{1,2,0:T(2,128)S(1)} copy-done((s32[1,16,2]{1,2,0:T(2,128)S(1)}, s32[1,16,2]{1,2,0:T(2,128)}, u32[]{:S(2)}) %copy-start.10) | copy-done | bytes 152
  2.1 0.7 %pack.1 = bf16[16,56,128]{2,1,0:T(8,128)(2,1)S(1)} custom-call(s32[2,16]{1,0:T(2,128)S(1)} %bitcast.6, s32[2,16]{1,0:T(2,128)S(1)} %bitcast.7, bf16[8,8,256]{2,1,0:T(8,128)(2,1)S(1)} %copy-done.3), custom_call_target="tpu_custom_call" | custom-call | bytes 229376 | tf_op jit(solution)/shard_map/pack/pallas_call | solution.py:178
  2.8 16.7 %all_to_all.10.x_ref = bf16[16,56,128]{2,1,0:T(8,128)(2,1)S(1)} all-to-all(bf16[16,56,128]{2,1,0:T(8,128)(2,1)S(1)} %pack.1), channel_id=1, replica_groups=mesh['groups'=2,'clus'=16] {'clus'}, dimensions={0} | all-to-all | bytes 458752 | tf_op jit(solution)/shard_map/all_to_all | solution.py:193
  19.5 0.0 copy-start
  19.5 2.2 %copy-done = bf16[256,32,256]{2,1,0:T(8,128)(2,1)S(1)} copy-done((bf16[256,32,256]{2,1,0:T(8,128)(2,1)S(1)}, bf16[256,32,256]{2,1,0:T(8,128)(2,1)}, u32[]{:S(2)}) %copy-start) | copy-done | bytes 4194328
  21.7 0.0 copy-start.1
  21.7 2.2 %copy-done.1 = bf16[256,32,256]{2,1,0:T(8,128)(2,1)S(1)} copy-done((bf16[256,32,256]{2,1,0:T(8,128)(2,1)S(1)}, bf16[256,32,256]{2,1,0:T(8,128)(2,1)}, u32[]{:S(2)}) %copy-start.1) | copy-done | bytes 4194328
  23.8 0.0 copy-start.11
  23.8 0.7 %copy-done.11 = s32[256]{0:T(256)S(1)} copy-done((s32[256]{0:T(256)S(1)}, s32[256]{0:T(256)}, u32[]{:S(2)}) %copy-start.11) | copy-done | bytes 1048
  24.5 0.0 copy-start.12
  24.5 0.7 %copy-done.12 = s32[256]{0:T(256)S(1)} copy-done((s32[256]{0:T(256)S(1)}, s32[256]{0:T(256)}, u32[]{:S(2)}) %copy-start.12) | copy-done | bytes 1048
  25.2 0.0 copy-start.2
  25.2 0.0 copy-start.4
  25.2 8.3 %far.1 = bf16[16,16,256]{2,1,0:T(8,128)(2,1)} custom-call(s32[256]{0:T(256)S(1)} %copy-done.11, s32[256]{0:T(256)S(1)} %copy-done.12, bf16[16,56,128]{2,1,0:T(8,128)(2,1)S(1)} %all_to_all.10.x_ref, bf16[256,32,256]{2,1,0:T(8,128)(2,1)S(1)} %copy-done, bf16[256,32,256]{2,1,0:T(8,128)(2,1)S(1)} %copy-done.1), custom_call_target="tpu_custom_call" | custom-call | flops 536870912 | bytes 8388608 | tf_op jit(solution)/shard_map/far/pallas_call | solution.py:194
  33.5 3.5 %all-to-all-start.1 = ((bf16[16,16,256]{2,1,0:T(8,128)(2,1)}), bf16[16,16,256]{2,1,0:T(8,128)(2,1)S(1)}, u32[]{:S(2)}, u32[]{:S(2)}) async-start(bf16[16,16,256]{2,1,0:T(8,128)(2,1)} %far.1), calls=%async_computation.1 | async-start | bytes 262144 | tf_op jit(solution)/shard_map/all_to_all | solution.py:212
  37.1 0.0 copy-done.2
  37.1 0.0 copy-done.4
  37.1 3.4 %near.1 = (f32[64,256]{1,0:T(8,128)S(1)}, bf16[64,256]{1,0:T(8,128)(2,1)S(1)}) custom-call(bf16[8,8,256]{2,1,0:T(8,128)(2,1)S(1)} %copy-done.4, bf16[8,3,256,256]{3,2,1,0:T(8,128)(2,1)S(1)} %copy-done.2, bf16[16,56,128]{2,1,0:T(8,128)(2,1)S(1)} %all_to_all.10.x_ref), custom_call_target="tpu_custom_call" | custom-call | flops 25165824 | bytes 3145728 | tf_op jit(solution)/shard_map/near/pallas_call | solution.py:213
  40.5 0.0 copy-start.5
  40.5 0.6 %copy-done.5 = f32[64,256]{1,0:T(8,128)} copy-done((f32[64,256]{1,0:T(8,128)}, f32[64,256]{1,0:T(8,128)S(1)}, u32[]{:S(2)}) %copy-start.5) | copy-done | bytes 65560
  41.1 0.0 copy-start.7
  41.1 0.6 %copy-done.7 = bf16[64,256]{1,0:T(8,128)(2,1)} copy-done((bf16[64,256]{1,0:T(8,128)(2,1)}, bf16[64,256]{1,0:T(8,128)(2,1)S(1)}, u32[]{:S(2)}) %copy-start.7) | copy-done | bytes 32792
  41.7 3.2 %all-to-all-done.1.back_ref = bf16[16,16,256]{2,1,0:T(8,128)(2,1)S(1)} async-done(((bf16[16,16,256]{2,1,0:T(8,128)(2,1)}), bf16[16,16,256]{2,1,0:T(8,128)(2,1)S(1)}, u32[]{:S(2)}, u32[]{:S(2)}) %all-to-all-start.1) | async-done | bytes 131104 | tf_op jit(solution)/shard_map/all_to_all | solution.py:212
  45.0 0.0 copy-start.6
  45.0 0.8 %copy-done.6 = f32[64,256]{1,0:T(8,128)S(1)} copy-done((f32[64,256]{1,0:T(8,128)S(1)}, f32[64,256]{1,0:T(8,128)}, u32[]{:S(2)}) %copy-start.6) | copy-done | bytes 65560
  45.8 0.0 copy-start.8
  45.8 0.8 %copy-done.8 = bf16[64,256]{1,0:T(8,128)(2,1)S(1)} copy-done((bf16[64,256]{1,0:T(8,128)(2,1)S(1)}, bf16[64,256]{1,0:T(8,128)(2,1)}, u32[]{:S(2)}) %copy-start.8) | copy-done | bytes 32792
  46.6 0.8 %sum.1 = f32[8,8,256]{2,1,0:T(8,128)} custom-call(bf16[16,16,256]{2,1,0:T(8,128)(2,1)S(1)} %all-to-all-done.1.back_ref, f32[64,256]{1,0:T(8,128)S(1)} %copy-done.6, bf16[64,256]{1,0:T(8,128)(2,1)S(1)} %copy-done.8), custom_call_target="tpu_custom_call" | custom-call | flops 8388608 | bytes 131072 | tf_op jit(solution)/shard_map/sum/pallas_call | solution.py:230
Async XLA Ops:
  0.0 0.8 %copy-start.3 = (bf16[8,8,256]{2,1,0:T(8,128)(2,1)S(1)}, bf16[8,8,256]{2,1,0:T(8,128)(2,1)}, u32[]{:S(2)}) copy-start(bf16[8,8,256]{2,1,0:T(8,128)(2,1)} %src_ref.1) | copy-start | bytes 98308
  0.8 0.7 %copy-start.9 = (s32[1,16,2]{1,2,0:T(2,128)S(1)}, s32[1,16,2]{1,2,0:T(2,128)}, u32[]{:S(2)}) copy-start(s32[1,16,2]{1,2,0:T(2,128)} %param.12) | copy-start | bytes 388
  1.4 0.7 %copy-start.10 = (s32[1,16,2]{1,2,0:T(2,128)S(1)}, s32[1,16,2]{1,2,0:T(2,128)}, u32[]{:S(2)}) copy-start(s32[1,16,2]{1,2,0:T(2,128)} %param.14) | copy-start | bytes 388
  19.5 2.2 %copy-start = (bf16[256,32,256]{2,1,0:T(8,128)(2,1)S(1)}, bf16[256,32,256]{2,1,0:T(8,128)(2,1)}, u32[]{:S(2)}) copy-start(bf16[256,32,256]{2,1,0:T(8,128)(2,1)} %u_hbm.1) | copy-start | bytes 12582916
  21.7 2.2 %copy-start.1 = (bf16[256,32,256]{2,1,0:T(8,128)(2,1)S(1)}, bf16[256,32,256]{2,1,0:T(8,128)(2,1)}, u32[]{:S(2)}) copy-start(bf16[256,32,256]{2,1,0:T(8,128)(2,1)} %v_hbm.1) | copy-start | bytes 12582916
  23.8 0.7 %copy-start.11 = (s32[256]{0:T(256)S(1)}, s32[256]{0:T(256)}, u32[]{:S(2)}) copy-start(s32[256]{0:T(256)} %slot_hbm.1) | copy-start | bytes 3076
  24.5 0.7 %copy-start.12 = (s32[256]{0:T(256)S(1)}, s32[256]{0:T(256)}, u32[]{:S(2)}) copy-start(s32[256]{0:T(256)} %dest_hbm.1) | copy-start | bytes 3076
  25.2 11.9 %copy-start.2 = (bf16[8,3,256,256]{3,2,1,0:T(8,128)(2,1)S(1)}, bf16[8,3,256,256]{3,2,1,0:T(8,128)(2,1)}, u32[]{:S(2)}) copy-start(bf16[8,3,256,256]{3,2,1,0:T(8,128)(2,1)} %near_hbm.1) | copy-start | bytes 9437188
  25.2 11.9 %copy-start.4 = (bf16[8,8,256]{2,1,0:T(8,128)(2,1)S(1)}, bf16[8,8,256]{2,1,0:T(8,128)(2,1)}, u32[]{:S(2)}) copy-start(bf16[8,8,256]{2,1,0:T(8,128)(2,1)} %src_ref.1) | copy-start | bytes 98308
  33.5 11.4 %all-to-all-start.1 = ((bf16[16,16,256]{2,1,0:T(8,128)(2,1)}), bf16[16,16,256]{2,1,0:T(8,128)(2,1)S(1)}, u32[]{:S(2)}, u32[]{:S(2)}) async-start(bf16[16,16,256]{2,1,0:T(8,128)(2,1)} %far.1), calls=%async_computation.1 | async-start | bytes 262144 | tf_op jit(solution)/shard_map/all_to_all | solution.py:212
  40.5 0.6 %copy-start.5 = (f32[64,256]{1,0:T(8,128)}, f32[64,256]{1,0:T(8,128)S(1)}, u32[]{:S(2)}) copy-start(f32[64,256]{1,0:T(8,128)S(1)} %get-tuple-element.7.near_ref) | copy-start | bytes 196612
  41.1 0.6 %copy-start.7 = (bf16[64,256]{1,0:T(8,128)(2,1)}, bf16[64,256]{1,0:T(8,128)(2,1)S(1)}, u32[]{:S(2)}) copy-start(bf16[64,256]{1,0:T(8,128)(2,1)S(1)} %get-tuple-element.8.place_ref) | copy-start | bytes 98308
  45.0 0.8 %copy-start.6 = (f32[64,256]{1,0:T(8,128)S(1)}, f32[64,256]{1,0:T(8,128)}, u32[]{:S(2)}) copy-start(f32[64,256]{1,0:T(8,128)} %copy-done.5) | copy-start | bytes 196612
  45.8 0.8 %copy-start.8 = (bf16[64,256]{1,0:T(8,128)(2,1)S(1)}, bf16[64,256]{1,0:T(8,128)(2,1)}, u32[]{:S(2)}) copy-start(bf16[64,256]{1,0:T(8,128)(2,1)} %copy-done.7) | copy-start | bytes 98308

commit v3 on v2

--- a/solution.py
+++ b/solution.py
@@ -56,7 +56,19 @@
 
 
 def far_kernel(
-    slot_hbm, dest_hbm, x_ref, u_hbm, v_hbm, out_ref, slot_ref, dest_ref, u_ref, v_ref, xf, *rest
+    slot_hbm,
+    dest_hbm,
+    x_hbm,
+    u_hbm,
+    v_hbm,
+    out_ref,
+    slot_ref,
+    dest_ref,
+    x_ref,
+    u_ref,
+    v_ref,
+    xf,
+    *rest,
 ):
     accs, sems = rest[:-1], rest[-1]
     peers = x_ref.shape[0]
@@ -65,11 +77,14 @@
     blocks, rank, _ = u_ref.shape
     group = leaf // rank
     size = blocks // CHUNKS
-    pairs = [(slot_hbm, slot_ref), (dest_hbm, dest_ref)]
+    pairs = [(x_hbm, x_ref), (slot_hbm, slot_ref), (dest_hbm, dest_ref)]
     for c in range(CHUNKS):
         part = pl.ds(c * size, size)
         pairs += [(u_hbm.at[part], u_ref.at[part]), (v_hbm.at[part], v_ref.at[part])]
     copies = fetch(pairs, sems)
+    for acc in accs:
+        acc[...] = jnp.zeros_like(acc)
+    copies[0].wait()
 
     def widen(p, carry):
         rows = x_ref[p].astype(jnp.float32)
@@ -78,15 +93,13 @@
         return carry
 
     lax.fori_loop(0, peers, widen, 0, unroll=min(peers, 16))
-    for acc in accs:
-        acc[...] = jnp.zeros_like(acc)
     owner = lax.broadcasted_iota(jnp.int32, (nvec, leaf), 1) // rank
-    copies[0].wait()
     copies[1].wait()
+    copies[2].wait()
     for g in range(blocks // group):
         if g * group % size == 0:
-            copies[2 + 2 * (g * group // size)].wait()
             copies[3 + 2 * (g * group // size)].wait()
+            copies[4 + 2 * (g * group // size)].wait()
         picked = jnp.concatenate(
             [xf[slot_ref[g * group + i]] for i in range(group)], axis=0
         ).astype(jnp.bfloat16)
@@ -118,12 +131,10 @@
     lax.fori_loop(0, peers, narrow, 0, unroll=min(peers, 16))
 
 
-def near_kernel(src_ref, near_hbm, x_ref, near_out, place_out, near_ref, place, sems):
+def near_kernel(src_ref, near_ref, x_ref, near_out, place_out, place):
     clusters, nvec, leaf = src_ref.shape
     peers = x_ref.shape[0]
     cap = place.shape[0] // (peers * nvec)
-    copies = fetch([(near_hbm.at[s], near_ref.at[s]) for s in range(clusters)], sems)
-
     width = leaf // 2
     lane = lax.broadcasted_iota(jnp.int32, (nvec, width), 1)
     sub = lax.broadcasted_iota(jnp.int32, (nvec, width), 0)
@@ -147,14 +158,16 @@
     after = jnp.where(me < peers - 1, after, 0.0).astype(jnp.bfloat16)
     rows = [before] + [src_ref[s] for s in range(clusters)] + [after]
     for s in range(clusters):
-        copies[s].wait()
         total = jnp.dot(rows[s], near_ref[s, 0], preferred_element_type=jnp.float32)
         for o in range(1, 3):
             total += jnp.dot(rows[s + o], near_ref[s, o], preferred_element_type=jnp.float32)
         near_out[s * nvec : (s + 1) * nvec] = total
 
 
-def sum_kernel(back_ref, near_ref, place_ref, out_ref):
+def sum_kernel(back_hbm, near_hbm, place_hbm, out_ref, back_ref, near_ref, place_ref, sems):
+    pairs = [(back_hbm, back_ref), (near_hbm, near_ref), (place_hbm, place_ref)]
+    for copy in fetch(pairs, sems):
+        copy.wait()
     peers, rows, leaf = back_ref.shape
     clusters, nvec, _ = out_ref.shape
     terms = back_ref[...].reshape(peers * rows, leaf)
@@ -174,7 +187,8 @@
     blocks, rank, _ = far_u.shape
     slots = peers * cap
     rows = 2 * (cap + 1) * nvec + nvec
-    params = pltpu.CompilerParams(vmem_limit_bytes=24 * 2**20)
+    part = pltpu.CompilerParams(vmem_limit_bytes=24 * 2**20)
+    whole = pltpu.CompilerParams(vmem_limit_bytes=64 * 2**20)
     message = pl.pallas_call(
         pack_kernel,
         out_shape=jax.ShapeDtypeStruct((peers, rows, leaf // 2), jnp.bfloat16),
@@ -186,7 +200,7 @@
             pltpu.VMEM((clusters, nvec, leaf), jnp.bfloat16),
             pltpu.SemaphoreType.DMA((3,)),
         ],
-        compiler_params=params,
+        compiler_params=whole,
         cost_estimate=cost(0, peers * rows * leaf),
         name="pack",
     )(send_list[0].T, ret_list[0].T, sources)
@@ -194,18 +208,19 @@
     returns = pl.pallas_call(
         far_kernel,
         out_shape=jax.ShapeDtypeStruct((peers, cap * nvec, leaf), jnp.bfloat16),
-        in_specs=[HBM, HBM, VMEM, HBM, HBM],
+        in_specs=[HBM] * 5,
         out_specs=VMEM,
         scratch_shapes=[
             pltpu.SMEM((blocks,), jnp.int32),
             pltpu.SMEM((blocks,), jnp.int32),
+            pltpu.VMEM(incoming.shape, jnp.bfloat16),
             pltpu.VMEM((blocks, rank, leaf), jnp.bfloat16),
             pltpu.VMEM((blocks, rank, leaf), jnp.bfloat16),
             pltpu.VMEM((slots, nvec, leaf), jnp.float32),
         ]
         + [pltpu.VMEM((slots, nvec, leaf), jnp.float32)] * (4 if peers <= 16 else 1)
-        + [pltpu.SemaphoreType.DMA((2 + 2 * CHUNKS,))],
-        compiler_params=params,
+        + [pltpu.SemaphoreType.DMA((3 + 2 * CHUNKS,))],
+        compiler_params=whole,
         cost_estimate=cost(4 * blocks * 8 * nvec * leaf * rank, 4 * blocks * rank * leaf),
         name="far",
     )(far_slot, ret_slot, incoming, far_u, far_v)
@@ -216,23 +231,25 @@
             jax.ShapeDtypeStruct((clusters * nvec, leaf), jnp.float32),
             jax.ShapeDtypeStruct((clusters * nvec, slots * nvec), jnp.bfloat16),
         ),
-        in_specs=[VMEM, HBM, VMEM],
+        in_specs=[VMEM, VMEM, VMEM],
         out_specs=(VMEM, VMEM),
-        scratch_shapes=[
-            pltpu.VMEM(near_blocks.shape, jnp.bfloat16),
-            pltpu.VMEM((slots * nvec, leaf // 2), jnp.float32),
-            pltpu.SemaphoreType.DMA((clusters,)),
-        ],
-        compiler_params=params,
+        scratch_shapes=[pltpu.VMEM((slots * nvec, leaf // 2), jnp.float32)],
+        compiler_params=part,
         cost_estimate=cost(2 * 3 * clusters * nvec * leaf * leaf, 6 * clusters * leaf * leaf),
         name="near",
     )(sources, near_blocks, incoming)
     return pl.pallas_call(
         sum_kernel,
         out_shape=jax.ShapeDtypeStruct((clusters, nvec, leaf), jnp.float32),
-        in_specs=[VMEM, VMEM, VMEM],
+        in_specs=[HBM, HBM, HBM],
         out_specs=VMEM,
-        compiler_params=params,
+        scratch_shapes=[
+            pltpu.VMEM(back.shape, jnp.bfloat16),
+            pltpu.VMEM(near_part.shape, jnp.float32),
+            pltpu.VMEM(place.shape, jnp.bfloat16),
+            pltpu.SemaphoreType.DMA((3,)),
+        ],
+        compiler_params=whole,
         cost_estimate=cost(2 * clusters * nvec * slots * nvec * leaf, slots * nvec * leaf * 2),
         name="sum",
     )(back, near_part, place)

time: 47.9 us -> 42.2 us (0.88)
  local copies, waits for them, and re-layouts: 10.7 us -> 4.81 us
  starting transfers between devices: 3.52 us -> 4.18 us
  waiting for transfers between devices: 3.24 us -> 2.61 us
    unnamed x26 -> x10, local copies, waits for them, and re-layouts: 10.7 us -> 4.81 us
    pallas_call x1, Pallas kernels: 3.39 us -> 0.51 us  [body(): pl.pallas_call(near_kernel, out_shape=(jax.ShapeDtypeStruct((clusters * n...]
    pallas_call x1, Pallas kernels: 8.31 us -> 9.32 us  [body(): pl.pallas_call(far_kernel, out_shape=jax.ShapeDtypeStruct((peers, cap * n...]
    pallas_call x1, Pallas kernels: 0.78 us -> 1.72 us  [body(): pl.pallas_call(sum_kernel, out_shape=jax.ShapeDtypeStruct((clusters, nvec...]
    pallas_call x1, Pallas kernels: 0.66 us -> 1.54 us  [body(): pl.pallas_call(pack_kernel, out_shape=jax.ShapeDtypeStruct((peers, rows,...]
    all_to_all x1, starting transfers between devices: 3.52 us -> 4.18 us  [body(): lax.all_to_all(returns, 'clus', split_axis=0, concat_axis=0, tiled=True)]
    all_to_all x1, waiting for transfers between devices: 3.24 us -> 2.61 us  [body(): lax.all_to_all(returns, 'clus', split_axis=0, concat_axis=0, tiled=True)]
  transfers between devices with their start and end apart: 1 -> 1, of which waited for: 1 -> 1; matrix products, arithmetic and copies ran while one was open for 0% -> 0% of each run, Pallas kernels for 7% -> 1%
where the time goes in v3:
time: 42.2 us; the launch traced here: 41.7 us
  blocking collectives  17 us (40%)
  Pallas kernels  13.1 us (31%)
  local copies, waits for them, and re-layouts  4.81 us (11%)
  starting transfers between devices  4.18 us (10%)
  waiting for transfers between devices  2.61 us (6%)
    all_to_all x1, blocking collectives, body(): lax.all_to_all(message, 'clus', split_axis=0, concat_axis=0, tiled=True)  17 us
    pallas_call x1, Pallas kernels, body(): pl.pallas_call(far_kernel, out_shape=jax.ShapeDtypeStruct((peers, cap * n...  9.32 us
    unnamed x10, local copies, waits for them, and re-layouts  4.81 us
    all_to_all x1, starting transfers between devices, body(): lax.all_to_all(returns, 'clus', split_axis=0, concat_axis=0, tiled=True)  4.18 us
    all_to_all x1, waiting for transfers between devices, body(): lax.all_to_all(returns, 'clus', split_axis=0, concat_axis=0, tiled=True)  2.61 us
    pallas_call x1, Pallas kernels, body(): pl.pallas_call(sum_kernel, out_shape=jax.ShapeDtypeStruct((clusters, nvec...  1.72 us
    pallas_call x1, Pallas kernels, body(): pl.pallas_call(pack_kernel, out_shape=jax.ShapeDtypeStruct((peers, rows,...  1.54 us
  transfers between devices with their start and end apart: 1, of which 1 were waited for; matrix products, arithmetic and copies ran while one was open for 0% of the time, Pallas kernels for 1%

profile of v3, /device:TPU:0, one launch (start us, length us, event | category | flops | bytes accessed | tf_op | source)
XLA Modules:
  0.0 41.7 jit_solution(2271835046809953909)
XLA Ops:
  0.0 1.5 %pack.1 = bf16[16,56,128]{2,1,0:T(8,128)(2,1)} custom-call(s32[2,16]{1,0:T(2,128)} %bitcast.6, s32[2,16]{1,0:T(2,128)} %bitcast.7, bf16[8,8,256]{2,1,0:T(8,128)(2,1)} %src_ref.1), custom_call_target="tpu_custom_call" | custom-call | bytes 229376 | tf_op jit(solution)/shard_map/pack/pallas_call | solution.py:192
  1.5 17.0 %all_to_all.10.x_hbm.x_ref = bf16[16,56,128]{2,1,0:T(8,128)(2,1)} all-to-all(bf16[16,56,128]{2,1,0:T(8,128)(2,1)} %pack.1), channel_id=1, replica_groups=mesh['groups'=2,'clus'=16] {'clus'}, dimensions={0} | all-to-all | bytes 458752 | tf_op jit(solution)/shard_map/all_to_all | solution.py:207
  18.5 9.3 %far.1 = bf16[16,16,256]{2,1,0:T(8,128)(2,1)} custom-call(s32[256]{0:T(256)} %slot_hbm.1, s32[256]{0:T(256)} %dest_hbm.1, bf16[16,56,128]{2,1,0:T(8,128)(2,1)} %all_to_all.10.x_hbm.x_ref, bf16[256,32,256]{2,1,0:T(8,128)(2,1)} %u_hbm.1, bf16[256,32,256]{2,1,0:T(8,128)(2,1)} %v_hbm.1), custom_call_target="tpu_custom_call" | custom-call | flops 536870912 | bytes 8388608 | tf_op jit(solution)/shard_map/far/pallas_call | solution.py:208
  27.9 4.2 %all-to-all-start.1 = ((bf16[16,16,256]{2,1,0:T(8,128)(2,1)}), bf16[16,16,256]{2,1,0:T(8,128)(2,1)}, u32[]{:S(2)}, u32[]{:S(2)}) async-start(bf16[16,16,256]{2,1,0:T(8,128)(2,1)} %far.1), calls=%async_computation.1 | async-start | bytes 262144 | tf_op jit(solution)/shard_map/all_to_all | solution.py:227
  32.1 0.0 copy-start
  32.1 1.9 %copy-done = bf16[8,3,256,256]{3,2,1,0:T(8,128)(2,1)S(1)} copy-done((bf16[8,3,256,256]{3,2,1,0:T(8,128)(2,1)S(1)}, bf16[8,3,256,256]{3,2,1,0:T(8,128)(2,1)}, u32[]{:S(2)}) %copy-start) | copy-done | bytes 3145752
  33.9 0.0 copy-start.1
  33.9 0.9 %copy-done.1 = bf16[16,56,128]{2,1,0:T(8,128)(2,1)S(1)} copy-done((bf16[16,56,128]{2,1,0:T(8,128)(2,1)S(1)}, bf16[16,56,128]{2,1,0:T(8,128)(2,1)}, u32[]{:S(2)}) %copy-start.1) | copy-done | bytes 229400
  34.9 0.0 copy-start.2
  34.9 0.8 %copy-done.2 = bf16[8,8,256]{2,1,0:T(8,128)(2,1)S(1)} copy-done((bf16[8,8,256]{2,1,0:T(8,128)(2,1)S(1)}, bf16[8,8,256]{2,1,0:T(8,128)(2,1)}, u32[]{:S(2)}) %copy-start.2) | copy-done | bytes 32792
  35.6 0.5 %near.1 = (f32[64,256]{1,0:T(8,128)S(1)}, bf16[64,256]{1,0:T(8,128)(2,1)S(1)}) custom-call(bf16[8,8,256]{2,1,0:T(8,128)(2,1)S(1)} %copy-done.2, bf16[8,3,256,256]{3,2,1,0:T(8,128)(2,1)S(1)} %copy-done, bf16[16,56,128]{2,1,0:T(8,128)(2,1)S(1)} %copy-done.1), custom_call_target="tpu_custom_call" | custom-call | flops 25165824 | bytes 3145728 | tf_op jit(solution)/shard_map/near/pallas_call | solution.py:228
  36.2 0.0 copy-start.3
  36.2 0.6 %copy-done.3 = f32[64,256]{1,0:T(8,128)} copy-done((f32[64,256]{1,0:T(8,128)}, f32[64,256]{1,0:T(8,128)S(1)}, u32[]{:S(2)}) %copy-start.3) | copy-done | bytes 65560
  36.8 0.0 copy-start.4
  36.8 0.6 %copy-done.4 = bf16[64,256]{1,0:T(8,128)(2,1)} copy-done((bf16[64,256]{1,0:T(8,128)(2,1)}, bf16[64,256]{1,0:T(8,128)(2,1)S(1)}, u32[]{:S(2)}) %copy-start.4) | copy-done | bytes 32792
  37.4 2.6 %all-to-all-done.1.back_hbm = bf16[16,16,256]{2,1,0:T(8,128)(2,1)} async-done(((bf16[16,16,256]{2,1,0:T(8,128)(2,1)}), bf16[16,16,256]{2,1,0:T(8,128)(2,1)}, u32[]{:S(2)}, u32[]{:S(2)}) %all-to-all-start.1) | async-done | bytes 131104 | tf_op jit(solution)/shard_map/all_to_all | solution.py:227
  40.0 1.7 %sum.1 = f32[8,8,256]{2,1,0:T(8,128)} custom-call(bf16[16,16,256]{2,1,0:T(8,128)(2,1)} %all-to-all-done.1.back_hbm, f32[64,256]{1,0:T(8,128)} %copy-done.3, bf16[64,256]{1,0:T(8,128)(2,1)} %copy-done.4), custom_call_target="tpu_custom_call" | custom-call | flops 8388608 | bytes 131072 | tf_op jit(solution)/shard_map/sum/pallas_call | solution.py:241
Async XLA Ops:
  27.9 12.1 %all-to-all-start.1 = ((bf16[16,16,256]{2,1,0:T(8,128)(2,1)}), bf16[16,16,256]{2,1,0:T(8,128)(2,1)}, u32[]{:S(2)}, u32[]{:S(2)}) async-start(bf16[16,16,256]{2,1,0:T(8,128)(2,1)} %far.1), calls=%async_computation.1 | async-start | bytes 262144 | tf_op jit(solution)/shard_map/all_to_all | solution.py:227
  32.1 1.9 %copy-start = (bf16[8,3,256,256]{3,2,1,0:T(8,128)(2,1)S(1)}, bf16[8,3,256,256]{3,2,1,0:T(8,128)(2,1)}, u32[]{:S(2)}) copy-start(bf16[8,3,256,256]{3,2,1,0:T(8,128)(2,1)} %near_ref.1) | copy-start | bytes 9437188
  33.9 0.9 %copy-start.1 = (bf16[16,56,128]{2,1,0:T(8,128)(2,1)S(1)}, bf16[16,56,128]{2,1,0:T(8,128)(2,1)}, u32[]{:S(2)}) copy-start(bf16[16,56,128]{2,1,0:T(8,128)(2,1)} %all_to_all.10.x_hbm.x_ref) | copy-start | bytes 688132
  34.9 0.8 %copy-start.2 = (bf16[8,8,256]{2,1,0:T(8,128)(2,1)S(1)}, bf16[8,8,256]{2,1,0:T(8,128)(2,1)}, u32[]{:S(2)}) copy-start(bf16[8,8,256]{2,1,0:T(8,128)(2,1)} %src_ref.1) | copy-start | bytes 98308
  36.2 0.6 %copy-start.3 = (f32[64,256]{1,0:T(8,128)}, f32[64,256]{1,0:T(8,128)S(1)}, u32[]{:S(2)}) copy-start(f32[64,256]{1,0:T(8,128)S(1)} %get-tuple-element.7.near_hbm) | copy-start | bytes 196612
  36.8 0.6 %copy-start.4 = (bf16[64,256]{1,0:T(8,128)(2,1)}, bf16[64,256]{1,0:T(8,128)(2,1)S(1)}, u32[]{:S(2)}) copy-start(bf16[64,256]{1,0:T(8,128)(2,1)S(1)} %get-tuple-element.8.place_hbm) | copy-start | bytes 98308

commit v4 on v2

v4 whole, which is shorter than its diff:
```python
import jax
import jax.numpy as jnp
from jax import lax
from jax.experimental import pallas as pl
from jax.experimental.pallas import tpu as pltpu
from jax.sharding import PartitionSpec as P

VMEM = pl.BlockSpec(memory_space=pltpu.VMEM)
SMEM = pl.BlockSpec(memory_space=pltpu.SMEM)


def halves(x):
    w = x.shape[1] // 2
    return [x[:, :w], x[:, w:]]


def pack_kernel(send_ref, ret_ref, src_ref, out_ref):
    clusters, nvec, leaf = src_ref.shape
    cap, peers = send_ref.shape
    me = lax.axis_index("clus")
    first = src_ref[0].astype(jnp.float32)
    last = src_ref[clusters - 1].astype(jnp.float32)

    def step(p, carry):
        rows = []
        for k in range(cap):
            rows += halves(src_ref[jnp.maximum(send_ref[k, p], 0)].astype(jnp.float32))
        rows += halves(jnp.where(p > me, last, first))
        rows.append(
            jnp.concatenate(
                [
                    jnp.full((nvec // cap, leaf // 2), ret_ref[k, p].astype(jnp.float32))
                    for k in range(cap)
                ],
                axis=0,
            )
        )
        out_ref[p] = jnp.concatenate(rows, axis=0).astype(out_ref.dtype)
        return carry

    lax.fori_loop(0, peers, step, 0, unroll=min(peers, 16))


def joined(rows, nvec):
    return jnp.concatenate([rows[:nvec], rows[nvec:]], axis=1)


def far_kernel(slot_ref, dest_ref, x_ref, u_ref, v_ref, out_ref, xf, *accs):
    peers = x_ref.shape[0]
    slots, nvec, leaf = xf.shape
    cap = slots // peers
    blocks, rank, _ = u_ref.shape
    group = leaf // rank
    for acc in accs:
        acc[...] = jnp.zeros_like(acc)

    def widen(p, carry):
        rows = x_ref[p].astype(jnp.float32)
        for k in range(cap):
            xf[p * cap + k] = joined(rows[2 * k * nvec : 2 * (k + 1) * nvec], nvec)
        return carry

    lax.fori_loop(0, peers, widen, 0, unroll=min(peers, 16))
    owner = lax.broadcasted_iota(jnp.int32, (nvec, leaf), 1) // rank
    for g in range(blocks // group):
        picked = jnp.concatenate(
            [xf[slot_ref[g * group + i]] for i in range(group)], axis=0
        ).astype(jnp.bfloat16)
        u = u_ref[g * group : (g + 1) * group].reshape(group * rank, leaf)
        full = lax.dot_general(
            picked, u, (((1,), (1,)), ((), ())), preferred_element_type=jnp.float32
        )
        kept = full[:nvec]
        for i in range(1, group):
            kept = jnp.where(owner == i, full[i * nvec : (i + 1) * nvec], kept)
        spread = jnp.concatenate(
            [jnp.where(owner == i, kept, 0.0) for i in range(group)], axis=0
        ).astype(jnp.bfloat16)
        v = v_ref[g * group : (g + 1) * group].reshape(group * rank, leaf)
        terms = jnp.dot(spread, v, preferred_element_type=jnp.float32)
        for i in range(group):
            accs[i % len(accs)][dest_ref[g * group + i]] += terms[i * nvec : (i + 1) * nvec]

    def narrow(p, carry):
        rows = []
        for k in range(cap):
            total = accs[0][p * cap + k]
            for acc in accs[1:]:
                total += acc[p * cap + k]
            rows.append(total)
        out_ref[p] = jnp.concatenate(rows, axis=0).astype(out_ref.dtype)
        return carry

    lax.fori_loop(0, peers, narrow, 0, unroll=min(peers, 16))


def sum_kernel(back_ref, src_ref, near_ref, x_ref, out_ref, place):
    clusters, nvec, leaf = src_ref.shape
    peers, back_rows, _ = back_ref.shape
    cap = back_rows // nvec
    width = leaf // 2
    lane = lax.broadcasted_iota(jnp.int32, (nvec, width), 1)
    sub = lax.broadcasted_iota(jnp.int32, (nvec, width), 0)
    cluster = jnp.where(lane % nvec == sub, lane // nvec, -2).astype(jnp.float32)

    def step(p, carry):
        meta = x_ref[p, 2 * (cap + 1) * nvec :, :].astype(jnp.float32)
        for k in range(cap):
            at = jnp.broadcast_to(meta[k * nvec // cap : k * nvec // cap + 1], (nvec, width))
            place[pl.ds((p * cap + k) * nvec, nvec)] = jnp.where(at == cluster, 1.0, 0.0)
        return carry

    lax.fori_loop(0, peers, step, 0, unroll=min(peers, 16))
    spread = place[...].T[: clusters * nvec].astype(jnp.bfloat16)
    terms = back_ref[...].reshape(peers * back_rows, leaf)
    far_part = jnp.dot(spread, terms, preferred_element_type=jnp.float32)

    me = lax.axis_index("clus")
    edge = slice(2 * cap * nvec, 2 * (cap + 1) * nvec)
    before = joined(x_ref[jnp.maximum(me - 1, 0)][edge].astype(jnp.float32), nvec)
    after = joined(x_ref[jnp.minimum(me + 1, peers - 1)][edge].astype(jnp.float32), nvec)
    before = jnp.where(me > 0, before, 0.0).astype(jnp.bfloat16)
    after = jnp.where(me < peers - 1, after, 0.0).astype(jnp.bfloat16)
    rows = [before] + [src_ref[s] for s in range(clusters)] + [after]
    for s in range(clusters):
        total = far_part[s * nvec : (s + 1) * nvec]
        for o in range(3):
            total += jnp.dot(rows[s + o], near_ref[s, o], preferred_element_type=jnp.float32)
        out_ref[s] = total


def cost(flops, moved):
    return pl.CostEstimate(flops=flops, bytes_accessed=moved, transcendentals=0)


def body(sources, near_blocks, far_u, far_v, send_list, far_slot, ret_list, ret_slot):
    clusters, nvec, leaf = sources.shape
    _, peers, cap = send_list.shape
    blocks, rank, _ = far_u.shape
    slots = peers * cap
    rows = 2 * (cap + 1) * nvec + nvec
    params = pltpu.CompilerParams(vmem_limit_bytes=8 * 2**20)
    message = pl.pallas_call(
        pack_kernel,
        out_shape=jax.ShapeDtypeStruct((peers, rows, leaf // 2), jnp.bfloat16),
        in_specs=[SMEM, SMEM, VMEM],
        out_specs=VMEM,
        compiler_params=params,
        cost_estimate=cost(10**10, peers * rows * leaf),
        name="pack",
    )(send_list[0].T, ret_list[0].T, sources)
    incoming = lax.all_to_all(message, "clus", split_axis=0, concat_axis=0, tiled=True)
    returns = pl.pallas_call(
        far_kernel,
        out_shape=jax.ShapeDtypeStruct((peers, cap * nvec, leaf), jnp.bfloat16),
        in_specs=[SMEM, SMEM, VMEM, VMEM, VMEM],
        out_specs=VMEM,
        scratch_shapes=[pltpu.VMEM((slots, nvec, leaf), jnp.float32)]
        * (5 if peers <= 16 else 2),
        compiler_params=params,
        cost_estimate=cost(4 * blocks * 8 * nvec * leaf * rank, 4 * blocks * rank * leaf),
        name="far",
    )(far_slot, ret_slot, incoming, far_u, far_v)
    back = lax.all_to_all(returns, "clus", split_axis=0, concat_axis=0, tiled=True)
    return pl.pallas_call(
        sum_kernel,
        out_shape=jax.ShapeDtypeStruct((clusters, nvec, leaf), jnp.float32),
        in_specs=[VMEM] * 4,
        out_specs=VMEM,
        scratch_shapes=[pltpu.VMEM((slots * nvec, leaf // 2), jnp.float32)],
        compiler_params=params,
        cost_estimate=cost(2 * 3 * clusters * nvec * leaf * leaf, 6 * clusters * leaf * leaf),
        name="sum",
    )(back, sources, near_blocks, incoming)


def solution(mesh):
    placed = (
        P(("groups", "clus"), None, None),
        P(("groups", "clus"), None, None, None),
        P(("groups", "clus"), None, None),
        P(("groups", "clus"), None, None),
        P(("groups", "clus"), None, None),
        P(("groups", "clus")),
        P(("groups", "clus"), None, None),
        P(("groups", "clus")),
    )
    return jax.shard_map(
        body,
        mesh=mesh,
        in_specs=placed,
        out_specs=P(("groups", "clus"), None, None),
        check_vma=False,
    )
```

time: 47.9 us -> 38.9 us (0.81)
  blocking collectives: 16.7 us -> 27.5 us
  local copies, waits for them, and re-layouts: 10.7 us -> 2.14 us
  Pallas kernels: 13.2 us -> 8.92 us
  starting transfers between devices: 3.52 us -> 0 us
  waiting for transfers between devices: 3.24 us -> 0 us
    all_to_all x0 -> x1, blocking collectives: none -> 10.6 us  [body(): lax.all_to_all(returns, 'clus', split_axis=0, concat_axis=0, tiled=True)]
    unnamed x26 -> x18, local copies, waits for them, and re-layouts: 10.7 us -> 2.14 us
    all_to_all x1 -> x0, starting transfers between devices: 3.52 us -> none  [body(): lax.all_to_all(returns, 'clus', split_axis=0, concat_axis=0, tiled=True)]
    pallas_call x1 -> x0, Pallas kernels: 3.39 us -> none  [body(): pl.pallas_call(near_kernel, out_shape=(jax.ShapeDtypeStruct((clusters * n...]
    all_to_all x1 -> x0, waiting for transfers between devices: 3.24 us -> none  [body(): lax.all_to_all(returns, 'clus', split_axis=0, concat_axis=0, tiled=True)]
    pallas_call x1, Pallas kernels: 8.31 us -> 7.08 us  [body(): pl.pallas_call(far_kernel, out_shape=jax.ShapeDtypeStruct((peers, cap * n...]
  transfers between devices with their start and end apart: 1 -> 0, of which waited for: 1 -> 0; matrix products, arithmetic and copies ran while one was open for 0% -> 0% of each run, Pallas kernels for 7% -> 0%
where the time goes in v4:
time: 38.9 us; the launch traced here: 38.6 us
  blocking collectives  27.5 us (71%)
  Pallas kernels  8.92 us (23%)
  local copies, waits for them, and re-layouts  2.14 us (6%)
    all_to_all x1, blocking collectives, body(): lax.all_to_all(message, 'clus', split_axis=0, concat_axis=0, tiled=True)  16.9 us
    all_to_all x1, blocking collectives, body(): lax.all_to_all(returns, 'clus', split_axis=0, concat_axis=0, tiled=True)  10.6 us
    pallas_call x1, Pallas kernels, body(): pl.pallas_call(far_kernel, out_shape=jax.ShapeDtypeStruct((peers, cap * n...  7.08 us
    unnamed x18, local copies, waits for them, and re-layouts  2.14 us
    pallas_call x1, Pallas kernels, body(): pl.pallas_call(sum_kernel, out_shape=jax.ShapeDtypeStruct((clusters, nvec...  1.2 us

profile of v4, /device:TPU:0, one launch (start us, length us, event | category | flops | bytes accessed | tf_op | source)
XLA Modules:
  0.0 38.6 jit_solution(13126597944419780153)
XLA Ops:
  0.0 0.0 copy-start.3
  0.0 0.8 %copy-done.3 = bf16[8,8,256]{2,1,0:T(8,128)(2,1)S(1)} copy-done((bf16[8,8,256]{2,1,0:T(8,128)(2,1)S(1)}, bf16[8,8,256]{2,1,0:T(8,128)(2,1)}, u32[]{:S(2)}) %copy-start.3) | copy-done | bytes 32792
  0.8 0.0 copy-start.7
  0.8 0.7 %copy-done.7 = s32[1,16,2]{1,2,0:T(2,128)S(1)} copy-done((s32[1,16,2]{1,2,0:T(2,128)S(1)}, s32[1,16,2]{1,2,0:T(2,128)}, u32[]{:S(2)}) %copy-start.7) | copy-done | bytes 152
  1.4 0.0 copy-start.8
  1.4 0.7 %copy-done.8 = s32[1,16,2]{1,2,0:T(2,128)S(1)} copy-done((s32[1,16,2]{1,2,0:T(2,128)S(1)}, s32[1,16,2]{1,2,0:T(2,128)}, u32[]{:S(2)}) %copy-start.8) | copy-done | bytes 152
  2.1 0.0 copy-start
  2.1 0.0 copy-start.1
  2.1 0.0 copy-start.5
  2.1 0.0 copy-start.6
  2.1 0.6 %pack.1 = bf16[16,56,128]{2,1,0:T(8,128)(2,1)S(1)} custom-call(s32[2,16]{1,0:T(2,128)S(1)} %bitcast.6, s32[2,16]{1,0:T(2,128)S(1)} %bitcast.7, bf16[8,8,256]{2,1,0:T(8,128)(2,1)S(1)} %copy-done.3), custom_call_target="tpu_custom_call" | custom-call | flops 10000000000 | bytes 229376 | tf_op jit(solution)/shard_map/pack/pallas_call | solution.py:143
  2.8 16.9 %all_to_all.10.x_ref = bf16[16,56,128]{2,1,0:T(8,128)(2,1)S(1)} all-to-all(bf16[16,56,128]{2,1,0:T(8,128)(2,1)S(1)} %pack.1), channel_id=1, replica_groups=mesh['groups'=2,'clus'=16] {'clus'}, dimensions={0} | all-to-all | bytes 458752 | tf_op jit(solution)/shard_map/all_to_all | solution.py:152
  19.7 0.0 copy-done
  19.7 0.0 copy-done.1
  19.7 0.0 copy-done.5
  19.7 0.0 copy-done.6
  19.7 0.0 copy-start.2
  19.8 0.0 copy-start.4
  19.8 7.1 %far.1 = bf16[16,16,256]{2,1,0:T(8,128)(2,1)S(1)} custom-call(s32[256]{0:T(256)S(1)} %copy-done.5, s32[256]{0:T(256)S(1)} %copy-done.6, bf16[16,56,128]{2,1,0:T(8,128)(2,1)S(1)} %all_to_all.10.x_ref, bf16[256,32,256]{2,1,0:T(8,128)(2,1)S(1)} %copy-done, bf16[256,32,256]{2,1,0:T(8,128)(2,1)S(1)} %copy-done.1), custom_call_target="tpu_custom_call" | custom-call | flops 536870912 | bytes 8388608 | tf_op jit(solution)/shard_map/far/pallas_call | solution.py:153
  26.8 10.6 %all_to_all.11.back_ref = bf16[16,16,256]{2,1,0:T(8,128)(2,1)S(1)} all-to-all(bf16[16,16,256]{2,1,0:T(8,128)(2,1)S(1)} %far.1), channel_id=1, replica_groups=mesh['groups'=2,'clus'=16] {'clus'}, dimensions={0} | all-to-all | bytes 262144 | tf_op jit(solution)/shard_map/all_to_all | solution.py:164
  37.4 0.0 copy-done.2
  37.4 0.0 copy-done.4
  37.4 1.2 %sum.1 = f32[8,8,256]{2,1,0:T(8,128)} custom-call(bf16[16,16,256]{2,1,0:T(8,128)(2,1)S(1)} %all_to_all.11.back_ref, bf16[8,8,256]{2,1,0:T(8,128)(2,1)S(1)} %copy-done.4, bf16[8,3,256,256]{3,2,1,0:T(8,128)(2,1)S(1)} %copy-done.2, bf16[16,56,128]{2,1,0:T(8,128)(2,1)S(1)} %all_to_all.10.x_ref), custom_call_target="tpu_custom_call" | custom-call | flops 25165824 | bytes 3145728 | tf_op jit(solution)/shard_map/sum/pallas_call | solution.py:165
Async XLA Ops:
  0.0 0.8 %copy-start.3 = (bf16[8,8,256]{2,1,0:T(8,128)(2,1)S(1)}, bf16[8,8,256]{2,1,0:T(8,128)(2,1)}, u32[]{:S(2)}) copy-start(bf16[8,8,256]{2,1,0:T(8,128)(2,1)} %src_ref.3) | copy-start | bytes 98308
  0.8 0.7 %copy-start.7 = (s32[1,16,2]{1,2,0:T(2,128)S(1)}, s32[1,16,2]{1,2,0:T(2,128)}, u32[]{:S(2)}) copy-start(s32[1,16,2]{1,2,0:T(2,128)} %param.12) | copy-start | bytes 388
  1.4 0.7 %copy-start.8 = (s32[1,16,2]{1,2,0:T(2,128)S(1)}, s32[1,16,2]{1,2,0:T(2,128)}, u32[]{:S(2)}) copy-start(s32[1,16,2]{1,2,0:T(2,128)} %param.14) | copy-start | bytes 388
  2.1 17.6 %copy-start = (bf16[256,32,256]{2,1,0:T(8,128)(2,1)S(1)}, bf16[256,32,256]{2,1,0:T(8,128)(2,1)}, u32[]{:S(2)}) copy-start(bf16[256,32,256]{2,1,0:T(8,128)(2,1)} %u_ref.1) | copy-start | bytes 12582916
  2.1 17.6 %copy-start.1 = (bf16[256,32,256]{2,1,0:T(8,128)(2,1)S(1)}, bf16[256,32,256]{2,1,0:T(8,128)(2,1)}, u32[]{:S(2)}) copy-start(bf16[256,32,256]{2,1,0:T(8,128)(2,1)} %v_ref.1) | copy-start | bytes 12582916
  2.1 17.6 %copy-start.5 = (s32[256]{0:T(256)S(1)}, s32[256]{0:T(256)}, u32[]{:S(2)}) copy-start(s32[256]{0:T(256)} %slot_ref.1) | copy-start | bytes 3076
  2.1 17.6 %copy-start.6 = (s32[256]{0:T(256)S(1)}, s32[256]{0:T(256)}, u32[]{:S(2)}) copy-start(s32[256]{0:T(256)} %dest_ref.1) | copy-start | bytes 3076
  19.7 17.7 %copy-start.2 = (bf16[8,3,256,256]{3,2,1,0:T(8,128)(2,1)S(1)}, bf16[8,3,256,256]{3,2,1,0:T(8,128)(2,1)}, u32[]{:S(2)}) copy-start(bf16[8,3,256,256]{3,2,1,0:T(8,128)(2,1)} %near_ref.1) | copy-start | bytes 9437188
  19.8 17.7 %copy-start.4 = (bf16[8,8,256]{2,1,0:T(8,128)(2,1)S(1)}, bf16[8,8,256]{2,1,0:T(8,128)(2,1)}, u32[]{:S(2)}) copy-start(bf16[8,8,256]{2,1,0:T(8,128)(2,1)} %src_ref.3) | copy-start | bytes 98308

commit v5 on v4

--- a/solution.py
+++ b/solution.py
@@ -6,6 +6,7 @@
 from jax.sharding import PartitionSpec as P
 
 VMEM = pl.BlockSpec(memory_space=pltpu.VMEM)
+CHUNKS = 4
 SMEM = pl.BlockSpec(memory_space=pltpu.SMEM)
 
 
@@ -45,14 +46,10 @@
     return jnp.concatenate([rows[:nvec], rows[nvec:]], axis=1)
 
 
-def far_kernel(slot_ref, dest_ref, x_ref, u_ref, v_ref, out_ref, xf, *accs):
+def widen_sources(x_ref, xf):
     peers = x_ref.shape[0]
-    slots, nvec, leaf = xf.shape
+    slots, nvec, _ = xf.shape
     cap = slots // peers
-    blocks, rank, _ = u_ref.shape
-    group = leaf // rank
-    for acc in accs:
-        acc[...] = jnp.zeros_like(acc)
 
     def widen(p, carry):
         rows = x_ref[p].astype(jnp.float32)
@@ -61,37 +58,80 @@
         return carry
 
     lax.fori_loop(0, peers, widen, 0, unroll=min(peers, 16))
+
+
+def project(picked, u, owner, nvec, group):
+    full = lax.dot_general(picked, u, (((1,), (1,)), ((), ())), preferred_element_type=jnp.float32)
+    kept = full[:nvec]
+    for i in range(1, group):
+        kept = jnp.where(owner == i, full[i * nvec : (i + 1) * nvec], kept)
+    return kept
+
+
+def far_kernel(slot_ref, dest_ref, x_ref, u_ref, v_ref, out_ref, xf, picked, wide):
+    peers = x_ref.shape[0]
+    slots, nvec, leaf = xf.shape
+    blocks, rank, _ = u_ref.shape
+    group = leaf // rank
+    groups = blocks // group
+    per = groups // CHUNKS
+    widen_sources(x_ref, xf)
+    for g in range(groups):
+        rows = [xf[slot_ref[g * group + i]] for i in range(group)]
+        picked[g] = jnp.concatenate(rows, axis=0).astype(jnp.bfloat16)
     owner = lax.broadcasted_iota(jnp.int32, (nvec, leaf), 1) // rank
-    for g in range(blocks // group):
-        picked = jnp.concatenate(
-            [xf[slot_ref[g * group + i]] for i in range(group)], axis=0
-        ).astype(jnp.bfloat16)
-        u = u_ref[g * group : (g + 1) * group].reshape(group * rank, leaf)
-        full = lax.dot_general(
-            picked, u, (((1,), (1,)), ((), ())), preferred_element_type=jnp.float32
+    total = None
+    for c in range(CHUNKS):
+        for g in range(c * per, (c + 1) * per):
+            u = u_ref[g * group : (g + 1) * group].reshape(leaf, leaf)
+            kept = project(picked[g], u, owner, nvec, group)
+            dest = jnp.full((nvec, leaf), dest_ref[g * group], jnp.int32)
+            for i in range(1, group):
+                dest = jnp.where(owner == i, dest_ref[g * group + i], dest)
+            dest = dest.astype(jnp.float32)
+            kept = jnp.concatenate([kept, kept], axis=0).astype(jnp.bfloat16)
+            dest = jnp.concatenate([dest, dest - 1.0], axis=0).astype(jnp.bfloat16)
+            for o in range(0, slots, 2):
+                wide[o * nvec : (o + 2) * nvec, g * leaf : (g + 1) * leaf] = jnp.where(
+                    dest == jnp.bfloat16(o), kept, jnp.bfloat16(0)
+                )
+        v = v_ref[c * per * group : (c + 1) * per * group].reshape(per * leaf, leaf)
+        part = jnp.dot(
+            wide[:, c * per * leaf : (c + 1) * per * leaf], v, preferred_element_type=jnp.float32
         )
-        kept = full[:nvec]
-        for i in range(1, group):
-            kept = jnp.where(owner == i, full[i * nvec : (i + 1) * nvec], kept)
+        total = part if total is None else total + part
+    out_ref[...] = total.reshape(out_ref.shape).astype(out_ref.dtype)
+
+
+def far_many_kernel(slot_ref, dest_ref, x_ref, u_ref, v_ref, out_ref, xf, coef, acc):
+    slots, nvec, leaf = xf.shape
+    blocks, rank, _ = u_ref.shape
+    group = leaf // rank
+    widen_sources(x_ref, xf)
+    acc[...] = jnp.zeros_like(acc)
+    owner = lax.broadcasted_iota(jnp.int32, (nvec, leaf), 1) // rank
+
+    def forward(g, carry):
+        rows = [xf[slot_ref[g * group + i]] for i in range(group)]
+        picked = jnp.concatenate(rows, axis=0).astype(jnp.bfloat16)
+        u = u_ref[pl.ds(g * group, group)].reshape(leaf, leaf)
+        coef[g] = project(picked, u, owner, nvec, group)
+        return carry
+
+    def backward(g, carry):
+        kept = coef[g]
         spread = jnp.concatenate(
             [jnp.where(owner == i, kept, 0.0) for i in range(group)], axis=0
         ).astype(jnp.bfloat16)
-        v = v_ref[g * group : (g + 1) * group].reshape(group * rank, leaf)
+        v = v_ref[pl.ds(g * group, group)].reshape(leaf, leaf)
         terms = jnp.dot(spread, v, preferred_element_type=jnp.float32)
         for i in range(group):
-            accs[i % len(accs)][dest_ref[g * group + i]] += terms[i * nvec : (i + 1) * nvec]
-
-    def narrow(p, carry):
-        rows = []
-        for k in range(cap):
-            total = accs[0][p * cap + k]
-            for acc in accs[1:]:
-                total += acc[p * cap + k]
-            rows.append(total)
-        out_ref[p] = jnp.concatenate(rows, axis=0).astype(out_ref.dtype)
-        return carry
-
-    lax.fori_loop(0, peers, narrow, 0, unroll=min(peers, 16))
+            acc[dest_ref[g * group + i]] += terms[i * nvec : (i + 1) * nvec]
+        return carry
+
+    lax.fori_loop(0, blocks // group, forward, 0, unroll=4)
+    lax.fori_loop(0, blocks // group, backward, 0, unroll=4)
+    out_ref[...] = acc[...].reshape(out_ref.shape).astype(out_ref.dtype)
 
 
 def sum_kernel(back_ref, src_ref, near_ref, x_ref, out_ref, place):
@@ -150,14 +190,24 @@
         name="pack",
     )(send_list[0].T, ret_list[0].T, sources)
     incoming = lax.all_to_all(message, "clus", split_axis=0, concat_axis=0, tiled=True)
+    few = slots <= 32
+    if few:
+        scratch = [
+            pltpu.VMEM((blocks * rank // leaf, leaf // rank * nvec, leaf), jnp.bfloat16),
+            pltpu.VMEM((slots * nvec, blocks * rank), jnp.bfloat16),
+        ]
+    else:
+        scratch = [
+            pltpu.VMEM((blocks * rank // leaf, nvec, leaf), jnp.float32),
+            pltpu.VMEM((slots, nvec, leaf), jnp.float32),
+        ]
     returns = pl.pallas_call(
-        far_kernel,
+        far_kernel if few else far_many_kernel,
         out_shape=jax.ShapeDtypeStruct((peers, cap * nvec, leaf), jnp.bfloat16),
         in_specs=[SMEM, SMEM, VMEM, VMEM, VMEM],
         out_specs=VMEM,
-        scratch_shapes=[pltpu.VMEM((slots, nvec, leaf), jnp.float32)]
-        * (5 if peers <= 16 else 2),
-        compiler_params=params,
+        scratch_shapes=[pltpu.VMEM((slots, nvec, leaf), jnp.float32)] + scratch,
+        compiler_params=pltpu.CompilerParams(vmem_limit_bytes=16 * 2**20),
         cost_estimate=cost(4 * blocks * 8 * nvec * leaf * rank, 4 * blocks * rank * leaf),
         name="far",
     )(far_slot, ret_slot, incoming, far_u, far_v)

time: 38.9 us -> 35.5 us (0.913)
  Pallas kernels: 8.92 us -> 5.53 us
    pallas_call x1, Pallas kernels: 7.08 us -> 3.69 us  [body(): pl.pallas_call(far_kernel if few else far_many_kernel, out_shape=jax.Shap...]
where the time goes in v5:
time: 35.5 us; the launch traced here: 35.2 us
  blocking collectives  27.5 us (77%)
  Pallas kernels  5.53 us (16%)
  local copies, waits for them, and re-layouts  2.14 us (6%)
    all_to_all x1, blocking collectives, body(): lax.all_to_all(message, 'clus', split_axis=0, concat_axis=0, tiled=True)  16.9 us
    all_to_all x1, blocking collectives, body(): lax.all_to_all(returns, 'clus', split_axis=0, concat_axis=0, tiled=True)  10.6 us
    pallas_call x1, Pallas kernels, body(): pl.pallas_call(far_kernel if few else far_many_kernel, out_shape=jax.Shap...  3.69 us
    unnamed x18, local copies, waits for them, and re-layouts  2.14 us
    pallas_call x1, Pallas kernels, body(): pl.pallas_call(sum_kernel, out_shape=jax.ShapeDtypeStruct((clusters, nvec...  1.21 us

profile of v5, /device:TPU:0, one launch (start us, length us, event | category | flops | bytes accessed | tf_op | source)
XLA Modules:
  0.0 35.2 jit_solution(5576989731579315120)
XLA Ops:
  0.0 0.0 copy-start.3
  0.0 0.8 %copy-done.3 = bf16[8,8,256]{2,1,0:T(8,128)(2,1)S(1)} copy-done((bf16[8,8,256]{2,1,0:T(8,128)(2,1)S(1)}, bf16[8,8,256]{2,1,0:T(8,128)(2,1)}, u32[]{:S(2)}) %copy-start.3) | copy-done | bytes 32792
  0.8 0.0 copy-start.7
  0.8 0.7 %copy-done.7 = s32[1,16,2]{1,2,0:T(2,128)S(1)} copy-done((s32[1,16,2]{1,2,0:T(2,128)S(1)}, s32[1,16,2]{1,2,0:T(2,128)}, u32[]{:S(2)}) %copy-start.7) | copy-done | bytes 152
  1.4 0.0 copy-start.8
  1.4 0.7 %copy-done.8 = s32[1,16,2]{1,2,0:T(2,128)S(1)} copy-done((s32[1,16,2]{1,2,0:T(2,128)S(1)}, s32[1,16,2]{1,2,0:T(2,128)}, u32[]{:S(2)}) %copy-start.8) | copy-done | bytes 152
  2.1 0.0 copy-start
  2.1 0.0 copy-start.1
  2.1 0.0 copy-start.5
  2.1 0.0 copy-start.6
  2.1 0.6 %pack.1 = bf16[16,56,128]{2,1,0:T(8,128)(2,1)S(1)} custom-call(s32[2,16]{1,0:T(2,128)S(1)} %bitcast.6, s32[2,16]{1,0:T(2,128)S(1)} %bitcast.7, bf16[8,8,256]{2,1,0:T(8,128)(2,1)S(1)} %copy-done.3), custom_call_target="tpu_custom_call" | custom-call | flops 10000000000 | bytes 229376 | tf_op jit(solution)/shard_map/pack/pallas_call | solution.py:183
  2.8 16.9 %all_to_all.10.x_ref = bf16[16,56,128]{2,1,0:T(8,128)(2,1)S(1)} all-to-all(bf16[16,56,128]{2,1,0:T(8,128)(2,1)S(1)} %pack.1), channel_id=1, replica_groups=mesh['groups'=2,'clus'=16] {'clus'}, dimensions={0} | all-to-all | bytes 458752 | tf_op jit(solution)/shard_map/all_to_all | solution.py:192
  19.7 0.0 copy-done
  19.7 0.0 copy-done.1
  19.7 0.0 copy-done.5
  19.7 0.0 copy-done.6
  19.7 0.0 copy-start.2
  19.8 0.0 copy-start.4
  19.8 3.7 %far.1 = bf16[16,16,256]{2,1,0:T(8,128)(2,1)S(1)} custom-call(s32[256]{0:T(256)S(1)} %copy-done.5, s32[256]{0:T(256)S(1)} %copy-done.6, bf16[16,56,128]{2,1,0:T(8,128)(2,1)S(1)} %all_to_all.10.x_ref, bf16[256,32,256]{2,1,0:T(8,128)(2,1)S(1)} %copy-done, bf16[256,32,256]{2,1,0:T(8,128)(2,1)S(1)} %copy-done.1), custom_call_target="tpu_custom_call" | custom-call | flops 536870912 | bytes 8388608 | tf_op jit(solution)/shard_map/far/pallas_call | solution.py:204
  23.5 10.6 %all_to_all.11.back_ref = bf16[16,16,256]{2,1,0:T(8,128)(2,1)S(1)} all-to-all(bf16[16,16,256]{2,1,0:T(8,128)(2,1)S(1)} %far.1), channel_id=1, replica_groups=mesh['groups'=2,'clus'=16] {'clus'}, dimensions={0} | all-to-all | bytes 262144 | tf_op jit(solution)/shard_map/all_to_all | solution.py:214
  34.0 0.0 copy-done.2
  34.0 0.0 copy-done.4
  34.0 1.2 %sum.1 = f32[8,8,256]{2,1,0:T(8,128)} custom-call(bf16[16,16,256]{2,1,0:T(8,128)(2,1)S(1)} %all_to_all.11.back_ref, bf16[8,8,256]{2,1,0:T(8,128)(2,1)S(1)} %copy-done.4, bf16[8,3,256,256]{3,2,1,0:T(8,128)(2,1)S(1)} %copy-done.2, bf16[16,56,128]{2,1,0:T(8,128)(2,1)S(1)} %all_to_all.10.x_ref), custom_call_target="tpu_custom_call" | custom-call | flops 25165824 | bytes 3145728 | tf_op jit(solution)/shard_map/sum/pallas_call | solution.py:215
Async XLA Ops:
  0.0 0.8 %copy-start.3 = (bf16[8,8,256]{2,1,0:T(8,128)(2,1)S(1)}, bf16[8,8,256]{2,1,0:T(8,128)(2,1)}, u32[]{:S(2)}) copy-start(bf16[8,8,256]{2,1,0:T(8,128)(2,1)} %src_ref.3) | copy-start | bytes 98308
  0.8 0.7 %copy-start.7 = (s32[1,16,2]{1,2,0:T(2,128)S(1)}, s32[1,16,2]{1,2,0:T(2,128)}, u32[]{:S(2)}) copy-start(s32[1,16,2]{1,2,0:T(2,128)} %param.12) | copy-start | bytes 388
  1.4 0.7 %copy-start.8 = (s32[1,16,2]{1,2,0:T(2,128)S(1)}, s32[1,16,2]{1,2,0:T(2,128)}, u32[]{:S(2)}) copy-start(s32[1,16,2]{1,2,0:T(2,128)} %param.14) | copy-start | bytes 388
  2.1 17.6 %copy-start = (bf16[256,32,256]{2,1,0:T(8,128)(2,1)S(1)}, bf16[256,32,256]{2,1,0:T(8,128)(2,1)}, u32[]{:S(2)}) copy-start(bf16[256,32,256]{2,1,0:T(8,128)(2,1)} %u_ref.1) | copy-start | bytes 12582916
  2.1 17.6 %copy-start.1 = (bf16[256,32,256]{2,1,0:T(8,128)(2,1)S(1)}, bf16[256,32,256]{2,1,0:T(8,128)(2,1)}, u32[]{:S(2)}) copy-start(bf16[256,32,256]{2,1,0:T(8,128)(2,1)} %v_ref.1) | copy-start | bytes 12582916
  2.1 17.6 %copy-start.5 = (s32[256]{0:T(256)S(1)}, s32[256]{0:T(256)}, u32[]{:S(2)}) copy-start(s32[256]{0:T(256)} %slot_ref.1) | copy-start | bytes 3076
  2.1 17.6 %copy-start.6 = (s32[256]{0:T(256)S(1)}, s32[256]{0:T(256)}, u32[]{:S(2)}) copy-start(s32[256]{0:T(256)} %dest_ref.1) | copy-start | bytes 3076
  19.7 14.3 %copy-start.2 = (bf16[8,3,256,256]{3,2,1,0:T(8,128)(2,1)S(1)}, bf16[8,3,256,256]{3,2,1,0:T(8,128)(2,1)}, u32[]{:S(2)}) copy-start(bf16[8,3,256,256]{3,2,1,0:T(8,128)(2,1)} %near_ref.1) | copy-start | bytes 9437188
  19.8 14.3 %copy-start.4 = (bf16[8,8,256]{2,1,0:T(8,128)(2,1)S(1)}, bf16[8,8,256]{2,1,0:T(8,128)(2,1)}, u32[]{:S(2)}) copy-start(bf16[8,8,256]{2,1,0:T(8,128)(2,1)} %src_ref.3) | copy-start | bytes 98308

commit v6 on v5

--- a/solution.py
+++ b/solution.py
@@ -15,7 +15,14 @@
     return [x[:, :w], x[:, w:]]
 
 
-def pack_kernel(send_ref, ret_ref, src_ref, out_ref):
+def pattern_kernel(out_ref):
+    nvec, width = out_ref.shape
+    lane = lax.broadcasted_iota(jnp.int32, (nvec, width), 1)
+    sub = lax.broadcasted_iota(jnp.int32, (nvec, width), 0)
+    out_ref[...] = jnp.where(lane % nvec == sub, lane // nvec, -2).astype(jnp.float32)
+
+
+def pack_kernel(send_ref, ret_ref, src_ref, pattern_ref, out_ref):
     clusters, nvec, leaf = src_ref.shape
     cap, peers = send_ref.shape
     me = lax.axis_index("clus")
@@ -134,14 +141,12 @@
     out_ref[...] = acc[...].reshape(out_ref.shape).astype(out_ref.dtype)
 
 
-def sum_kernel(back_ref, src_ref, near_ref, x_ref, out_ref, place):
+def sum_kernel(back_ref, src_ref, near_ref, x_ref, pattern_ref, out_ref, place):
     clusters, nvec, leaf = src_ref.shape
     peers, back_rows, _ = back_ref.shape
     cap = back_rows // nvec
     width = leaf // 2
-    lane = lax.broadcasted_iota(jnp.int32, (nvec, width), 1)
-    sub = lax.broadcasted_iota(jnp.int32, (nvec, width), 0)
-    cluster = jnp.where(lane % nvec == sub, lane // nvec, -2).astype(jnp.float32)
+    cluster = pattern_ref[...]
 
     def step(p, carry):
         meta = x_ref[p, 2 * (cap + 1) * nvec :, :].astype(jnp.float32)
@@ -163,10 +168,12 @@
     after = jnp.where(me < peers - 1, after, 0.0).astype(jnp.bfloat16)
     rows = [before] + [src_ref[s] for s in range(clusters)] + [after]
     for s in range(clusters):
-        total = far_part[s * nvec : (s + 1) * nvec]
-        for o in range(3):
-            total += jnp.dot(rows[s + o], near_ref[s, o], preferred_element_type=jnp.float32)
-        out_ref[s] = total
+        total = jnp.dot(
+            jnp.concatenate(rows[s : s + 3], axis=1),
+            near_ref[s].reshape(3 * leaf, leaf),
+            preferred_element_type=jnp.float32,
+        )
+        out_ref[s] = far_part[s * nvec : (s + 1) * nvec] + total
 
 
 def cost(flops, moved):
@@ -180,15 +187,23 @@
     slots = peers * cap
     rows = 2 * (cap + 1) * nvec + nvec
     params = pltpu.CompilerParams(vmem_limit_bytes=8 * 2**20)
+    pattern = pl.pallas_call(
+        pattern_kernel,
+        out_shape=jax.ShapeDtypeStruct((nvec, leaf // 2), jnp.float32),
+        out_specs=VMEM,
+        compiler_params=params,
+        cost_estimate=cost(10**10, nvec * leaf * 2),
+        name="pattern",
+    )()
     message = pl.pallas_call(
         pack_kernel,
         out_shape=jax.ShapeDtypeStruct((peers, rows, leaf // 2), jnp.bfloat16),
-        in_specs=[SMEM, SMEM, VMEM],
+        in_specs=[SMEM, SMEM, VMEM, VMEM],
         out_specs=VMEM,
         compiler_params=params,
         cost_estimate=cost(10**10, peers * rows * leaf),
         name="pack",
-    )(send_list[0].T, ret_list[0].T, sources)
+    )(send_list[0].T, ret_list[0].T, sources, pattern)
     incoming = lax.all_to_all(message, "clus", split_axis=0, concat_axis=0, tiled=True)
     few = slots <= 32
     if few:
@@ -215,13 +230,13 @@
     return pl.pallas_call(
         sum_kernel,
         out_shape=jax.ShapeDtypeStruct((clusters, nvec, leaf), jnp.float32),
-        in_specs=[VMEM] * 4,
+        in_specs=[VMEM] * 5,
         out_specs=VMEM,
         scratch_shapes=[pltpu.VMEM((slots * nvec, leaf // 2), jnp.float32)],
         compiler_params=params,
         cost_estimate=cost(2 * 3 * clusters * nvec * leaf * leaf, 6 * clusters * leaf * leaf),
         name="sum",
-    )(back, sources, near_blocks, incoming)
+    )(back, sources, near_blocks, incoming, pattern)
 
 
 def solution(mesh):

time: 35.5 us -> 34.1 us (0.961)
  local copies, waits for them, and re-layouts: 2.14 us -> 0.78 us
    unnamed x18 -> x16, local copies, waits for them, and re-layouts: 2.14 us -> 0.78 us
where the time goes in v6:
time: 34.1 us; the launch traced here: 33.9 us
  blocking collectives  27.5 us (81%)
  Pallas kernels  5.56 us (16%)
  local copies, waits for them, and re-layouts  0.78 us (2%)
    all_to_all x1, blocking collectives, body(): lax.all_to_all(message, 'clus', split_axis=0, concat_axis=0, tiled=True)  16.9 us
    all_to_all x1, blocking collectives, body(): lax.all_to_all(returns, 'clus', split_axis=0, concat_axis=0, tiled=True)  10.6 us
    pallas_call x1, Pallas kernels, body(): pl.pallas_call(far_kernel if few else far_many_kernel, out_shape=jax.Shap...  3.68 us
    pallas_call x1, Pallas kernels, body(): pl.pallas_call(sum_kernel, out_shape=jax.ShapeDtypeStruct((clusters, nvec...  1.23 us
    unnamed x16, local copies, waits for them, and re-layouts  0.78 us

profile of v6, /device:TPU:0, one launch (start us, length us, event | category | flops | bytes accessed | tf_op | source)
XLA Modules:
  0.0 33.9 jit_solution(18392256547684199851)
XLA Ops:
  0.0 0.0 copy-start.3
  0.0 0.0 copy-start.7
  0.0 0.0 copy-start.6
  0.0 0.7 %copy-done.3 = bf16[8,8,256]{2,1,0:T(8,128)(2,1)S(1)} copy-done((bf16[8,8,256]{2,1,0:T(8,128)(2,1)S(1)}, bf16[8,8,256]{2,1,0:T(8,128)(2,1)}, u32[]{:S(2)}) %copy-start.3) | copy-done | bytes 32792
  0.8 0.0 copy-done.7
  0.8 0.0 copy-done.6
  0.8 0.0 copy-start
  0.8 0.0 copy-start.1
  0.8 0.0 copy-start.4
  0.8 0.0 copy-start.5
  0.8 0.6 %pack.1 = bf16[16,56,128]{2,1,0:T(8,128)(2,1)S(1)} custom-call(s32[2,16]{1,0:T(2,128)S(1)} %bitcast.6, s32[2,16]{1,0:T(2,128)S(1)} %bitcast.7, bf16[8,8,256]{2,1,0:T(8,128)(2,1)S(1)} %copy-done.3, f32[8,128]{1,0:T(8,128)S(1)} %pattern.1.pattern_ref), custom_call_target="tpu_custom_call" | custom-call | flops 10000000000 | bytes 229376 | tf_op jit(solution)/shard_map/pack/pallas_call | solution.py:198
  1.4 16.9 %all_to_all.10.x_ref = bf16[16,56,128]{2,1,0:T(8,128)(2,1)S(1)} all-to-all(bf16[16,56,128]{2,1,0:T(8,128)(2,1)S(1)} %pack.1), channel_id=1, replica_groups=mesh['groups'=2,'clus'=16] {'clus'}, dimensions={0} | all-to-all | bytes 458752 | tf_op jit(solution)/shard_map/all_to_all | solution.py:207
  18.4 0.0 copy-done
  18.4 0.0 copy-done.1
  18.4 0.0 copy-done.4
  18.4 0.0 copy-done.5
  18.4 0.0 copy-start.2
  18.4 3.7 %far.1 = bf16[16,16,256]{2,1,0:T(8,128)(2,1)S(1)} custom-call(s32[256]{0:T(256)S(1)} %copy-done.4, s32[256]{0:T(256)S(1)} %copy-done.5, bf16[16,56,128]{2,1,0:T(8,128)(2,1)S(1)} %all_to_all.10.x_ref, bf16[256,32,256]{2,1,0:T(8,128)(2,1)S(1)} %copy-done, bf16[256,32,256]{2,1,0:T(8,128)(2,1)S(1)} %copy-done.1), custom_call_target="tpu_custom_call" | custom-call | flops 536870912 | bytes 8388608 | tf_op jit(solution)/shard_map/far/pallas_call | solution.py:219
  22.1 10.6 %all_to_all.11.back_ref = bf16[16,16,256]{2,1,0:T(8,128)(2,1)S(1)} all-to-all(bf16[16,16,256]{2,1,0:T(8,128)(2,1)S(1)} %far.1), channel_id=1, replica_groups=mesh['groups'=2,'clus'=16] {'clus'}, dimensions={0} | all-to-all | bytes 262144 | tf_op jit(solution)/shard_map/all_to_all | solution.py:229
  32.7 0.0 copy-done.2
  32.7 1.2 %sum.1 = f32[8,8,256]{2,1,0:T(8,128)} custom-call(bf16[16,16,256]{2,1,0:T(8,128)(2,1)S(1)} %all_to_all.11.back_ref, bf16[8,8,256]{2,1,0:T(8,128)(2,1)S(1)} %copy-done.3, bf16[8,3,256,256]{3,2,1,0:T(8,128)(2,1)S(1)} %copy-done.2, bf16[16,56,128]{2,1,0:T(8,128)(2,1)S(1)} %all_to_all.10.x_ref, f32[8,128]{1,0:T(8,128)S(1)} %pattern.1.pattern_ref), custom_call_target="tpu_custom_call" | custom-call | flops 25165824 | bytes 3145728 | tf_op jit(solution)/shard_map/sum/pallas_call | solution.py:230
  (1 shorter events, 0.0 us)
Async XLA Ops:
  0.0 0.8 %copy-start.3 = (bf16[8,8,256]{2,1,0:T(8,128)(2,1)S(1)}, bf16[8,8,256]{2,1,0:T(8,128)(2,1)}, u32[]{:S(2)}) copy-start(bf16[8,8,256]{2,1,0:T(8,128)(2,1)} %src_ref.3) | copy-start | bytes 98308
  0.0 0.8 %copy-start.7 = (s32[1,16,2]{1,2,0:T(2,128)S(1)}, s32[1,16,2]{1,2,0:T(2,128)}, u32[]{:S(2)}) copy-start(s32[1,16,2]{1,2,0:T(2,128)} %param.14) | copy-start | bytes 388
  0.0 0.8 %copy-start.6 = (s32[1,16,2]{1,2,0:T(2,128)S(1)}, s32[1,16,2]{1,2,0:T(2,128)}, u32[]{:S(2)}) copy-start(s32[1,16,2]{1,2,0:T(2,128)} %param.12) | copy-start | bytes 388
  0.8 17.6 %copy-start = (bf16[256,32,256]{2,1,0:T(8,128)(2,1)S(1)}, bf16[256,32,256]{2,1,0:T(8,128)(2,1)}, u32[]{:S(2)}) copy-start(bf16[256,32,256]{2,1,0:T(8,128)(2,1)} %u_ref.1) | copy-start | bytes 12582916
  0.8 17.6 %copy-start.1 = (bf16[256,32,256]{2,1,0:T(8,128)(2,1)S(1)}, bf16[256,32,256]{2,1,0:T(8,128)(2,1)}, u32[]{:S(2)}) copy-start(bf16[256,32,256]{2,1,0:T(8,128)(2,1)} %v_ref.1) | copy-start | bytes 12582916
  0.8 17.6 %copy-start.4 = (s32[256]{0:T(256)S(1)}, s32[256]{0:T(256)}, u32[]{:S(2)}) copy-start(s32[256]{0:T(256)} %slot_ref.1) | copy-start | bytes 3076
  0.8 17.6 %copy-start.5 = (s32[256]{0:T(256)S(1)}, s32[256]{0:T(256)}, u32[]{:S(2)}) copy-start(s32[256]{0:T(256)} %dest_ref.1) | copy-start | bytes 3076
  18.4 14.3 %copy-start.2 = (bf16[8,3,256,256]{3,2,1,0:T(8,128)(2,1)S(1)}, bf16[8,3,256,256]{3,2,1,0:T(8,128)(2,1)}, u32[]{:S(2)}) copy-start(bf16[8,3,256,256]{3,2,1,0:T(8,128)(2,1)} %near_ref.1) | copy-start | bytes 9437188

commit v7 on v6

--- a/solution.py
+++ b/solution.py
@@ -67,6 +67,22 @@
     lax.fori_loop(0, peers, widen, 0, unroll=min(peers, 16))
 
 
+def placement(x_ref, pattern_ref, place, place_out):
+    nvec, width = pattern_ref.shape
+    peers, rows, _ = x_ref.shape
+    cap = place.shape[0] // (peers * nvec)
+
+    def step(p, carry):
+        meta = x_ref[p, rows - nvec :, :].astype(jnp.float32)
+        for k in range(cap):
+            at = jnp.broadcast_to(meta[k * nvec // cap : k * nvec // cap + 1], (nvec, width))
+            place[pl.ds((p * cap + k) * nvec, nvec)] = jnp.where(at == pattern_ref[...], 1.0, 0.0)
+        return carry
+
+    lax.fori_loop(0, peers, step, 0, unroll=min(peers, 16))
+    place_out[...] = place[...].T[: place_out.shape[0]].astype(jnp.bfloat16)
+
+
 def project(picked, u, owner, nvec, group):
     full = lax.dot_general(picked, u, (((1,), (1,)), ((), ())), preferred_element_type=jnp.float32)
     kept = full[:nvec]
@@ -75,7 +91,7 @@
     return kept
 
 
-def far_kernel(slot_ref, dest_ref, x_ref, u_ref, v_ref, out_ref, xf, picked, wide):
+def far_kernel(slot_ref, dest_ref, x_ref, u_ref, v_ref, pattern_ref, out_ref, place_out, xf, place, picked, wide, acc):
     peers = x_ref.shape[0]
     slots, nvec, leaf = xf.shape
     blocks, rank, _ = u_ref.shape
@@ -83,18 +99,21 @@
     groups = blocks // group
     per = groups // CHUNKS
     widen_sources(x_ref, xf)
-    for g in range(groups):
-        rows = [xf[slot_ref[g * group + i]] for i in range(group)]
-        picked[g] = jnp.concatenate(rows, axis=0).astype(jnp.bfloat16)
+    placement(x_ref, pattern_ref, place, place_out)
     owner = lax.broadcasted_iota(jnp.int32, (nvec, leaf), 1) // rank
-    total = None
-    for c in range(CHUNKS):
-        for g in range(c * per, (c + 1) * per):
-            u = u_ref[g * group : (g + 1) * group].reshape(leaf, leaf)
+    acc[...] = jnp.zeros_like(acc)
+
+    def chunk(c, carry):
+        first = c * per
+        for g in range(per):
+            rows = [xf[slot_ref[(first + g) * group + i]] for i in range(group)]
+            picked[g] = jnp.concatenate(rows, axis=0).astype(jnp.bfloat16)
+        for g in range(per):
+            u = u_ref[pl.ds((first + g) * group, group)].reshape(leaf, leaf)
             kept = project(picked[g], u, owner, nvec, group)
-            dest = jnp.full((nvec, leaf), dest_ref[g * group], jnp.int32)
+            dest = jnp.full((nvec, leaf), dest_ref[(first + g) * group], jnp.int32)
             for i in range(1, group):
-                dest = jnp.where(owner == i, dest_ref[g * group + i], dest)
+                dest = jnp.where(owner == i, dest_ref[(first + g) * group + i], dest)
             dest = dest.astype(jnp.float32)
             kept = jnp.concatenate([kept, kept], axis=0).astype(jnp.bfloat16)
             dest = jnp.concatenate([dest, dest - 1.0], axis=0).astype(jnp.bfloat16)
@@ -102,19 +121,20 @@
                 wide[o * nvec : (o + 2) * nvec, g * leaf : (g + 1) * leaf] = jnp.where(
                     dest == jnp.bfloat16(o), kept, jnp.bfloat16(0)
                 )
-        v = v_ref[c * per * group : (c + 1) * per * group].reshape(per * leaf, leaf)
-        part = jnp.dot(
-            wide[:, c * per * leaf : (c + 1) * per * leaf], v, preferred_element_type=jnp.float32
-        )
-        total = part if total is None else total + part
-    out_ref[...] = total.reshape(out_ref.shape).astype(out_ref.dtype)
-
-
-def far_many_kernel(slot_ref, dest_ref, x_ref, u_ref, v_ref, out_ref, xf, coef, acc):
+        v = v_ref[pl.ds(first * group, per * group)].reshape(per * leaf, leaf)
+        acc[...] += jnp.dot(wide[...], v, preferred_element_type=jnp.float32)
+        return carry
+
+    lax.fori_loop(0, CHUNKS, chunk, 0)
+    out_ref[...] = acc[...].reshape(out_ref.shape).astype(out_ref.dtype)
+
+
+def far_many_kernel(slot_ref, dest_ref, x_ref, u_ref, v_ref, pattern_ref, out_ref, place_out, xf, place, coef, acc):
     slots, nvec, leaf = xf.shape
     blocks, rank, _ = u_ref.shape
     group = leaf // rank
     widen_sources(x_ref, xf)
+    placement(x_ref, pattern_ref, place, place_out)
     acc[...] = jnp.zeros_like(acc)
     owner = lax.broadcasted_iota(jnp.int32, (nvec, leaf), 1) // rank
 
@@ -141,24 +161,12 @@
     out_ref[...] = acc[...].reshape(out_ref.shape).astype(out_ref.dtype)
 
 
-def sum_kernel(back_ref, src_ref, near_ref, x_ref, pattern_ref, out_ref, place):
+def sum_kernel(back_ref, src_ref, near_ref, x_ref, place_ref, out_ref):
     clusters, nvec, leaf = src_ref.shape
     peers, back_rows, _ = back_ref.shape
     cap = back_rows // nvec
-    width = leaf // 2
-    cluster = pattern_ref[...]
-
-    def step(p, carry):
-        meta = x_ref[p, 2 * (cap + 1) * nvec :, :].astype(jnp.float32)
-        for k in range(cap):
-            at = jnp.broadcast_to(meta[k * nvec // cap : k * nvec // cap + 1], (nvec, width))
-            place[pl.ds((p * cap + k) * nvec, nvec)] = jnp.where(at == cluster, 1.0, 0.0)
-        return carry
-
-    lax.fori_loop(0, peers, step, 0, unroll=min(peers, 16))
-    spread = place[...].T[: clusters * nvec].astype(jnp.bfloat16)
     terms = back_ref[...].reshape(peers * back_rows, leaf)
-    far_part = jnp.dot(spread, terms, preferred_element_type=jnp.float32)
+    far_part = jnp.dot(place_ref[...], terms, preferred_element_type=jnp.float32)
 
     me = lax.axis_index("clus")
     edge = slice(2 * cap * nvec, 2 * (cap + 1) * nvec)
@@ -208,35 +216,42 @@
     few = slots <= 32
     if few:
         scratch = [
-            pltpu.VMEM((blocks * rank // leaf, leaf // rank * nvec, leaf), jnp.bfloat16),
-            pltpu.VMEM((slots * nvec, blocks * rank), jnp.bfloat16),
+            pltpu.VMEM((blocks * rank // leaf // CHUNKS, leaf // rank * nvec, leaf), jnp.bfloat16),
+            pltpu.VMEM((slots * nvec, blocks * rank // CHUNKS), jnp.bfloat16),
+            pltpu.VMEM((slots * nvec, leaf), jnp.float32),
         ]
     else:
         scratch = [
             pltpu.VMEM((blocks * rank // leaf, nvec, leaf), jnp.float32),
             pltpu.VMEM((slots, nvec, leaf), jnp.float32),
         ]
-    returns = pl.pallas_call(
+    returns, place = pl.pallas_call(
         far_kernel if few else far_many_kernel,
-        out_shape=jax.ShapeDtypeStruct((peers, cap * nvec, leaf), jnp.bfloat16),
-        in_specs=[SMEM, SMEM, VMEM, VMEM, VMEM],
-        out_specs=VMEM,
-        scratch_shapes=[pltpu.VMEM((slots, nvec, leaf), jnp.float32)] + scratch,
+        out_shape=(
+            jax.ShapeDtypeStruct((peers, cap * nvec, leaf), jnp.bfloat16),
+            jax.ShapeDtypeStruct((clusters * nvec, slots * nvec), jnp.bfloat16),
+        ),
+        in_specs=[SMEM, SMEM, VMEM, VMEM, VMEM, VMEM],
+        out_specs=(VMEM, VMEM),
+        scratch_shapes=[
+            pltpu.VMEM((slots, nvec, leaf), jnp.float32),
+            pltpu.VMEM((slots * nvec, leaf // 2), jnp.float32),
+        ]
+        + scratch,
         compiler_params=pltpu.CompilerParams(vmem_limit_bytes=16 * 2**20),
         cost_estimate=cost(4 * blocks * 8 * nvec * leaf * rank, 4 * blocks * rank * leaf),
         name="far",
-    )(far_slot, ret_slot, incoming, far_u, far_v)
+    )(far_slot, ret_slot, incoming, far_u, far_v, pattern)
     back = lax.all_to_all(returns, "clus", split_axis=0, concat_axis=0, tiled=True)
     return pl.pallas_call(
         sum_kernel,
         out_shape=jax.ShapeDtypeStruct((clusters, nvec, leaf), jnp.float32),
         in_specs=[VMEM] * 5,
         out_specs=VMEM,
-        scratch_shapes=[pltpu.VMEM((slots * nvec, leaf // 2), jnp.float32)],
         compiler_params=params,
         cost_estimate=cost(2 * 3 * clusters * nvec * leaf * leaf, 6 * clusters * leaf * leaf),
         name="sum",
-    )(back, sources, near_blocks, incoming, pattern)
+    )(back, sources, near_blocks, incoming, place)
 
 
 def solution(mesh):

time: 34.1 us -> 34.6 us (1.015)
  Pallas kernels: 5.56 us -> 6.02 us
    pallas_call x1, Pallas kernels: 3.68 us -> 4.17 us  [body(): pl.pallas_call(far_kernel if few else far_many_kernel, out_shape=(jax.Sha...]
where the time goes in v7:
time: 34.6 us; the launch traced here: 34.4 us
  blocking collectives  27.5 us (79%)
  Pallas kernels  6.02 us (17%)
  local copies, waits for them, and re-layouts  0.78 us (2%)
    all_to_all x1, blocking collectives, body(): lax.all_to_all(message, 'clus', split_axis=0, concat_axis=0, tiled=True)  16.9 us
    all_to_all x1, blocking collectives, body(): lax.all_to_all(returns, 'clus', split_axis=0, concat_axis=0, tiled=True)  10.6 us
    pallas_call x1, Pallas kernels, body(): pl.pallas_call(far_kernel if few else far_many_kernel, out_shape=(jax.Sha...  4.17 us
    pallas_call x1, Pallas kernels, body(): pl.pallas_call(sum_kernel, out_shape=jax.ShapeDtypeStruct((clusters, nvec...  1.2 us
    unnamed x16, local copies, waits for them, and re-layouts  0.78 us

profile of v7, /device:TPU:0, one launch (start us, length us, event | category | flops | bytes accessed | tf_op | source)
XLA Modules:
  0.0 34.4 jit_solution(1588234091965525241)
XLA Ops:
  0.0 0.0 copy-start.3
  0.0 0.0 copy-start.7
  0.0 0.0 copy-start.6
  0.0 0.7 %copy-done.3 = bf16[8,8,256]{2,1,0:T(8,128)(2,1)S(1)} copy-done((bf16[8,8,256]{2,1,0:T(8,128)(2,1)S(1)}, bf16[8,8,256]{2,1,0:T(8,128)(2,1)}, u32[]{:S(2)}) %copy-start.3) | copy-done | bytes 32792
  0.8 0.0 copy-done.7
  0.8 0.0 copy-done.6
  0.8 0.0 copy-start
  0.8 0.0 copy-start.1
  0.8 0.0 copy-start.4
  0.8 0.0 copy-start.5
  0.8 0.6 %pack.1 = bf16[16,56,128]{2,1,0:T(8,128)(2,1)S(1)} custom-call(s32[2,16]{1,0:T(2,128)S(1)} %bitcast.6, s32[2,16]{1,0:T(2,128)S(1)} %bitcast.7, bf16[8,8,256]{2,1,0:T(8,128)(2,1)S(1)} %copy-done.3, f32[8,128]{1,0:T(8,128)S(1)} %pattern.1.pattern_ref), custom_call_target="tpu_custom_call" | custom-call | flops 10000000000 | bytes 229376 | tf_op jit(solution)/shard_map/pack/pallas_call | solution.py:206
  1.4 16.9 %all_to_all.10.x_ref = bf16[16,56,128]{2,1,0:T(8,128)(2,1)S(1)} all-to-all(bf16[16,56,128]{2,1,0:T(8,128)(2,1)S(1)} %pack.1), channel_id=1, replica_groups=mesh['groups'=2,'clus'=16] {'clus'}, dimensions={0} | all-to-all | bytes 458752 | tf_op jit(solution)/shard_map/all_to_all | solution.py:215
  18.4 0.0 copy-done
  18.4 0.0 copy-done.1
  18.4 0.0 copy-done.4
  18.4 0.0 copy-done.5
  18.4 0.0 copy-start.2
  18.4 4.2 %far.1 = (bf16[16,16,256]{2,1,0:T(8,128)(2,1)S(1)}, bf16[64,256]{1,0:T(8,128)(2,1)S(1)}) custom-call(s32[256]{0:T(256)S(1)} %copy-done.4, s32[256]{0:T(256)S(1)} %copy-done.5, bf16[16,56,128]{2,1,0:T(8,128)(2,1)S(1)} %all_to_all.10.x_ref, bf16[256,32,256]{2,1,0:T(8,128)(2,1)S(1)} %copy-done, bf16[256,32,256]{2,1,0:T(8,128)(2,1)S(1)} %copy-done.1, ...), custom_call_target="tpu_custom_call" | custom-call | flops 536870912 | bytes 8388608 | tf_op jit(solution)/shard_map/far/pallas_call | solution.py:228
  22.6 10.6 %all_to_all.11.back_ref = bf16[16,16,256]{2,1,0:T(8,128)(2,1)S(1)} all-to-all(bf16[16,16,256]{2,1,0:T(8,128)(2,1)S(1)} %get-tuple-element.7), channel_id=1, replica_groups=mesh['groups'=2,'clus'=16] {'clus'}, dimensions={0} | all-to-all | bytes 262144 | tf_op jit(solution)/shard_map/all_to_all | solution.py:245
  33.2 0.0 copy-done.2
  33.2 1.2 %sum.1 = f32[8,8,256]{2,1,0:T(8,128)} custom-call(bf16[16,16,256]{2,1,0:T(8,128)(2,1)S(1)} %all_to_all.11.back_ref, bf16[8,8,256]{2,1,0:T(8,128)(2,1)S(1)} %copy-done.3, bf16[8,3,256,256]{3,2,1,0:T(8,128)(2,1)S(1)} %copy-done.2, bf16[16,56,128]{2,1,0:T(8,128)(2,1)S(1)} %all_to_all.10.x_ref, bf16[64,256]{1,0:T(8,128)(2,1)S(1)} %get-tuple-element.8.place_ref), custom_call_target="tpu_custom_call" | custom-call | flops 25165824 | bytes 3145728 | tf_op jit(solution)/shard_map/sum/pallas_call | solution.py:246
  (1 shorter events, 0.0 us)
Async XLA Ops:
  0.0 0.8 %copy-start.3 = (bf16[8,8,256]{2,1,0:T(8,128)(2,1)S(1)}, bf16[8,8,256]{2,1,0:T(8,128)(2,1)}, u32[]{:S(2)}) copy-start(bf16[8,8,256]{2,1,0:T(8,128)(2,1)} %src_ref.3) | copy-start | bytes 98308
  0.0 0.8 %copy-start.7 = (s32[1,16,2]{1,2,0:T(2,128)S(1)}, s32[1,16,2]{1,2,0:T(2,128)}, u32[]{:S(2)}) copy-start(s32[1,16,2]{1,2,0:T(2,128)} %param.14) | copy-start | bytes 388
  0.0 0.8 %copy-start.6 = (s32[1,16,2]{1,2,0:T(2,128)S(1)}, s32[1,16,2]{1,2,0:T(2,128)}, u32[]{:S(2)}) copy-start(s32[1,16,2]{1,2,0:T(2,128)} %param.12) | copy-start | bytes 388
  0.8 17.6 %copy-start = (bf16[256,32,256]{2,1,0:T(8,128)(2,1)S(1)}, bf16[256,32,256]{2,1,0:T(8,128)(2,1)}, u32[]{:S(2)}) copy-start(bf16[256,32,256]{2,1,0:T(8,128)(2,1)} %u_ref.1) | copy-start | bytes 12582916
  0.8 17.6 %copy-start.1 = (bf16[256,32,256]{2,1,0:T(8,128)(2,1)S(1)}, bf16[256,32,256]{2,1,0:T(8,128)(2,1)}, u32[]{:S(2)}) copy-start(bf16[256,32,256]{2,1,0:T(8,128)(2,1)} %v_ref.1) | copy-start | bytes 12582916
  0.8 17.6 %copy-start.4 = (s32[256]{0:T(256)S(1)}, s32[256]{0:T(256)}, u32[]{:S(2)}) copy-start(s32[256]{0:T(256)} %slot_ref.1) | copy-start | bytes 3076
  0.8 17.6 %copy-start.5 = (s32[256]{0:T(256)S(1)}, s32[256]{0:T(256)}, u32[]{:S(2)}) copy-start(s32[256]{0:T(256)} %dest_ref.1) | copy-start | bytes 3076
  18.4 14.8 %copy-start.2 = (bf16[8,3,256,256]{3,2,1,0:T(8,128)(2,1)S(1)}, bf16[8,3,256,256]{3,2,1,0:T(8,128)(2,1)}, u32[]{:S(2)}) copy-start(bf16[8,3,256,256]{3,2,1,0:T(8,128)(2,1)} %near_ref.1) | copy-start | bytes 9437188

commit v8 on v6

--- a/solution.py
+++ b/solution.py
@@ -25,6 +25,7 @@
 def pack_kernel(send_ref, ret_ref, src_ref, pattern_ref, out_ref):
     clusters, nvec, leaf = src_ref.shape
     cap, peers = send_ref.shape
+    inner = out_ref.shape[0]
     me = lax.axis_index("clus")
     first = src_ref[0].astype(jnp.float32)
     last = src_ref[clusters - 1].astype(jnp.float32)
@@ -43,10 +44,34 @@
                 axis=0,
             )
         )
-        out_ref[p] = jnp.concatenate(rows, axis=0).astype(out_ref.dtype)
+        out_ref[p % inner, p // inner] = jnp.concatenate(rows, axis=0).astype(out_ref.dtype)
         return carry
 
     lax.fori_loop(0, peers, step, 0, unroll=min(peers, 16))
+
+
+def regroup_kernel(x_ref, out_ref):
+    for i in range(x_ref.shape[0]):
+        for j in range(x_ref.shape[1]):
+            out_ref[j, i] = x_ref[i, j]
+
+
+def exchange(x, inner, params):
+    outer = x.shape[1]
+    rows = [[o * inner + i for i in range(inner)] for o in range(outer)]
+    columns = [[o * inner + i for o in range(outer)] for i in range(inner)]
+    x = lax.all_to_all(x, "clus", 0, 0, axis_index_groups=rows, tiled=True)
+    x = pl.pallas_call(
+        regroup_kernel,
+        out_shape=jax.ShapeDtypeStruct((outer, inner) + x.shape[2:], x.dtype),
+        in_specs=[VMEM],
+        out_specs=VMEM,
+        compiler_params=params,
+        cost_estimate=cost(0, 2 * x.size * 2),
+        name="regroup",
+    )(x)
+    x = lax.all_to_all(x, "clus", 0, 0, axis_index_groups=columns, tiled=True)
+    return x.reshape((inner * outer,) + x.shape[2:])
 
 
 def joined(rows, nvec):
@@ -73,6 +98,12 @@
     for i in range(1, group):
         kept = jnp.where(owner == i, full[i * nvec : (i + 1) * nvec], kept)
     return kept
+
+
+def put(total, out_ref):
+    inner, outer, rows, _ = out_ref.shape
+    for p in range(inner * outer):
+        out_ref[p % inner, p // inner] = total[p * rows : (p + 1) * rows].astype(out_ref.dtype)
 
 
 def far_kernel(slot_ref, dest_ref, x_ref, u_ref, v_ref, out_ref, xf, picked, wide):
@@ -107,7 +138,7 @@
             wide[:, c * per * leaf : (c + 1) * per * leaf], v, preferred_element_type=jnp.float32
         )
         total = part if total is None else total + part
-    out_ref[...] = total.reshape(out_ref.shape).astype(out_ref.dtype)
+    put(total, out_ref)
 
 
 def far_many_kernel(slot_ref, dest_ref, x_ref, u_ref, v_ref, out_ref, xf, coef, acc):
@@ -138,7 +169,7 @@
 
     lax.fori_loop(0, blocks // group, forward, 0, unroll=4)
     lax.fori_loop(0, blocks // group, backward, 0, unroll=4)
-    out_ref[...] = acc[...].reshape(out_ref.shape).astype(out_ref.dtype)
+    put(acc[...].reshape(slots * nvec, leaf), out_ref)
 
 
 def sum_kernel(back_ref, src_ref, near_ref, x_ref, pattern_ref, out_ref, place):
@@ -185,6 +216,7 @@
     _, peers, cap = send_list.shape
     blocks, rank, _ = far_u.shape
     slots = peers * cap
+    inner = 4 if peers % 4 == 0 else 1
     rows = 2 * (cap + 1) * nvec + nvec
     params = pltpu.CompilerParams(vmem_limit_bytes=8 * 2**20)
     pattern = pl.pallas_call(
@@ -197,14 +229,14 @@
     )()
     message = pl.pallas_call(
         pack_kernel,
-        out_shape=jax.ShapeDtypeStruct((peers, rows, leaf // 2), jnp.bfloat16),
+        out_shape=jax.ShapeDtypeStruct((inner, peers // inner, rows, leaf // 2), jnp.bfloat16),
         in_specs=[SMEM, SMEM, VMEM, VMEM],
         out_specs=VMEM,
         compiler_params=params,
         cost_estimate=cost(10**10, peers * rows * leaf),
         name="pack",
     )(send_list[0].T, ret_list[0].T, sources, pattern)
-    incoming = lax.all_to_all(message, "clus", split_axis=0, concat_axis=0, tiled=True)
+    incoming = exchange(message, inner, params)
     few = slots <= 32
     if few:
         scratch = [
@@ -218,7 +250,7 @@
         ]
     returns = pl.pallas_call(
         far_kernel if few else far_many_kernel,
-        out_shape=jax.ShapeDtypeStruct((peers, cap * nvec, leaf), jnp.bfloat16),
+        out_shape=jax.ShapeDtypeStruct((inner, peers // inner, cap * nvec, leaf), jnp.bfloat16),
         in_specs=[SMEM, SMEM, VMEM, VMEM, VMEM],
         out_specs=VMEM,
         scratch_shapes=[pltpu.VMEM((slots, nvec, leaf), jnp.float32)] + scratch,
@@ -226,7 +258,7 @@
         cost_estimate=cost(4 * blocks * 8 * nvec * leaf * rank, 4 * blocks * rank * leaf),
         name="far",
     )(far_slot, ret_slot, incoming, far_u, far_v)
-    back = lax.all_to_all(returns, "clus", split_axis=0, concat_axis=0, tiled=True)
+    back = exchange(returns, inner, params)
     return pl.pallas_call(
         sum_kernel,
         out_shape=jax.ShapeDtypeStruct((clusters, nvec, leaf), jnp.float32),

time: 34.1 us -> 44.9 us (1.32)
  blocking collectives: 27.5 us -> 38.1 us
    all_to_all x2 -> x4, blocking collectives: 27.5 us -> 38.1 us  [the longest x2 21.1 us: exchange(): x = lax.all_to_all(x, 'clus', 0, 0, axis_index_groups=columns, tiled=True)]
where the time goes in v8:
time: 44.9 us; the launch traced here: 44.6 us
  blocking collectives  38.1 us (85%)
  Pallas kernels  5.6 us (12%)
  local copies, waits for them, and re-layouts  0.78 us (2%)
    all_to_all x2, blocking collectives, exchange(): x = lax.all_to_all(x, 'clus', 0, 0, axis_index_groups=columns, tiled=True)  21.1 us
    all_to_all x2, blocking collectives, exchange(): x = lax.all_to_all(x, 'clus', 0, 0, axis_index_groups=rows, tiled=True)  17 us
    pallas_call x1, Pallas kernels, body(): pl.pallas_call(far_kernel if few else far_many_kernel, out_shape=jax.Shap...  3.69 us
    pallas_call x1, Pallas kernels, body(): pl.pallas_call(sum_kernel, out_shape=jax.ShapeDtypeStruct((clusters, nvec...  1.23 us

profile of v8, /device:TPU:0, one launch (start us, length us, event | category | flops | bytes accessed | tf_op | source)
XLA Modules:
  0.0 44.6 jit_solution(17214523547845114705)
XLA Ops:
  0.0 0.0 copy-start.3
  0.0 0.0 copy-start.7
  0.0 0.0 copy-start.6
  0.0 0.7 %copy-done.3 = bf16[8,8,256]{2,1,0:T(8,128)(2,1)S(1)} copy-done((bf16[8,8,256]{2,1,0:T(8,128)(2,1)S(1)}, bf16[8,8,256]{2,1,0:T(8,128)(2,1)}, u32[]{:S(2)}) %copy-start.3) | copy-done | bytes 32792
  0.8 0.0 copy-done.7
  0.8 0.0 copy-done.6
  0.8 0.0 copy-start
  0.8 0.0 copy-start.1
  0.8 0.0 copy-start.4
  0.8 0.0 copy-start.5
  0.8 0.6 %pack.1 = bf16[4,4,56,128]{3,2,1,0:T(8,128)(2,1)S(1)} custom-call(s32[2,16]{1,0:T(2,128)S(1)} %bitcast.11, s32[2,16]{1,0:T(2,128)S(1)} %bitcast.12, bf16[8,8,256]{2,1,0:T(8,128)(2,1)S(1)} %copy-done.3, f32[8,128]{1,0:T(8,128)S(1)} %pattern.1.pattern_ref), custom_call_target="tpu_custom_call" | custom-call | flops 10000000000 | bytes 229376 | tf_op jit(solution)/shard_map/pack/pallas_call | solution.py:230
  1.4 10.0 %all_to_all.20.x_ref = bf16[4,4,56,128]{3,2,1,0:T(8,128)(2,1)S(1)} all-to-all(bf16[4,4,56,128]{3,2,1,0:T(8,128)(2,1)S(1)} %pack.1), channel_id=1, replica_groups={{0,1,2,3},{4,5,6,7},{8,9,10,11},{12,13,14,15},{16,17,18,19},{20,21,22,2..., dimensions={0} | all-to-all | bytes 458752 | tf_op jit(solution)/shard_map/all_to_all | solution.py:63
  11.4 12.6 %all_to_all.21 = bf16[4,4,56,128]{3,2,1,0:T(8,128)(2,1)S(1)} all-to-all(bf16[4,4,56,128]{3,2,1,0:T(8,128)(2,1)S(1)} %regroup.2), channel_id=1, replica_groups={{0,4,8,12},{1,5,9,13},{2,6,10,14},{3,7,11,15},{16,20,24,28},{17,21,25,2..., dimensions={0} | all-to-all | bytes 458752 | tf_op jit(solution)/shard_map/all_to_all | solution.py:73
  24.0 0.0 copy-done
  24.0 0.0 copy-done.1
  24.0 0.0 copy-done.4
  24.0 0.0 copy-done.5
  24.0 0.0 copy-start.2
  24.0 3.7 %far.1 = bf16[4,4,16,256]{3,2,1,0:T(8,128)(2,1)S(1)} custom-call(s32[256]{0:T(256)S(1)} %copy-done.4, s32[256]{0:T(256)S(1)} %copy-done.5, bf16[16,56,128]{2,1,0:T(8,128)(2,1)S(1)} %bitcast.8, bf16[256,32,256]{2,1,0:T(8,128)(2,1)S(1)} %copy-done, bf16[256,32,256]{2,1,0:T(8,128)(2,1)S(1)} %copy-done.1), custom_call_target="tpu_custom_call" | custom-call | flops 536870912 | bytes 8388608 | tf_op jit(solution)/shard_map/far/pallas_call | solution.py:251
  27.7 7.0 %all_to_all.22.x_ref = bf16[4,4,16,256]{3,2,1,0:T(8,128)(2,1)S(1)} all-to-all(bf16[4,4,16,256]{3,2,1,0:T(8,128)(2,1)S(1)} %far.1), channel_id=1, replica_groups={{0,1,2,3},{4,5,6,7},{8,9,10,11},{12,13,14,15},{16,17,18,19},{20,21,22,2..., dimensions={0} | all-to-all | bytes 262144 | tf_op jit(solution)/shard_map/all_to_all | solution.py:63
  34.8 8.6 %all_to_all.23 = bf16[4,4,16,256]{3,2,1,0:T(8,128)(2,1)S(1)} all-to-all(bf16[4,4,16,256]{3,2,1,0:T(8,128)(2,1)S(1)} %regroup.3), channel_id=1, replica_groups={{0,4,8,12},{1,5,9,13},{2,6,10,14},{3,7,11,15},{16,20,24,28},{17,21,25,2..., dimensions={0} | all-to-all | bytes 262144 | tf_op jit(solution)/shard_map/all_to_all | solution.py:73
  43.3 0.0 copy-done.2
  43.3 1.2 %sum.1 = f32[8,8,256]{2,1,0:T(8,128)} custom-call(bf16[16,16,256]{2,1,0:T(8,128)(2,1)S(1)} %bitcast.10, bf16[8,8,256]{2,1,0:T(8,128)(2,1)S(1)} %copy-done.3, bf16[8,3,256,256]{3,2,1,0:T(8,128)(2,1)S(1)} %copy-done.2, bf16[16,56,128]{2,1,0:T(8,128)(2,1)S(1)} %bitcast.9, f32[8,128]{1,0:T(8,128)S(1)} %pattern.1.pattern_ref), custom_call_target="tpu_custom_call" | custom-call | flops 25165824 | bytes 3145728 | tf_op jit(solution)/shard_map/sum/pallas_call | solution.py:262
  (3 shorter events, 0.0 us)
Async XLA Ops:
  0.0 0.8 %copy-start.3 = (bf16[8,8,256]{2,1,0:T(8,128)(2,1)S(1)}, bf16[8,8,256]{2,1,0:T(8,128)(2,1)}, u32[]{:S(2)}) copy-start(bf16[8,8,256]{2,1,0:T(8,128)(2,1)} %src_ref.3) | copy-start | bytes 98308
  0.0 0.8 %copy-start.7 = (s32[1,16,2]{1,2,0:T(2,128)S(1)}, s32[1,16,2]{1,2,0:T(2,128)}, u32[]{:S(2)}) copy-start(s32[1,16,2]{1,2,0:T(2,128)} %param.14) | copy-start | bytes 388
  0.0 0.8 %copy-start.6 = (s32[1,16,2]{1,2,0:T(2,128)S(1)}, s32[1,16,2]{1,2,0:T(2,128)}, u32[]{:S(2)}) copy-start(s32[1,16,2]{1,2,0:T(2,128)} %param.12) | copy-start | bytes 388
  0.8 23.3 %copy-start = (bf16[256,32,256]{2,1,0:T(8,128)(2,1)S(1)}, bf16[256,32,256]{2,1,0:T(8,128)(2,1)}, u32[]{:S(2)}) copy-start(bf16[256,32,256]{2,1,0:T(8,128)(2,1)} %u_ref.1) | copy-start | bytes 12582916
  0.8 23.3 %copy-start.1 = (bf16[256,32,256]{2,1,0:T(8,128)(2,1)S(1)}, bf16[256,32,256]{2,1,0:T(8,128)(2,1)}, u32[]{:S(2)}) copy-start(bf16[256,32,256]{2,1,0:T(8,128)(2,1)} %v_ref.1) | copy-start | bytes 12582916
  0.8 23.2 %copy-start.4 = (s32[256]{0:T(256)S(1)}, s32[256]{0:T(256)}, u32[]{:S(2)}) copy-start(s32[256]{0:T(256)} %slot_ref.1) | copy-start | bytes 3076
  0.8 23.2 %copy-start.5 = (s32[256]{0:T(256)S(1)}, s32[256]{0:T(256)}, u32[]{:S(2)}) copy-start(s32[256]{0:T(256)} %dest_ref.1) | copy-start | bytes 3076
  24.0 19.3 %copy-start.2 = (bf16[8,3,256,256]{3,2,1,0:T(8,128)(2,1)S(1)}, bf16[8,3,256,256]{3,2,1,0:T(8,128)(2,1)}, u32[]{:S(2)}) copy-start(bf16[8,3,256,256]{3,2,1,0:T(8,128)(2,1)} %near_ref.1) | copy-start | bytes 9437188

commit v9 on v6

--- a/solution.py
+++ b/solution.py
@@ -6,8 +6,8 @@
 from jax.sharding import PartitionSpec as P
 
 VMEM = pl.BlockSpec(memory_space=pltpu.VMEM)
-CHUNKS = 4
-SMEM = pl.BlockSpec(memory_space=pltpu.SMEM)
+ANY = pl.BlockSpec(memory_space=pl.ANY)
+CHUNKS = 8
 
 
 def halves(x):
@@ -26,31 +26,54 @@
     clusters, nvec, leaf = src_ref.shape
     cap, peers = send_ref.shape
     me = lax.axis_index("clus")
+    rows = peers * nvec
+    repeat = lax.broadcasted_iota(jnp.int32, (rows, peers), 0) // nvec
+    repeat = (repeat == lax.broadcasted_iota(jnp.int32, (rows, peers), 1)).astype(jnp.bfloat16)
+
+    def columns(list_ref):
+        entries = list_ref[...].astype(jnp.float32).astype(jnp.bfloat16)
+        return lax.dot_general(
+            repeat, entries, (((1,), (1,)), ((), ())), preferred_element_type=jnp.float32
+        )
+
+    send = jnp.maximum(columns(send_ref), 0.0)
+    ret = columns(ret_ref)
+    row = lax.broadcasted_iota(jnp.int32, (rows, clusters * nvec), 0)
+    lane = lax.broadcasted_iota(jnp.int32, (rows, clusters * nvec), 1)
+    cluster = jnp.where(row % nvec == lane % nvec, lane // nvec, -2).astype(jnp.float32)
+    source = src_ref[...].reshape(clusters * nvec, leaf)
+    picked = []
+    for k in range(cap):
+        pick = jnp.where(send[:, k : k + 1] == cluster, 1.0, 0.0).astype(jnp.bfloat16)
+        picked.append(jnp.dot(pick, source, preferred_element_type=jnp.float32))
+    vector = lax.broadcasted_iota(jnp.int32, (rows, leaf // 2), 0) % nvec
+    places = jnp.broadcast_to(ret[:, :1], (rows, leaf // 2))
+    for k in range(1, cap):
+        places = jnp.where(vector >= k * nvec // cap, ret[:, k : k + 1], places)
     first = src_ref[0].astype(jnp.float32)
     last = src_ref[clusters - 1].astype(jnp.float32)
-
-    def step(p, carry):
-        rows = []
+    for p in range(peers):
+        at = slice(p * nvec, (p + 1) * nvec)
+        parts = []
         for k in range(cap):
-            rows += halves(src_ref[jnp.maximum(send_ref[k, p], 0)].astype(jnp.float32))
-        rows += halves(jnp.where(p > me, last, first))
-        rows.append(
-            jnp.concatenate(
-                [
-                    jnp.full((nvec // cap, leaf // 2), ret_ref[k, p].astype(jnp.float32))
-                    for k in range(cap)
-                ],
-                axis=0,
-            )
-        )
-        out_ref[p] = jnp.concatenate(rows, axis=0).astype(out_ref.dtype)
-        return carry
-
-    lax.fori_loop(0, peers, step, 0, unroll=min(peers, 16))
+            parts += halves(picked[k][at])
+        parts += halves(jnp.where(p > me, last, first))
+        parts.append(places[at])
+        out_ref[p] = jnp.concatenate(parts, axis=0).astype(out_ref.dtype)
 
 
 def joined(rows, nvec):
     return jnp.concatenate([rows[:nvec], rows[nvec:]], axis=1)
+
+
+def load_slots(slots_any, dests_any, slot_ref, dest_ref, sems):
+    copies = [
+        pltpu.make_async_copy(slots_any, slot_ref, sems.at[0]),
+        pltpu.make_async_copy(dests_any, dest_ref, sems.at[1]),
+    ]
+    for copy in copies:
+        copy.start()
+    return copies
 
 
 def widen_sources(x_ref, xf):
@@ -75,14 +98,19 @@
     return kept
 
 
-def far_kernel(slot_ref, dest_ref, x_ref, u_ref, v_ref, out_ref, xf, picked, wide):
+def far_kernel(
+    slots_any, dests_any, x_ref, u_ref, v_ref, out_ref, slot_ref, dest_ref, sems, xf, picked, wide
+):
     peers = x_ref.shape[0]
     slots, nvec, leaf = xf.shape
     blocks, rank, _ = u_ref.shape
     group = leaf // rank
     groups = blocks // group
     per = groups // CHUNKS
+    copies = load_slots(slots_any, dests_any, slot_ref, dest_ref, sems)
     widen_sources(x_ref, xf)
+    for copy in copies:
+        copy.wait()
     for g in range(groups):
         rows = [xf[slot_ref[g * group + i]] for i in range(group)]
         picked[g] = jnp.concatenate(rows, axis=0).astype(jnp.bfloat16)
@@ -110,11 +138,16 @@
     out_ref[...] = total.reshape(out_ref.shape).astype(out_ref.dtype)
 
 
-def far_many_kernel(slot_ref, dest_ref, x_ref, u_ref, v_ref, out_ref, xf, coef, acc):
+def far_many_kernel(
+    slots_any, dests_any, x_ref, u_ref, v_ref, out_ref, slot_ref, dest_ref, sems, xf, coef, acc
+):
     slots, nvec, leaf = xf.shape
     blocks, rank, _ = u_ref.shape
     group = leaf // rank
+    copies = load_slots(slots_any, dests_any, slot_ref, dest_ref, sems)
     widen_sources(x_ref, xf)
+    for copy in copies:
+        copy.wait()
     acc[...] = jnp.zeros_like(acc)
     owner = lax.broadcasted_iota(jnp.int32, (nvec, leaf), 1) // rank
 
@@ -198,7 +231,7 @@
     message = pl.pallas_call(
         pack_kernel,
         out_shape=jax.ShapeDtypeStruct((peers, rows, leaf // 2), jnp.bfloat16),
-        in_specs=[SMEM, SMEM, VMEM, VMEM],
+        in_specs=[VMEM] * 4,
         out_specs=VMEM,
         compiler_params=params,
         cost_estimate=cost(10**10, peers * rows * leaf),
@@ -219,9 +252,15 @@
     returns = pl.pallas_call(
         far_kernel if few else far_many_kernel,
         out_shape=jax.ShapeDtypeStruct((peers, cap * nvec, leaf), jnp.bfloat16),
-        in_specs=[SMEM, SMEM, VMEM, VMEM, VMEM],
-        out_specs=VMEM,
-        scratch_shapes=[pltpu.VMEM((slots, nvec, leaf), jnp.float32)] + scratch,
+        in_specs=[ANY, ANY, VMEM, VMEM, VMEM],
+        out_specs=VMEM,
+        scratch_shapes=[
+            pltpu.SMEM((blocks,), jnp.int32),
+            pltpu.SMEM((blocks,), jnp.int32),
+            pltpu.SemaphoreType.DMA((2,)),
+            pltpu.VMEM((slots, nvec, leaf), jnp.float32),
+        ]
+        + scratch,
         compiler_params=pltpu.CompilerParams(vmem_limit_bytes=16 * 2**20),
         cost_estimate=cost(4 * blocks * 8 * nvec * leaf * rank, 4 * blocks * rank * leaf),
         name="far",

time: 34.1 us -> 33.6 us (0.985)
  Pallas kernels: 5.56 us -> 5.06 us
where the time goes in v9:
time: 33.6 us; the launch traced here: 33.4 us
  blocking collectives  27.5 us (82%)
  Pallas kernels  5.06 us (15%)
  local copies, waits for them, and re-layouts  0.78 us (2%)
    all_to_all x1, blocking collectives, body(): lax.all_to_all(message, 'clus', split_axis=0, concat_axis=0, tiled=True)  16.9 us
    all_to_all x1, blocking collectives, body(): lax.all_to_all(returns, 'clus', split_axis=0, concat_axis=0, tiled=True)  10.6 us
    pallas_call x1, Pallas kernels, body(): pl.pallas_call(far_kernel if few else far_many_kernel, out_shape=jax.Shap...  3.44 us
    pallas_call x1, Pallas kernels, body(): pl.pallas_call(sum_kernel, out_shape=jax.ShapeDtypeStruct((clusters, nvec...  1.23 us
    unnamed x16, local copies, waits for them, and re-layouts  0.78 us

profile of v9, /device:TPU:0, one launch (start us, length us, event | category | flops | bytes accessed | tf_op | source)
XLA Modules:
  0.0 33.4 jit_solution(17340965580439189030)
XLA Ops:
  0.0 0.0 copy-start.3
  0.0 0.0 copy-start.7
  0.0 0.0 copy-start.6
  0.0 0.7 %copy-done.3 = bf16[8,8,256]{2,1,0:T(8,128)(2,1)S(1)} copy-done((bf16[8,8,256]{2,1,0:T(8,128)(2,1)S(1)}, bf16[8,8,256]{2,1,0:T(8,128)(2,1)}, u32[]{:S(2)}) %copy-start.3) | copy-done | bytes 32792
  0.8 0.0 copy-done.7
  0.8 0.0 copy-done.6
  0.8 0.0 copy-start
  0.8 0.0 copy-start.1
  0.8 0.0 copy-start.4
  0.8 0.0 copy-start.5
  0.8 0.4 %pack.1 = bf16[16,56,128]{2,1,0:T(8,128)(2,1)S(1)} custom-call(s32[2,16]{1,0:T(2,128)S(1)} %bitcast.6, s32[2,16]{1,0:T(2,128)S(1)} %bitcast.7, bf16[8,8,256]{2,1,0:T(8,128)(2,1)S(1)} %copy-done.3, f32[8,128]{1,0:T(8,128)S(1)} %pattern.1.pattern_ref), custom_call_target="tpu_custom_call" | custom-call | flops 10000000000 | bytes 229376 | tf_op jit(solution)/shard_map/pack/pallas_call | solution.py:231
  1.2 16.9 %all_to_all.10.x_ref = bf16[16,56,128]{2,1,0:T(8,128)(2,1)S(1)} all-to-all(bf16[16,56,128]{2,1,0:T(8,128)(2,1)S(1)} %pack.1), channel_id=1, replica_groups=mesh['groups'=2,'clus'=16] {'clus'}, dimensions={0} | all-to-all | bytes 458752 | tf_op jit(solution)/shard_map/all_to_all | solution.py:240
  18.1 0.0 copy-done
  18.1 0.0 copy-done.1
  18.1 0.0 copy-done.4
  18.1 0.0 copy-done.5
  18.1 0.0 copy-start.2
  18.2 3.4 %far.1 = bf16[16,16,256]{2,1,0:T(8,128)(2,1)S(1)} custom-call(s32[256]{0:T(256)S(1)} %copy-done.4, s32[256]{0:T(256)S(1)} %copy-done.5, bf16[16,56,128]{2,1,0:T(8,128)(2,1)S(1)} %all_to_all.10.x_ref, bf16[256,32,256]{2,1,0:T(8,128)(2,1)S(1)} %copy-done, bf16[256,32,256]{2,1,0:T(8,128)(2,1)S(1)} %copy-done.1), custom_call_target="tpu_custom_call" | custom-call | flops 536870912 | bytes 8388608 | tf_op jit(solution)/shard_map/far/pallas_call | solution.py:252
  21.6 10.6 %all_to_all.11.back_ref = bf16[16,16,256]{2,1,0:T(8,128)(2,1)S(1)} all-to-all(bf16[16,16,256]{2,1,0:T(8,128)(2,1)S(1)} %far.1), channel_id=1, replica_groups=mesh['groups'=2,'clus'=16] {'clus'}, dimensions={0} | all-to-all | bytes 262144 | tf_op jit(solution)/shard_map/all_to_all | solution.py:268
  32.2 0.0 copy-done.2
  32.2 1.2 %sum.1 = f32[8,8,256]{2,1,0:T(8,128)} custom-call(bf16[16,16,256]{2,1,0:T(8,128)(2,1)S(1)} %all_to_all.11.back_ref, bf16[8,8,256]{2,1,0:T(8,128)(2,1)S(1)} %copy-done.3, bf16[8,3,256,256]{3,2,1,0:T(8,128)(2,1)S(1)} %copy-done.2, bf16[16,56,128]{2,1,0:T(8,128)(2,1)S(1)} %all_to_all.10.x_ref, f32[8,128]{1,0:T(8,128)S(1)} %pattern.1.pattern_ref), custom_call_target="tpu_custom_call" | custom-call | flops 25165824 | bytes 3145728 | tf_op jit(solution)/shard_map/sum/pallas_call | solution.py:269
  (1 shorter events, 0.0 us)
Async XLA Ops:
  0.0 0.8 %copy-start.3 = (bf16[8,8,256]{2,1,0:T(8,128)(2,1)S(1)}, bf16[8,8,256]{2,1,0:T(8,128)(2,1)}, u32[]{:S(2)}) copy-start(bf16[8,8,256]{2,1,0:T(8,128)(2,1)} %src_ref.3) | copy-start | bytes 98308
  0.0 0.8 %copy-start.7 = (s32[1,16,2]{1,2,0:T(2,128)S(1)}, s32[1,16,2]{1,2,0:T(2,128)}, u32[]{:S(2)}) copy-start(s32[1,16,2]{1,2,0:T(2,128)} %param.14) | copy-start | bytes 388
  0.0 0.8 %copy-start.6 = (s32[1,16,2]{1,2,0:T(2,128)S(1)}, s32[1,16,2]{1,2,0:T(2,128)}, u32[]{:S(2)}) copy-start(s32[1,16,2]{1,2,0:T(2,128)} %param.12) | copy-start | bytes 388
  0.8 17.4 %copy-start = (bf16[256,32,256]{2,1,0:T(8,128)(2,1)S(1)}, bf16[256,32,256]{2,1,0:T(8,128)(2,1)}, u32[]{:S(2)}) copy-start(bf16[256,32,256]{2,1,0:T(8,128)(2,1)} %u_ref.1) | copy-start | bytes 12582916
  0.8 17.4 %copy-start.1 = (bf16[256,32,256]{2,1,0:T(8,128)(2,1)S(1)}, bf16[256,32,256]{2,1,0:T(8,128)(2,1)}, u32[]{:S(2)}) copy-start(bf16[256,32,256]{2,1,0:T(8,128)(2,1)} %v_ref.1) | copy-start | bytes 12582916
  0.8 17.4 %copy-start.4 = (s32[256]{0:T(256)S(1)}, s32[256]{0:T(256)}, u32[]{:S(2)}) copy-start(s32[256]{0:T(256)} %slots_any.1) | copy-start | bytes 3076
  0.8 17.3 %copy-start.5 = (s32[256]{0:T(256)S(1)}, s32[256]{0:T(256)}, u32[]{:S(2)}) copy-start(s32[256]{0:T(256)} %dests_any.1) | copy-start | bytes 3076
  18.1 14.0 %copy-start.2 = (bf16[8,3,256,256]{3,2,1,0:T(8,128)(2,1)S(1)}, bf16[8,3,256,256]{3,2,1,0:T(8,128)(2,1)}, u32[]{:S(2)}) copy-start(bf16[8,3,256,256]{3,2,1,0:T(8,128)(2,1)} %near_ref.1) | copy-start | bytes 9437188

commit v10 on v9

--- a/solution.py
+++ b/solution.py
@@ -76,6 +76,41 @@
     return copies
 
 
+def near_product(src_ref, near_ref, x_ref, near_out):
+    clusters, nvec, leaf = src_ref.shape
+    peers, rows, _ = x_ref.shape
+    me = lax.axis_index("clus")
+    edge = slice(rows - 3 * nvec, rows - nvec)
+    before = joined(x_ref[jnp.maximum(me - 1, 0)][edge].astype(jnp.float32), nvec)
+    after = joined(x_ref[jnp.minimum(me + 1, peers - 1)][edge].astype(jnp.float32), nvec)
+    before = jnp.where(me > 0, before, 0.0).astype(jnp.bfloat16)
+    after = jnp.where(me < peers - 1, after, 0.0).astype(jnp.bfloat16)
+    sources = [before] + [src_ref[s] for s in range(clusters)] + [after]
+    for s in range(clusters):
+        near_out[s * nvec : (s + 1) * nvec] = jnp.dot(
+            jnp.concatenate(sources[s : s + 3], axis=1),
+            near_ref[s].reshape(3 * leaf, leaf),
+            preferred_element_type=jnp.float32,
+        )
+
+
+def placement(x_ref, pattern_ref, place, place_out):
+    nvec, width = pattern_ref.shape
+    peers, rows, _ = x_ref.shape
+    cap = place.shape[0] // (peers * nvec)
+    cluster = pattern_ref[...]
+
+    def step(p, carry):
+        meta = x_ref[p, rows - nvec :, :].astype(jnp.float32)
+        for k in range(cap):
+            at = jnp.broadcast_to(meta[k * nvec // cap : k * nvec // cap + 1], (nvec, width))
+            place[pl.ds((p * cap + k) * nvec, nvec)] = jnp.where(at == cluster, 1.0, 0.0)
+        return carry
+
+    lax.fori_loop(0, peers, step, 0, unroll=min(peers, 16))
+    place_out[...] = place[...].T[: place_out.shape[0]].astype(jnp.bfloat16)
+
+
 def widen_sources(x_ref, xf):
     peers = x_ref.shape[0]
     slots, nvec, _ = xf.shape
@@ -99,7 +134,23 @@
 
 
 def far_kernel(
-    slots_any, dests_any, x_ref, u_ref, v_ref, out_ref, slot_ref, dest_ref, sems, xf, picked, wide
+    slots_any,
+    dests_any,
+    x_ref,
+    u_ref,
+    v_ref,
+    src_ref,
+    near_ref,
+    pattern_ref,
+    out_ref,
+    near_out,
+    place_out,
+    slot_ref,
+    dest_ref,
+    sems,
+    place,
+    xf,
+    picked, wide,
 ):
     peers = x_ref.shape[0]
     slots, nvec, leaf = xf.shape
@@ -109,6 +160,8 @@
     per = groups // CHUNKS
     copies = load_slots(slots_any, dests_any, slot_ref, dest_ref, sems)
     widen_sources(x_ref, xf)
+    near_product(src_ref, near_ref, x_ref, near_out)
+    placement(x_ref, pattern_ref, place, place_out)
     for copy in copies:
         copy.wait()
     for g in range(groups):
@@ -139,13 +192,31 @@
 
 
 def far_many_kernel(
-    slots_any, dests_any, x_ref, u_ref, v_ref, out_ref, slot_ref, dest_ref, sems, xf, coef, acc
+    slots_any,
+    dests_any,
+    x_ref,
+    u_ref,
+    v_ref,
+    src_ref,
+    near_ref,
+    pattern_ref,
+    out_ref,
+    near_out,
+    place_out,
+    slot_ref,
+    dest_ref,
+    sems,
+    place,
+    xf,
+    coef, acc,
 ):
     slots, nvec, leaf = xf.shape
     blocks, rank, _ = u_ref.shape
     group = leaf // rank
     copies = load_slots(slots_any, dests_any, slot_ref, dest_ref, sems)
     widen_sources(x_ref, xf)
+    near_product(src_ref, near_ref, x_ref, near_out)
+    placement(x_ref, pattern_ref, place, place_out)
     for copy in copies:
         copy.wait()
     acc[...] = jnp.zeros_like(acc)
@@ -174,39 +245,11 @@
     out_ref[...] = acc[...].reshape(out_ref.shape).astype(out_ref.dtype)
 
 
-def sum_kernel(back_ref, src_ref, near_ref, x_ref, pattern_ref, out_ref, place):
-    clusters, nvec, leaf = src_ref.shape
-    peers, back_rows, _ = back_ref.shape
-    cap = back_rows // nvec
-    width = leaf // 2
-    cluster = pattern_ref[...]
-
-    def step(p, carry):
-        meta = x_ref[p, 2 * (cap + 1) * nvec :, :].astype(jnp.float32)
-        for k in range(cap):
-            at = jnp.broadcast_to(meta[k * nvec // cap : k * nvec // cap + 1], (nvec, width))
-            place[pl.ds((p * cap + k) * nvec, nvec)] = jnp.where(at == cluster, 1.0, 0.0)
-        return carry
-
-    lax.fori_loop(0, peers, step, 0, unroll=min(peers, 16))
-    spread = place[...].T[: clusters * nvec].astype(jnp.bfloat16)
-    terms = back_ref[...].reshape(peers * back_rows, leaf)
-    far_part = jnp.dot(spread, terms, preferred_element_type=jnp.float32)
-
-    me = lax.axis_index("clus")
-    edge = slice(2 * cap * nvec, 2 * (cap + 1) * nvec)
-    before = joined(x_ref[jnp.maximum(me - 1, 0)][edge].astype(jnp.float32), nvec)
-    after = joined(x_ref[jnp.minimum(me + 1, peers - 1)][edge].astype(jnp.float32), nvec)
-    before = jnp.where(me > 0, before, 0.0).astype(jnp.bfloat16)
-    after = jnp.where(me < peers - 1, after, 0.0).astype(jnp.bfloat16)
-    rows = [before] + [src_ref[s] for s in range(clusters)] + [after]
-    for s in range(clusters):
-        total = jnp.dot(
-            jnp.concatenate(rows[s : s + 3], axis=1),
-            near_ref[s].reshape(3 * leaf, leaf),
-            preferred_element_type=jnp.float32,
-        )
-        out_ref[s] = far_part[s * nvec : (s + 1) * nvec] + total
+def sum_kernel(back_ref, near_ref, place_ref, out_ref):
+    peers, rows, leaf = back_ref.shape
+    terms = back_ref[...].reshape(peers * rows, leaf)
+    total = near_ref[...] + jnp.dot(place_ref[...], terms, preferred_element_type=jnp.float32)
+    out_ref[...] = total.reshape(out_ref.shape)
 
 
 def cost(flops, moved):
@@ -249,33 +292,37 @@
             pltpu.VMEM((blocks * rank // leaf, nvec, leaf), jnp.float32),
             pltpu.VMEM((slots, nvec, leaf), jnp.float32),
         ]
-    returns = pl.pallas_call(
+    returns, near_part, place = pl.pallas_call(
         far_kernel if few else far_many_kernel,
-        out_shape=jax.ShapeDtypeStruct((peers, cap * nvec, leaf), jnp.bfloat16),
-        in_specs=[ANY, ANY, VMEM, VMEM, VMEM],
-        out_specs=VMEM,
+        out_shape=(
+            jax.ShapeDtypeStruct((peers, cap * nvec, leaf), jnp.bfloat16),
+            jax.ShapeDtypeStruct((clusters * nvec, leaf), jnp.float32),
+            jax.ShapeDtypeStruct((clusters * nvec, slots * nvec), jnp.bfloat16),
+        ),
+        in_specs=[ANY, ANY] + [VMEM] * 6,
+        out_specs=(VMEM, VMEM, VMEM),
         scratch_shapes=[
             pltpu.SMEM((blocks,), jnp.int32),
             pltpu.SMEM((blocks,), jnp.int32),
             pltpu.SemaphoreType.DMA((2,)),
+            pltpu.VMEM((slots * nvec, leaf // 2), jnp.float32),
             pltpu.VMEM((slots, nvec, leaf), jnp.float32),
         ]
         + scratch,
         compiler_params=pltpu.CompilerParams(vmem_limit_bytes=16 * 2**20),
         cost_estimate=cost(4 * blocks * 8 * nvec * leaf * rank, 4 * blocks * rank * leaf),
         name="far",
-    )(far_slot, ret_slot, incoming, far_u, far_v)
+    )(far_slot, ret_slot, incoming, far_u, far_v, sources, near_blocks, pattern)
     back = lax.all_to_all(returns, "clus", split_axis=0, concat_axis=0, tiled=True)
     return pl.pallas_call(
         sum_kernel,
         out_shape=jax.ShapeDtypeStruct((clusters, nvec, leaf), jnp.float32),
-        in_specs=[VMEM] * 5,
+        in_specs=[VMEM] * 3,
         out_specs=VMEM,
-        scratch_shapes=[pltpu.VMEM((slots * nvec, leaf // 2), jnp.float32)],
         compiler_params=params,
-        cost_estimate=cost(2 * 3 * clusters * nvec * leaf * leaf, 6 * clusters * leaf * leaf),
+        cost_estimate=cost(2 * clusters * nvec * slots * nvec * leaf, slots * nvec * leaf * 2),
         name="sum",
-    )(back, sources, near_blocks, incoming, pattern)
+    )(back, near_part, place)
 
 
 def solution(mesh):

time: 33.6 us -> 33.6 us (level)
    pallas_call x1, Pallas kernels: 1.23 us -> 0.78 us  [body(): pl.pallas_call(sum_kernel, out_shape=jax.ShapeDtypeStruct((clusters, nvec...]
    pallas_call x1, Pallas kernels: 3.44 us -> 3.82 us  [body(): pl.pallas_call(far_kernel if few else far_many_kernel, out_shape=(jax.Sha...]
where the time goes in v10:
time: 33.6 us; the launch traced here: 33.3 us
  blocking collectives  27.5 us (82%)
  Pallas kernels  4.99 us (15%)
  local copies, waits for them, and re-layouts  0.78 us (2%)
    all_to_all x1, blocking collectives, body(): lax.all_to_all(message, 'clus', split_axis=0, concat_axis=0, tiled=True)  16.9 us
    all_to_all x1, blocking collectives, body(): lax.all_to_all(returns, 'clus', split_axis=0, concat_axis=0, tiled=True)  10.6 us
    pallas_call x1, Pallas kernels, body(): pl.pallas_call(far_kernel if few else far_many_kernel, out_shape=(jax.Sha...  3.82 us
    pallas_call x1, Pallas kernels, body(): pl.pallas_call(sum_kernel, out_shape=jax.ShapeDtypeStruct((clusters, nvec...  0.78 us
    unnamed x16, local copies, waits for them, and re-layouts  0.78 us

profile of v10, /device:TPU:0, one launch (start us, length us, event | category | flops | bytes accessed | tf_op | source)
XLA Modules:
  0.0 33.3 jit_solution(4273846760114094440)
XLA Ops:
  0.0 0.0 copy-start.3
  0.0 0.0 copy-start.7
  0.0 0.0 copy-start.6
  0.0 0.7 %copy-done.3 = bf16[8,8,256]{2,1,0:T(8,128)(2,1)S(1)} copy-done((bf16[8,8,256]{2,1,0:T(8,128)(2,1)S(1)}, bf16[8,8,256]{2,1,0:T(8,128)(2,1)}, u32[]{:S(2)}) %copy-start.3) | copy-done | bytes 32792
  0.8 0.0 copy-done.7
  0.8 0.0 copy-done.6
  0.8 0.0 copy-start
  0.8 0.0 copy-start.1
  0.8 0.0 copy-start.2
  0.8 0.0 copy-start.4
  0.8 0.0 copy-start.5
  0.8 0.4 %pack.1 = bf16[16,56,128]{2,1,0:T(8,128)(2,1)S(1)} custom-call(s32[2,16]{1,0:T(2,128)S(1)} %bitcast.6, s32[2,16]{1,0:T(2,128)S(1)} %bitcast.7, bf16[8,8,256]{2,1,0:T(8,128)(2,1)S(1)} %copy-done.3, f32[8,128]{1,0:T(8,128)S(1)} %pattern.1.pattern_ref), custom_call_target="tpu_custom_call" | custom-call | flops 10000000000 | bytes 229376 | tf_op jit(solution)/shard_map/pack/pallas_call | solution.py:274
  1.2 16.9 %all_to_all.10.x_ref = bf16[16,56,128]{2,1,0:T(8,128)(2,1)S(1)} all-to-all(bf16[16,56,128]{2,1,0:T(8,128)(2,1)S(1)} %pack.1), channel_id=1, replica_groups=mesh['groups'=2,'clus'=16] {'clus'}, dimensions={0} | all-to-all | bytes 458752 | tf_op jit(solution)/shard_map/all_to_all | solution.py:283
  18.1 0.0 copy-done
  18.1 0.0 copy-done.1
  18.1 0.0 copy-done.2
  18.1 0.0 copy-done.4
  18.1 0.0 copy-done.5
  18.2 3.8 %far.1 = (bf16[16,16,256]{2,1,0:T(8,128)(2,1)S(1)}, f32[64,256]{1,0:T(8,128)S(1)}, bf16[64,256]{1,0:T(8,128)(2,1)S(1)}) custom-call(s32[256]{0:T(256)S(1)} %copy-done.4, s32[256]{0:T(256)S(1)} %copy-done.5, bf16[16,56,128]{2,1,0:T(8,128)(2,1)S(1)} %all_to_all.10.x_ref, bf16[256,32,256]{2,1,0:T(8,128)(2,1)S(1)} %copy-done, ...), custom_call_target="tpu_custom_call" | custom-call | flops 536870912 | bytes 8388608 | tf_op jit(solution)/shard_map/far/pallas_call | solution.py:295
  22.0 10.6 %all_to_all.11.back_ref = bf16[16,16,256]{2,1,0:T(8,128)(2,1)S(1)} all-to-all(bf16[16,16,256]{2,1,0:T(8,128)(2,1)S(1)} %get-tuple-element.8), channel_id=1, replica_groups=mesh['groups'=2,'clus'=16] {'clus'}, dimensions={0} | all-to-all | bytes 262144 | tf_op jit(solution)/shard_map/all_to_all | solution.py:316
  32.6 0.8 %sum.1 = f32[8,8,256]{2,1,0:T(8,128)} custom-call(bf16[16,16,256]{2,1,0:T(8,128)(2,1)S(1)} %all_to_all.11.back_ref, f32[64,256]{1,0:T(8,128)S(1)} %get-tuple-element.9.near_ref, bf16[64,256]{1,0:T(8,128)(2,1)S(1)} %get-tuple-element.10.place_ref), custom_call_target="tpu_custom_call" | custom-call | flops 8388608 | bytes 131072 | tf_op jit(solution)/shard_map/sum/pallas_call | solution.py:317
  (1 shorter events, 0.0 us)
Async XLA Ops:
  0.0 0.8 %copy-start.3 = (bf16[8,8,256]{2,1,0:T(8,128)(2,1)S(1)}, bf16[8,8,256]{2,1,0:T(8,128)(2,1)}, u32[]{:S(2)}) copy-start(bf16[8,8,256]{2,1,0:T(8,128)(2,1)} %src_ref.3) | copy-start | bytes 98308
  0.0 0.8 %copy-start.7 = (s32[1,16,2]{1,2,0:T(2,128)S(1)}, s32[1,16,2]{1,2,0:T(2,128)}, u32[]{:S(2)}) copy-start(s32[1,16,2]{1,2,0:T(2,128)} %param.14) | copy-start | bytes 388
  0.0 0.8 %copy-start.6 = (s32[1,16,2]{1,2,0:T(2,128)S(1)}, s32[1,16,2]{1,2,0:T(2,128)}, u32[]{:S(2)}) copy-start(s32[1,16,2]{1,2,0:T(2,128)} %param.12) | copy-start | bytes 388
  0.8 17.4 %copy-start = (bf16[256,32,256]{2,1,0:T(8,128)(2,1)S(1)}, bf16[256,32,256]{2,1,0:T(8,128)(2,1)}, u32[]{:S(2)}) copy-start(bf16[256,32,256]{2,1,0:T(8,128)(2,1)} %u_ref.1) | copy-start | bytes 12582916
  0.8 17.4 %copy-start.1 = (bf16[256,32,256]{2,1,0:T(8,128)(2,1)S(1)}, bf16[256,32,256]{2,1,0:T(8,128)(2,1)}, u32[]{:S(2)}) copy-start(bf16[256,32,256]{2,1,0:T(8,128)(2,1)} %v_ref.1) | copy-start | bytes 12582916
  0.8 17.4 %copy-start.2 = (bf16[8,3,256,256]{3,2,1,0:T(8,128)(2,1)S(1)}, bf16[8,3,256,256]{3,2,1,0:T(8,128)(2,1)}, u32[]{:S(2)}) copy-start(bf16[8,3,256,256]{3,2,1,0:T(8,128)(2,1)} %near_ref.1) | copy-start | bytes 9437188
  0.8 17.4 %copy-start.4 = (s32[256]{0:T(256)S(1)}, s32[256]{0:T(256)}, u32[]{:S(2)}) copy-start(s32[256]{0:T(256)} %slots_any.1) | copy-start | bytes 3076
  0.8 17.4 %copy-start.5 = (s32[256]{0:T(256)S(1)}, s32[256]{0:T(256)}, u32[]{:S(2)}) copy-start(s32[256]{0:T(256)} %dests_any.1) | copy-start | bytes 3076

commit v11 on v10

--- a/solution.py
+++ b/solution.py
@@ -27,17 +27,21 @@
     cap, peers = send_ref.shape
     me = lax.axis_index("clus")
     rows = peers * nvec
-    repeat = lax.broadcasted_iota(jnp.int32, (rows, peers), 0) // nvec
-    repeat = (repeat == lax.broadcasted_iota(jnp.int32, (rows, peers), 1)).astype(jnp.bfloat16)
-
-    def columns(list_ref):
+    peer = lax.broadcasted_iota(jnp.int32, (rows, peers), 0) // nvec
+    kind = lax.broadcasted_iota(jnp.int32, (rows, peers), 0) % nvec // cap
+    column = lax.broadcasted_iota(jnp.int32, (rows, peers), 1)
+
+    def entries_at(list_ref, which):
         entries = list_ref[...].astype(jnp.float32).astype(jnp.bfloat16)
         return lax.dot_general(
-            repeat, entries, (((1,), (1,)), ((), ())), preferred_element_type=jnp.float32
+            jnp.where(which == column, 1.0, 0.0).astype(jnp.bfloat16),
+            entries,
+            (((1,), (1,)), ((), ())),
+            preferred_element_type=jnp.float32,
         )
 
-    send = jnp.maximum(columns(send_ref), 0.0)
-    ret = columns(ret_ref)
+    send = jnp.maximum(entries_at(send_ref, peer), 0.0)
+    ret = entries_at(ret_ref, jnp.where(kind == 1, me - 1, jnp.where(kind == 2, me + 1, peer)))
     row = lax.broadcasted_iota(jnp.int32, (rows, clusters * nvec), 0)
     lane = lax.broadcasted_iota(jnp.int32, (rows, clusters * nvec), 1)
     cluster = jnp.where(row % nvec == lane % nvec, lane // nvec, -2).astype(jnp.float32)
@@ -49,7 +53,7 @@
     vector = lax.broadcasted_iota(jnp.int32, (rows, leaf // 2), 0) % nvec
     places = jnp.broadcast_to(ret[:, :1], (rows, leaf // 2))
     for k in range(1, cap):
-        places = jnp.where(vector >= k * nvec // cap, ret[:, k : k + 1], places)
+        places = jnp.where(vector % cap == k, ret[:, k : k + 1], places)
     first = src_ref[0].astype(jnp.float32)
     last = src_ref[clusters - 1].astype(jnp.float32)
     for p in range(peers):
@@ -57,8 +61,8 @@
         parts = []
         for k in range(cap):
             parts += halves(picked[k][at])
-        parts += halves(jnp.where(p > me, last, first))
-        parts.append(places[at])
+        edge = halves(jnp.where(p > me, last, first))[0]
+        parts.append(jnp.where(jnp.abs(p - me) == 1, edge, places[at]))
         out_ref[p] = jnp.concatenate(parts, axis=0).astype(out_ref.dtype)
 
 
@@ -80,11 +84,14 @@
     clusters, nvec, leaf = src_ref.shape
     peers, rows, _ = x_ref.shape
     me = lax.axis_index("clus")
-    edge = slice(rows - 3 * nvec, rows - nvec)
-    before = joined(x_ref[jnp.maximum(me - 1, 0)][edge].astype(jnp.float32), nvec)
-    after = joined(x_ref[jnp.minimum(me + 1, peers - 1)][edge].astype(jnp.float32), nvec)
-    before = jnp.where(me > 0, before, 0.0).astype(jnp.bfloat16)
-    after = jnp.where(me < peers - 1, after, 0.0).astype(jnp.bfloat16)
+    before = x_ref[jnp.maximum(me - 1, 0)][rows - nvec :].astype(jnp.float32)
+    after = x_ref[jnp.minimum(me + 1, peers - 1)][rows - nvec :].astype(jnp.float32)
+    before = jnp.where(me > 0, before, 0.0)
+    after = jnp.where(me < peers - 1, after, 0.0)
+    before, after = [
+        jnp.concatenate([x, jnp.zeros_like(x)], axis=1).astype(jnp.bfloat16)
+        for x in (before, after)
+    ]
     sources = [before] + [src_ref[s] for s in range(clusters)] + [after]
     for s in range(clusters):
         near_out[s * nvec : (s + 1) * nvec] = jnp.dot(
@@ -99,11 +106,13 @@
     peers, rows, _ = x_ref.shape
     cap = place.shape[0] // (peers * nvec)
     cluster = pattern_ref[...]
+    me = lax.axis_index("clus")
 
     def step(p, carry):
-        meta = x_ref[p, rows - nvec :, :].astype(jnp.float32)
+        tile = x_ref[p, rows - nvec :, :].astype(jnp.float32)
+        tile = jnp.where(jnp.abs(p - me) == 1, -1.0, tile)
         for k in range(cap):
-            at = jnp.broadcast_to(meta[k * nvec // cap : k * nvec // cap + 1], (nvec, width))
+            at = jnp.broadcast_to(tile[k : k + 1], (nvec, width))
             place[pl.ds((p * cap + k) * nvec, nvec)] = jnp.where(at == cluster, 1.0, 0.0)
         return carry
 
@@ -131,6 +140,25 @@
     for i in range(1, group):
         kept = jnp.where(owner == i, full[i * nvec : (i + 1) * nvec], kept)
     return kept
+
+
+def put_returns(total, x_ref, src_ref, out_ref):
+    peers, rows, width = x_ref.shape
+    clusters, nvec, _ = src_ref.shape
+    each = total.shape[0] // peers
+    cap = each // nvec
+    me = lax.axis_index("clus")
+    first = halves(src_ref[0].astype(jnp.float32))[1]
+    last = halves(src_ref[clusters - 1].astype(jnp.float32))[1]
+    sub = lax.broadcasted_iota(jnp.int32, (nvec, width), 0)
+    for p in range(peers):
+        before = x_ref[max(p - 1, 0), rows - nvec :, :].astype(jnp.float32)
+        after = x_ref[min(p + 1, peers - 1), rows - nvec :, :].astype(jnp.float32)
+        handed = jnp.where(sub // cap == 2, before, after)
+        edge = jnp.where(p > me, last, first)
+        parts = halves(total[p * each : (p + 1) * each])
+        parts.append(jnp.where(jnp.abs(p - me) == 1, edge, handed))
+        out_ref[p] = jnp.concatenate(parts, axis=0).astype(out_ref.dtype)
 
 
 def far_kernel(
@@ -188,7 +216,7 @@
             wide[:, c * per * leaf : (c + 1) * per * leaf], v, preferred_element_type=jnp.float32
         )
         total = part if total is None else total + part
-    out_ref[...] = total.reshape(out_ref.shape).astype(out_ref.dtype)
+    put_returns(total, x_ref, src_ref, out_ref)
 
 
 def far_many_kernel(
@@ -242,14 +270,58 @@
 
     lax.fori_loop(0, blocks // group, forward, 0, unroll=4)
     lax.fori_loop(0, blocks // group, backward, 0, unroll=4)
-    out_ref[...] = acc[...].reshape(out_ref.shape).astype(out_ref.dtype)
-
-
-def sum_kernel(back_ref, near_ref, place_ref, out_ref):
-    peers, rows, leaf = back_ref.shape
-    terms = back_ref[...].reshape(peers * rows, leaf)
-    total = near_ref[...] + jnp.dot(place_ref[...], terms, preferred_element_type=jnp.float32)
-    out_ref[...] = total.reshape(out_ref.shape)
+    put_returns(acc[...].reshape(slots * nvec, leaf), x_ref, src_ref, out_ref)
+
+
+def sum_kernel(back_ref, near_out_ref, place_ref, near_ref, out_ref):
+    peers, rows, width = back_ref.shape
+    clusters, nvec, leaf = out_ref.shape
+    each = (rows - nvec) // 2
+    cap = each // nvec
+    me = lax.axis_index("clus")
+    terms = jnp.concatenate(
+        [back_ref[:, i * each : (i + 1) * each, :].reshape(peers * each, width) for i in range(2)],
+        axis=1,
+    )
+    total = near_out_ref[...] + jnp.dot(
+        place_ref[...], terms, preferred_element_type=jnp.float32
+    )
+
+    relay = jnp.where(me + 3 < peers, me + 3, me - 3)
+    tile = back_ref[relay][rows - nvec :].astype(jnp.float32)
+    before = back_ref[jnp.maximum(me - 1, 0)].astype(jnp.float32)
+    after = back_ref[jnp.minimum(me + 1, peers - 1)].astype(jnp.float32)
+    row = lax.broadcasted_iota(jnp.int32, (clusters * nvec, width), 0)
+    lane = lax.broadcasted_iota(jnp.int32, (clusters * nvec, width), 1)
+    named = jnp.full((1, width), -1.0, jnp.float32)
+    for i in range(2 * cap):
+        k, alive = (i + 2 * cap, me > 0) if i < cap else (i, me < peers - 1)
+        entry = jnp.where(alive, tile[k : k + 1], -1.0)
+        named = jnp.where(lane[:1] // nvec == i, entry, named)
+    match = (named == (row // nvec).astype(jnp.float32)) & (lane % nvec == row % nvec)
+    match = jnp.where(match, 1.0, 0.0)[:, : 2 * each].astype(jnp.bfloat16)
+    sides = jnp.concatenate(
+        [
+            jnp.concatenate([side[:each], side[each : 2 * each]], axis=1)
+            for side in (before, after)
+        ],
+        axis=0,
+    ).astype(jnp.bfloat16)
+    total += jnp.dot(match, sides, preferred_element_type=jnp.float32)
+
+    edges = []
+    for side, alive, at in ((before, me > 0, (0, 0)), (after, me < peers - 1, (clusters - 1, 2))):
+        edge = jnp.where(alive, side[2 * each :], 0.0).astype(jnp.bfloat16)
+        edges.append(
+            jnp.dot(edge, near_ref[at[0], at[1], width:, :], preferred_element_type=jnp.float32)
+        )
+    for s in range(clusters):
+        part = total[s * nvec : (s + 1) * nvec]
+        if s == 0:
+            part += edges[0]
+        if s == clusters - 1:
+            part += edges[1]
+        out_ref[s] = part
 
 
 def cost(flops, moved):
@@ -261,7 +333,7 @@
     _, peers, cap = send_list.shape
     blocks, rank, _ = far_u.shape
     slots = peers * cap
-    rows = 2 * (cap + 1) * nvec + nvec
+    rows = 2 * cap * nvec + nvec
     params = pltpu.CompilerParams(vmem_limit_bytes=8 * 2**20)
     pattern = pl.pallas_call(
         pattern_kernel,
@@ -295,7 +367,7 @@
     returns, near_part, place = pl.pallas_call(
         far_kernel if few else far_many_kernel,
         out_shape=(
-            jax.ShapeDtypeStruct((peers, cap * nvec, leaf), jnp.bfloat16),
+            jax.ShapeDtypeStruct((peers, rows, leaf // 2), jnp.bfloat16),
             jax.ShapeDtypeStruct((clusters * nvec, leaf), jnp.float32),
             jax.ShapeDtypeStruct((clusters * nvec, slots * nvec), jnp.bfloat16),
         ),
@@ -317,12 +389,12 @@
     return pl.pallas_call(
         sum_kernel,
         out_shape=jax.ShapeDtypeStruct((clusters, nvec, leaf), jnp.float32),
-        in_specs=[VMEM] * 3,
+        in_specs=[VMEM] * 4,
         out_specs=VMEM,
         compiler_params=params,
         cost_estimate=cost(2 * clusters * nvec * slots * nvec * leaf, slots * nvec * leaf * 2),
         name="sum",
-    )(back, near_part, place)
+    )(back, near_part, place, near_blocks)
 
 
 def solution(mesh):

time: 33.6 us -> 33 us (0.982)
  blocking collectives: 27.5 us -> 26.9 us
    all_to_all x1, blocking collectives: 16.9 us -> 15.9 us  [body(): lax.all_to_all(message, 'clus', split_axis=0, concat_axis=0, tiled=True)]
    all_to_all x1, blocking collectives: 10.6 us -> 11.1 us  [body(): lax.all_to_all(returns, 'clus', split_axis=0, concat_axis=0, tiled=True)]
where the time goes in v11:
time: 33 us; the launch traced here: 32.8 us
  blocking collectives  26.9 us (82%)
  Pallas kernels  5.02 us (15%)
  local copies, waits for them, and re-layouts  0.78 us (2%)
    all_to_all x1, blocking collectives, body(): lax.all_to_all(message, 'clus', split_axis=0, concat_axis=0, tiled=True)  15.9 us
    all_to_all x1, blocking collectives, body(): lax.all_to_all(returns, 'clus', split_axis=0, concat_axis=0, tiled=True)  11.1 us
    pallas_call x1, Pallas kernels, body(): pl.pallas_call(far_kernel if few else far_many_kernel, out_shape=(jax.Sha...  3.82 us
    pallas_call x1, Pallas kernels, body(): pl.pallas_call(sum_kernel, out_shape=jax.ShapeDtypeStruct((clusters, nvec...  0.82 us
    unnamed x16, local copies, waits for them, and re-layouts  0.78 us

profile of v11, /device:TPU:0, one launch (start us, length us, event | category | flops | bytes accessed | tf_op | source)
XLA Modules:
  0.0 32.8 jit_solution(15898795339914350384)
XLA Ops:
  0.0 0.0 copy-start.3
  0.0 0.0 copy-start.7
  0.0 0.0 copy-start.6
  0.0 0.7 %copy-done.3 = bf16[8,8,256]{2,1,0:T(8,128)(2,1)S(1)} copy-done((bf16[8,8,256]{2,1,0:T(8,128)(2,1)S(1)}, bf16[8,8,256]{2,1,0:T(8,128)(2,1)}, u32[]{:S(2)}) %copy-start.3) | copy-done | bytes 32792
  0.8 0.0 copy-done.7
  0.8 0.0 copy-done.6
  0.8 0.0 copy-start
  0.8 0.0 copy-start.1
  0.8 0.0 copy-start.2
  0.8 0.0 copy-start.4
  0.8 0.0 copy-start.5
  0.8 0.4 %pack.1 = bf16[16,40,128]{2,1,0:T(8,128)(2,1)S(1)} custom-call(s32[2,16]{1,0:T(2,128)S(1)} %bitcast.6, s32[2,16]{1,0:T(2,128)S(1)} %bitcast.7, bf16[8,8,256]{2,1,0:T(8,128)(2,1)S(1)} %copy-done.3, f32[8,128]{1,0:T(8,128)S(1)} %pattern.1.pattern_ref), custom_call_target="tpu_custom_call" | custom-call | flops 10000000000 | bytes 163840 | tf_op jit(solution)/shard_map/pack/pallas_call | solution.py:346
  1.2 15.9 %all_to_all.10.x_ref = bf16[16,40,128]{2,1,0:T(8,128)(2,1)S(1)} all-to-all(bf16[16,40,128]{2,1,0:T(8,128)(2,1)S(1)} %pack.1), channel_id=1, replica_groups=mesh['groups'=2,'clus'=16] {'clus'}, dimensions={0} | all-to-all | bytes 327680 | tf_op jit(solution)/shard_map/all_to_all | solution.py:355
  17.1 0.0 copy-done
  17.1 0.0 copy-done.1
  17.1 0.0 copy-done.2
  17.1 0.0 copy-done.4
  17.1 0.0 copy-done.5
  17.1 3.8 %far.1 = (bf16[16,40,128]{2,1,0:T(8,128)(2,1)S(1)}, f32[64,256]{1,0:T(8,128)S(1)}, bf16[64,256]{1,0:T(8,128)(2,1)S(1)}) custom-call(s32[256]{0:T(256)S(1)} %copy-done.4, s32[256]{0:T(256)S(1)} %copy-done.5, bf16[16,40,128]{2,1,0:T(8,128)(2,1)S(1)} %all_to_all.10.x_ref, bf16[256,32,256]{2,1,0:T(8,128)(2,1)S(1)} %copy-done.1, ...), custom_call_target="tpu_custom_call" | custom-call | flops 536870912 | bytes 8388608 | tf_op jit(solution)/shard_map/far/pallas_call | solution.py:367
  20.9 11.1 %all_to_all.11.back_ref = bf16[16,40,128]{2,1,0:T(8,128)(2,1)S(1)} all-to-all(bf16[16,40,128]{2,1,0:T(8,128)(2,1)S(1)} %get-tuple-element.8), channel_id=1, replica_groups=mesh['groups'=2,'clus'=16] {'clus'}, dimensions={0} | all-to-all | bytes 327680 | tf_op jit(solution)/shard_map/all_to_all | solution.py:388
  32.0 0.8 %sum.1 = f32[8,8,256]{2,1,0:T(8,128)} custom-call(bf16[16,40,128]{2,1,0:T(8,128)(2,1)S(1)} %all_to_all.11.back_ref, f32[64,256]{1,0:T(8,128)S(1)} %get-tuple-element.9.near_out_ref, bf16[64,256]{1,0:T(8,128)(2,1)S(1)} %get-tuple-element.10.place_ref, bf16[8,3,256,256]{3,2,1,0:T(8,128)(2,1)S(1)} %copy-done), custom_call_target="tpu_custom_call" | custom-call | flops 8388608 | bytes 131072 | tf_op jit(solution)/shard_map/sum/pallas_call | solution.py:389
  (1 shorter events, 0.0 us)
Async XLA Ops:
  0.0 0.8 %copy-start.3 = (bf16[8,8,256]{2,1,0:T(8,128)(2,1)S(1)}, bf16[8,8,256]{2,1,0:T(8,128)(2,1)}, u32[]{:S(2)}) copy-start(bf16[8,8,256]{2,1,0:T(8,128)(2,1)} %src_ref.3) | copy-start | bytes 98308
  0.0 0.8 %copy-start.7 = (s32[1,16,2]{1,2,0:T(2,128)S(1)}, s32[1,16,2]{1,2,0:T(2,128)}, u32[]{:S(2)}) copy-start(s32[1,16,2]{1,2,0:T(2,128)} %param.14) | copy-start | bytes 388
  0.0 0.8 %copy-start.6 = (s32[1,16,2]{1,2,0:T(2,128)S(1)}, s32[1,16,2]{1,2,0:T(2,128)}, u32[]{:S(2)}) copy-start(s32[1,16,2]{1,2,0:T(2,128)} %param.12) | copy-start | bytes 388
  0.8 16.3 %copy-start = (bf16[8,3,256,256]{3,2,1,0:T(8,128)(2,1)S(1)}, bf16[8,3,256,256]{3,2,1,0:T(8,128)(2,1)}, u32[]{:S(2)}) copy-start(bf16[8,3,256,256]{3,2,1,0:T(8,128)(2,1)} %near_ref.3) | copy-start | bytes 9437188
  0.8 16.3 %copy-start.1 = (bf16[256,32,256]{2,1,0:T(8,128)(2,1)S(1)}, bf16[256,32,256]{2,1,0:T(8,128)(2,1)}, u32[]{:S(2)}) copy-start(bf16[256,32,256]{2,1,0:T(8,128)(2,1)} %u_ref.1) | copy-start | bytes 12582916
  0.8 16.3 %copy-start.2 = (bf16[256,32,256]{2,1,0:T(8,128)(2,1)S(1)}, bf16[256,32,256]{2,1,0:T(8,128)(2,1)}, u32[]{:S(2)}) copy-start(bf16[256,32,256]{2,1,0:T(8,128)(2,1)} %v_ref.1) | copy-start | bytes 12582916
  0.8 16.3 %copy-start.4 = (s32[256]{0:T(256)S(1)}, s32[256]{0:T(256)}, u32[]{:S(2)}) copy-start(s32[256]{0:T(256)} %slots_any.1) | copy-start | bytes 3076
  0.8 16.3 %copy-start.5 = (s32[256]{0:T(256)S(1)}, s32[256]{0:T(256)}, u32[]{:S(2)}) copy-start(s32[256]{0:T(256)} %dests_any.1) | copy-start | bytes 3076

commit v12 on v11

--- a/solution.py
+++ b/solution.py
@@ -7,7 +7,7 @@
 
 VMEM = pl.BlockSpec(memory_space=pltpu.VMEM)
 ANY = pl.BlockSpec(memory_space=pl.ANY)
-CHUNKS = 8
+CHUNKS = 4
 
 
 def halves(x):
@@ -188,10 +188,10 @@
     per = groups // CHUNKS
     copies = load_slots(slots_any, dests_any, slot_ref, dest_ref, sems)
     widen_sources(x_ref, xf)
-    near_product(src_ref, near_ref, x_ref, near_out)
     placement(x_ref, pattern_ref, place, place_out)
     for copy in copies:
         copy.wait()
+    near_product(src_ref, near_ref, x_ref, near_out)
     for g in range(groups):
         rows = [xf[slot_ref[g * group + i]] for i in range(group)]
         picked[g] = jnp.concatenate(rows, axis=0).astype(jnp.bfloat16)
@@ -243,10 +243,10 @@
     group = leaf // rank
     copies = load_slots(slots_any, dests_any, slot_ref, dest_ref, sems)
     widen_sources(x_ref, xf)
-    near_product(src_ref, near_ref, x_ref, near_out)
     placement(x_ref, pattern_ref, place, place_out)
     for copy in copies:
         copy.wait()
+    near_product(src_ref, near_ref, x_ref, near_out)
     acc[...] = jnp.zeros_like(acc)
     owner = lax.broadcasted_iota(jnp.int32, (nvec, leaf), 1) // rank
 

time: 33 us -> 33.3 us (level)
  no operation moved by 1% of the time
where the time goes in v12:
time: 33.3 us; the launch traced here: 33.1 us
  blocking collectives  26.9 us (81%)
  Pallas kernels  5.33 us (16%)
  local copies, waits for them, and re-layouts  0.78 us (2%)
    all_to_all x1, blocking collectives, body(): lax.all_to_all(message, 'clus', split_axis=0, concat_axis=0, tiled=True)  15.9 us
    all_to_all x1, blocking collectives, body(): lax.all_to_all(returns, 'clus', split_axis=0, concat_axis=0, tiled=True)  11.1 us
    pallas_call x1, Pallas kernels, body(): pl.pallas_call(far_kernel if few else far_many_kernel, out_shape=(jax.Sha...  4.13 us
    pallas_call x1, Pallas kernels, body(): pl.pallas_call(sum_kernel, out_shape=jax.ShapeDtypeStruct((clusters, nvec...  0.82 us
    unnamed x16, local copies, waits for them, and re-layouts  0.78 us

profile of v12, /device:TPU:0, one launch (start us, length us, event | category | flops | bytes accessed | tf_op | source)
XLA Modules:
  0.0 33.1 jit_solution(17953638695109414841)
XLA Ops:
  0.0 0.0 copy-start.3
  0.0 0.0 copy-start.7
  0.0 0.0 copy-start.6
  0.0 0.7 %copy-done.3 = bf16[8,8,256]{2,1,0:T(8,128)(2,1)S(1)} copy-done((bf16[8,8,256]{2,1,0:T(8,128)(2,1)S(1)}, bf16[8,8,256]{2,1,0:T(8,128)(2,1)}, u32[]{:S(2)}) %copy-start.3) | copy-done | bytes 32792
  0.8 0.0 copy-done.7
  0.8 0.0 copy-done.6
  0.8 0.0 copy-start
  0.8 0.0 copy-start.1
  0.8 0.0 copy-start.2
  0.8 0.0 copy-start.4
  0.8 0.0 copy-start.5
  0.8 0.4 %pack.1 = bf16[16,40,128]{2,1,0:T(8,128)(2,1)S(1)} custom-call(s32[2,16]{1,0:T(2,128)S(1)} %bitcast.6, s32[2,16]{1,0:T(2,128)S(1)} %bitcast.7, bf16[8,8,256]{2,1,0:T(8,128)(2,1)S(1)} %copy-done.3, f32[8,128]{1,0:T(8,128)S(1)} %pattern.1.pattern_ref), custom_call_target="tpu_custom_call" | custom-call | flops 10000000000 | bytes 163840 | tf_op jit(solution)/shard_map/pack/pallas_call | solution.py:346
  1.2 15.9 %all_to_all.10.x_ref = bf16[16,40,128]{2,1,0:T(8,128)(2,1)S(1)} all-to-all(bf16[16,40,128]{2,1,0:T(8,128)(2,1)S(1)} %pack.1), channel_id=1, replica_groups=mesh['groups'=2,'clus'=16] {'clus'}, dimensions={0} | all-to-all | bytes 327680 | tf_op jit(solution)/shard_map/all_to_all | solution.py:355
  17.1 0.0 copy-done
  17.1 0.0 copy-done.1
  17.1 0.0 copy-done.2
  17.1 0.0 copy-done.4
  17.1 0.0 copy-done.5
  17.1 4.1 %far.1 = (bf16[16,40,128]{2,1,0:T(8,128)(2,1)S(1)}, f32[64,256]{1,0:T(8,128)S(1)}, bf16[64,256]{1,0:T(8,128)(2,1)S(1)}) custom-call(s32[256]{0:T(256)S(1)} %copy-done.4, s32[256]{0:T(256)S(1)} %copy-done.5, bf16[16,40,128]{2,1,0:T(8,128)(2,1)S(1)} %all_to_all.10.x_ref, bf16[256,32,256]{2,1,0:T(8,128)(2,1)S(1)} %copy-done.1, ...), custom_call_target="tpu_custom_call" | custom-call | flops 536870912 | bytes 8388608 | tf_op jit(solution)/shard_map/far/pallas_call | solution.py:367
  21.2 11.1 %all_to_all.11.back_ref = bf16[16,40,128]{2,1,0:T(8,128)(2,1)S(1)} all-to-all(bf16[16,40,128]{2,1,0:T(8,128)(2,1)S(1)} %get-tuple-element.8), channel_id=1, replica_groups=mesh['groups'=2,'clus'=16] {'clus'}, dimensions={0} | all-to-all | bytes 327680 | tf_op jit(solution)/shard_map/all_to_all | solution.py:388
  32.3 0.8 %sum.1 = f32[8,8,256]{2,1,0:T(8,128)} custom-call(bf16[16,40,128]{2,1,0:T(8,128)(2,1)S(1)} %all_to_all.11.back_ref, f32[64,256]{1,0:T(8,128)S(1)} %get-tuple-element.9.near_out_ref, bf16[64,256]{1,0:T(8,128)(2,1)S(1)} %get-tuple-element.10.place_ref, bf16[8,3,256,256]{3,2,1,0:T(8,128)(2,1)S(1)} %copy-done), custom_call_target="tpu_custom_call" | custom-call | flops 8388608 | bytes 131072 | tf_op jit(solution)/shard_map/sum/pallas_call | solution.py:389
  (1 shorter events, 0.0 us)
Async XLA Ops:
  0.0 0.8 %copy-start.3 = (bf16[8,8,256]{2,1,0:T(8,128)(2,1)S(1)}, bf16[8,8,256]{2,1,0:T(8,128)(2,1)}, u32[]{:S(2)}) copy-start(bf16[8,8,256]{2,1,0:T(8,128)(2,1)} %src_ref.3) | copy-start | bytes 98308
  0.0 0.8 %copy-start.7 = (s32[1,16,2]{1,2,0:T(2,128)S(1)}, s32[1,16,2]{1,2,0:T(2,128)}, u32[]{:S(2)}) copy-start(s32[1,16,2]{1,2,0:T(2,128)} %param.14) | copy-start | bytes 388
  0.0 0.8 %copy-start.6 = (s32[1,16,2]{1,2,0:T(2,128)S(1)}, s32[1,16,2]{1,2,0:T(2,128)}, u32[]{:S(2)}) copy-start(s32[1,16,2]{1,2,0:T(2,128)} %param.12) | copy-start | bytes 388
  0.8 16.3 %copy-start = (bf16[8,3,256,256]{3,2,1,0:T(8,128)(2,1)S(1)}, bf16[8,3,256,256]{3,2,1,0:T(8,128)(2,1)}, u32[]{:S(2)}) copy-start(bf16[8,3,256,256]{3,2,1,0:T(8,128)(2,1)} %near_ref.3) | copy-start | bytes 9437188
  0.8 16.3 %copy-start.1 = (bf16[256,32,256]{2,1,0:T(8,128)(2,1)S(1)}, bf16[256,32,256]{2,1,0:T(8,128)(2,1)}, u32[]{:S(2)}) copy-start(bf16[256,32,256]{2,1,0:T(8,128)(2,1)} %u_ref.1) | copy-start | bytes 12582916
  0.8 16.3 %copy-start.2 = (bf16[256,32,256]{2,1,0:T(8,128)(2,1)S(1)}, bf16[256,32,256]{2,1,0:T(8,128)(2,1)}, u32[]{:S(2)}) copy-start(bf16[256,32,256]{2,1,0:T(8,128)(2,1)} %v_ref.1) | copy-start | bytes 12582916
  0.8 16.3 %copy-start.4 = (s32[256]{0:T(256)S(1)}, s32[256]{0:T(256)}, u32[]{:S(2)}) copy-start(s32[256]{0:T(256)} %slots_any.1) | copy-start | bytes 3076
  0.8 16.3 %copy-start.5 = (s32[256]{0:T(256)S(1)}, s32[256]{0:T(256)}, u32[]{:S(2)}) copy-start(s32[256]{0:T(256)} %dests_any.1) | copy-start | bytes 3076

commit v13 on v12

--- a/solution.py
+++ b/solution.py
@@ -7,7 +7,7 @@
 
 VMEM = pl.BlockSpec(memory_space=pltpu.VMEM)
 ANY = pl.BlockSpec(memory_space=pl.ANY)
-CHUNKS = 4
+CHUNKS = 16
 
 
 def halves(x):

time: 33.3 us -> 32.9 us (0.988)
  Pallas kernels: 5.33 us -> 4.95 us
    pallas_call x1, Pallas kernels: 4.13 us -> 3.75 us  [body(): pl.pallas_call(far_kernel if few else far_many_kernel, out_shape=(jax.Sha...]
where the time goes in v13:
time: 32.9 us; the launch traced here: 32.7 us
  blocking collectives  26.9 us (82%)
  Pallas kernels  4.95 us (15%)
  local copies, waits for them, and re-layouts  0.78 us (2%)
    all_to_all x1, blocking collectives, body(): lax.all_to_all(message, 'clus', split_axis=0, concat_axis=0, tiled=True)  15.9 us
    all_to_all x1, blocking collectives, body(): lax.all_to_all(returns, 'clus', split_axis=0, concat_axis=0, tiled=True)  11.1 us
    pallas_call x1, Pallas kernels, body(): pl.pallas_call(far_kernel if few else far_many_kernel, out_shape=(jax.Sha...  3.75 us
    pallas_call x1, Pallas kernels, body(): pl.pallas_call(sum_kernel, out_shape=jax.ShapeDtypeStruct((clusters, nvec...  0.82 us
    unnamed x16, local copies, waits for them, and re-layouts  0.78 us

profile of v13, /device:TPU:0, one launch (start us, length us, event | category | flops | bytes accessed | tf_op | source)
XLA Modules:
  0.0 32.7 jit_solution(9572234219927437943)
XLA Ops:
  0.0 0.0 copy-start.3
  0.0 0.0 copy-start.7
  0.0 0.0 copy-start.6
  0.0 0.7 %copy-done.3 = bf16[8,8,256]{2,1,0:T(8,128)(2,1)S(1)} copy-done((bf16[8,8,256]{2,1,0:T(8,128)(2,1)S(1)}, bf16[8,8,256]{2,1,0:T(8,128)(2,1)}, u32[]{:S(2)}) %copy-start.3) | copy-done | bytes 32792
  0.8 0.0 copy-done.7
  0.8 0.0 copy-done.6
  0.8 0.0 copy-start
  0.8 0.0 copy-start.1
  0.8 0.0 copy-start.2
  0.8 0.0 copy-start.4
  0.8 0.0 copy-start.5
  0.8 0.4 %pack.1 = bf16[16,40,128]{2,1,0:T(8,128)(2,1)S(1)} custom-call(s32[2,16]{1,0:T(2,128)S(1)} %bitcast.6, s32[2,16]{1,0:T(2,128)S(1)} %bitcast.7, bf16[8,8,256]{2,1,0:T(8,128)(2,1)S(1)} %copy-done.3, f32[8,128]{1,0:T(8,128)S(1)} %pattern.1.pattern_ref), custom_call_target="tpu_custom_call" | custom-call | flops 10000000000 | bytes 163840 | tf_op jit(solution)/shard_map/pack/pallas_call | solution.py:346
  1.2 15.9 %all_to_all.10.x_ref = bf16[16,40,128]{2,1,0:T(8,128)(2,1)S(1)} all-to-all(bf16[16,40,128]{2,1,0:T(8,128)(2,1)S(1)} %pack.1), channel_id=1, replica_groups=mesh['groups'=2,'clus'=16] {'clus'}, dimensions={0} | all-to-all | bytes 327680 | tf_op jit(solution)/shard_map/all_to_all | solution.py:355
  17.1 0.0 copy-done
  17.1 0.0 copy-done.1
  17.1 0.0 copy-done.2
  17.1 0.0 copy-done.4
  17.1 0.0 copy-done.5
  17.1 3.8 %far.1 = (bf16[16,40,128]{2,1,0:T(8,128)(2,1)S(1)}, f32[64,256]{1,0:T(8,128)S(1)}, bf16[64,256]{1,0:T(8,128)(2,1)S(1)}) custom-call(s32[256]{0:T(256)S(1)} %copy-done.4, s32[256]{0:T(256)S(1)} %copy-done.5, bf16[16,40,128]{2,1,0:T(8,128)(2,1)S(1)} %all_to_all.10.x_ref, bf16[256,32,256]{2,1,0:T(8,128)(2,1)S(1)} %copy-done.1, ...), custom_call_target="tpu_custom_call" | custom-call | flops 536870912 | bytes 8388608 | tf_op jit(solution)/shard_map/far/pallas_call | solution.py:367
  20.9 11.1 %all_to_all.11.back_ref = bf16[16,40,128]{2,1,0:T(8,128)(2,1)S(1)} all-to-all(bf16[16,40,128]{2,1,0:T(8,128)(2,1)S(1)} %get-tuple-element.8), channel_id=1, replica_groups=mesh['groups'=2,'clus'=16] {'clus'}, dimensions={0} | all-to-all | bytes 327680 | tf_op jit(solution)/shard_map/all_to_all | solution.py:388
  31.9 0.8 %sum.1 = f32[8,8,256]{2,1,0:T(8,128)} custom-call(bf16[16,40,128]{2,1,0:T(8,128)(2,1)S(1)} %all_to_all.11.back_ref, f32[64,256]{1,0:T(8,128)S(1)} %get-tuple-element.9.near_out_ref, bf16[64,256]{1,0:T(8,128)(2,1)S(1)} %get-tuple-element.10.place_ref, bf16[8,3,256,256]{3,2,1,0:T(8,128)(2,1)S(1)} %copy-done), custom_call_target="tpu_custom_call" | custom-call | flops 8388608 | bytes 131072 | tf_op jit(solution)/shard_map/sum/pallas_call | solution.py:389
  (1 shorter events, 0.0 us)
Async XLA Ops:
  0.0 0.8 %copy-start.3 = (bf16[8,8,256]{2,1,0:T(8,128)(2,1)S(1)}, bf16[8,8,256]{2,1,0:T(8,128)(2,1)}, u32[]{:S(2)}) copy-start(bf16[8,8,256]{2,1,0:T(8,128)(2,1)} %src_ref.3) | copy-start | bytes 98308
  0.0 0.8 %copy-start.7 = (s32[1,16,2]{1,2,0:T(2,128)S(1)}, s32[1,16,2]{1,2,0:T(2,128)}, u32[]{:S(2)}) copy-start(s32[1,16,2]{1,2,0:T(2,128)} %param.14) | copy-start | bytes 388
  0.0 0.8 %copy-start.6 = (s32[1,16,2]{1,2,0:T(2,128)S(1)}, s32[1,16,2]{1,2,0:T(2,128)}, u32[]{:S(2)}) copy-start(s32[1,16,2]{1,2,0:T(2,128)} %param.12) | copy-start | bytes 388
  0.8 16.3 %copy-start = (bf16[8,3,256,256]{3,2,1,0:T(8,128)(2,1)S(1)}, bf16[8,3,256,256]{3,2,1,0:T(8,128)(2,1)}, u32[]{:S(2)}) copy-start(bf16[8,3,256,256]{3,2,1,0:T(8,128)(2,1)} %near_ref.3) | copy-start | bytes 9437188
  0.8 16.3 %copy-start.1 = (bf16[256,32,256]{2,1,0:T(8,128)(2,1)S(1)}, bf16[256,32,256]{2,1,0:T(8,128)(2,1)}, u32[]{:S(2)}) copy-start(bf16[256,32,256]{2,1,0:T(8,128)(2,1)} %u_ref.1) | copy-start | bytes 12582916
  0.8 16.3 %copy-start.2 = (bf16[256,32,256]{2,1,0:T(8,128)(2,1)S(1)}, bf16[256,32,256]{2,1,0:T(8,128)(2,1)}, u32[]{:S(2)}) copy-start(bf16[256,32,256]{2,1,0:T(8,128)(2,1)} %v_ref.1) | copy-start | bytes 12582916
  0.8 16.3 %copy-start.4 = (s32[256]{0:T(256)S(1)}, s32[256]{0:T(256)}, u32[]{:S(2)}) copy-start(s32[256]{0:T(256)} %slots_any.1) | copy-start | bytes 3076
  0.8 16.3 %copy-start.5 = (s32[256]{0:T(256)S(1)}, s32[256]{0:T(256)}, u32[]{:S(2)}) copy-start(s32[256]{0:T(256)} %dests_any.1) | copy-start | bytes 3076

commit v14 on v13

--- a/solution.py
+++ b/solution.py
@@ -196,11 +196,24 @@
         rows = [xf[slot_ref[g * group + i]] for i in range(group)]
         picked[g] = jnp.concatenate(rows, axis=0).astype(jnp.bfloat16)
     owner = lax.broadcasted_iota(jnp.int32, (nvec, leaf), 1) // rank
+
+    def coefficients(c):
+        return [
+            project(
+                picked[g],
+                u_ref[g * group : (g + 1) * group].reshape(leaf, leaf),
+                owner,
+                nvec,
+                group,
+            )
+            for g in range(c * per, (c + 1) * per)
+        ]
+
     total = None
+    ahead = coefficients(0)
     for c in range(CHUNKS):
-        for g in range(c * per, (c + 1) * per):
-            u = u_ref[g * group : (g + 1) * group].reshape(leaf, leaf)
-            kept = project(picked[g], u, owner, nvec, group)
+        now, ahead = ahead, coefficients(c + 1) if c + 1 < CHUNKS else None
+        for g, kept in zip(range(c * per, (c + 1) * per), now):
             dest = jnp.full((nvec, leaf), dest_ref[g * group], jnp.int32)
             for i in range(1, group):
                 dest = jnp.where(owner == i, dest_ref[g * group + i], dest)

time: 32.9 us -> 32.9 us (level)
  no operation moved by 1% of the time
where the time goes in v14:
time: 32.9 us; the launch traced here: 32.7 us
  blocking collectives  26.9 us (82%)
  Pallas kernels  4.95 us (15%)
  local copies, waits for them, and re-layouts  0.78 us (2%)
    all_to_all x1, blocking collectives, body(): lax.all_to_all(message, 'clus', split_axis=0, concat_axis=0, tiled=True)  15.9 us
    all_to_all x1, blocking collectives, body(): lax.all_to_all(returns, 'clus', split_axis=0, concat_axis=0, tiled=True)  11.1 us
    pallas_call x1, Pallas kernels, body(): pl.pallas_call(far_kernel if few else far_many_kernel, out_shape=(jax.Sha...  3.75 us
    pallas_call x1, Pallas kernels, body(): pl.pallas_call(sum_kernel, out_shape=jax.ShapeDtypeStruct((clusters, nvec...  0.82 us
    unnamed x16, local copies, waits for them, and re-layouts  0.78 us

profile of v14, /device:TPU:0, one launch (start us, length us, event | category | flops | bytes accessed | tf_op | source)
XLA Modules:
  0.0 32.7 jit_solution(9572234219927437943)
XLA Ops:
  0.0 0.0 copy-start.3
  0.0 0.0 copy-start.7
  0.0 0.0 copy-start.6
  0.0 0.7 %copy-done.3 = bf16[8,8,256]{2,1,0:T(8,128)(2,1)S(1)} copy-done((bf16[8,8,256]{2,1,0:T(8,128)(2,1)S(1)}, bf16[8,8,256]{2,1,0:T(8,128)(2,1)}, u32[]{:S(2)}) %copy-start.3) | copy-done | bytes 32792
  0.8 0.0 copy-done.7
  0.8 0.0 copy-done.6
  0.8 0.0 copy-start
  0.8 0.0 copy-start.1
  0.8 0.0 copy-start.2
  0.8 0.0 copy-start.4
  0.8 0.0 copy-start.5
  0.8 0.4 %pack.1 = bf16[16,40,128]{2,1,0:T(8,128)(2,1)S(1)} custom-call(s32[2,16]{1,0:T(2,128)S(1)} %bitcast.6, s32[2,16]{1,0:T(2,128)S(1)} %bitcast.7, bf16[8,8,256]{2,1,0:T(8,128)(2,1)S(1)} %copy-done.3, f32[8,128]{1,0:T(8,128)S(1)} %pattern.1.pattern_ref), custom_call_target="tpu_custom_call" | custom-call | flops 10000000000 | bytes 163840 | tf_op jit(solution)/shard_map/pack/pallas_call | solution.py:359
  1.2 15.9 %all_to_all.10.x_ref = bf16[16,40,128]{2,1,0:T(8,128)(2,1)S(1)} all-to-all(bf16[16,40,128]{2,1,0:T(8,128)(2,1)S(1)} %pack.1), channel_id=1, replica_groups=mesh['groups'=2,'clus'=16] {'clus'}, dimensions={0} | all-to-all | bytes 327680 | tf_op jit(solution)/shard_map/all_to_all | solution.py:368
  17.1 0.0 copy-done
  17.1 0.0 copy-done.1
  17.1 0.0 copy-done.2
  17.1 0.0 copy-done.4
  17.1 0.0 copy-done.5
  17.1 3.8 %far.1 = (bf16[16,40,128]{2,1,0:T(8,128)(2,1)S(1)}, f32[64,256]{1,0:T(8,128)S(1)}, bf16[64,256]{1,0:T(8,128)(2,1)S(1)}) custom-call(s32[256]{0:T(256)S(1)} %copy-done.4, s32[256]{0:T(256)S(1)} %copy-done.5, bf16[16,40,128]{2,1,0:T(8,128)(2,1)S(1)} %all_to_all.10.x_ref, bf16[256,32,256]{2,1,0:T(8,128)(2,1)S(1)} %copy-done.1, ...), custom_call_target="tpu_custom_call" | custom-call | flops 536870912 | bytes 8388608 | tf_op jit(solution)/shard_map/far/pallas_call | solution.py:380
  20.9 11.1 %all_to_all.11.back_ref = bf16[16,40,128]{2,1,0:T(8,128)(2,1)S(1)} all-to-all(bf16[16,40,128]{2,1,0:T(8,128)(2,1)S(1)} %get-tuple-element.8), channel_id=1, replica_groups=mesh['groups'=2,'clus'=16] {'clus'}, dimensions={0} | all-to-all | bytes 327680 | tf_op jit(solution)/shard_map/all_to_all | solution.py:401
  31.9 0.8 %sum.1 = f32[8,8,256]{2,1,0:T(8,128)} custom-call(bf16[16,40,128]{2,1,0:T(8,128)(2,1)S(1)} %all_to_all.11.back_ref, f32[64,256]{1,0:T(8,128)S(1)} %get-tuple-element.9.near_out_ref, bf16[64,256]{1,0:T(8,128)(2,1)S(1)} %get-tuple-element.10.place_ref, bf16[8,3,256,256]{3,2,1,0:T(8,128)(2,1)S(1)} %copy-done), custom_call_target="tpu_custom_call" | custom-call | flops 8388608 | bytes 131072 | tf_op jit(solution)/shard_map/sum/pallas_call | solution.py:402
  (1 shorter events, 0.0 us)
Async XLA Ops:
  0.0 0.8 %copy-start.3 = (bf16[8,8,256]{2,1,0:T(8,128)(2,1)S(1)}, bf16[8,8,256]{2,1,0:T(8,128)(2,1)}, u32[]{:S(2)}) copy-start(bf16[8,8,256]{2,1,0:T(8,128)(2,1)} %src_ref.3) | copy-start | bytes 98308
  0.0 0.8 %copy-start.7 = (s32[1,16,2]{1,2,0:T(2,128)S(1)}, s32[1,16,2]{1,2,0:T(2,128)}, u32[]{:S(2)}) copy-start(s32[1,16,2]{1,2,0:T(2,128)} %param.14) | copy-start | bytes 388
  0.0 0.8 %copy-start.6 = (s32[1,16,2]{1,2,0:T(2,128)S(1)}, s32[1,16,2]{1,2,0:T(2,128)}, u32[]{:S(2)}) copy-start(s32[1,16,2]{1,2,0:T(2,128)} %param.12) | copy-start | bytes 388
  0.8 16.3 %copy-start = (bf16[8,3,256,256]{3,2,1,0:T(8,128)(2,1)S(1)}, bf16[8,3,256,256]{3,2,1,0:T(8,128)(2,1)}, u32[]{:S(2)}) copy-start(bf16[8,3,256,256]{3,2,1,0:T(8,128)(2,1)} %near_ref.3) | copy-start | bytes 9437188
  0.8 16.3 %copy-start.1 = (bf16[256,32,256]{2,1,0:T(8,128)(2,1)S(1)}, bf16[256,32,256]{2,1,0:T(8,128)(2,1)}, u32[]{:S(2)}) copy-start(bf16[256,32,256]{2,1,0:T(8,128)(2,1)} %u_ref.1) | copy-start | bytes 12582916
  0.8 16.3 %copy-start.2 = (bf16[256,32,256]{2,1,0:T(8,128)(2,1)S(1)}, bf16[256,32,256]{2,1,0:T(8,128)(2,1)}, u32[]{:S(2)}) copy-start(bf16[256,32,256]{2,1,0:T(8,128)(2,1)} %v_ref.1) | copy-start | bytes 12582916
  0.8 16.3 %copy-start.4 = (s32[256]{0:T(256)S(1)}, s32[256]{0:T(256)}, u32[]{:S(2)}) copy-start(s32[256]{0:T(256)} %slots_any.1) | copy-start | bytes 3076
  0.8 16.3 %copy-start.5 = (s32[256]{0:T(256)S(1)}, s32[256]{0:T(256)}, u32[]{:S(2)}) copy-start(s32[256]{0:T(256)} %dests_any.1) | copy-start | bytes 3076

commit v15 on v13

--- a/solution.py
+++ b/solution.py
@@ -178,7 +178,7 @@
     sems,
     place,
     xf,
-    picked, wide,
+    wide,
 ):
     peers = x_ref.shape[0]
     slots, nvec, leaf = xf.shape
@@ -192,15 +192,22 @@
     for copy in copies:
         copy.wait()
     near_product(src_ref, near_ref, x_ref, near_out)
-    for g in range(groups):
-        rows = [xf[slot_ref[g * group + i]] for i in range(group)]
-        picked[g] = jnp.concatenate(rows, axis=0).astype(jnp.bfloat16)
     owner = lax.broadcasted_iota(jnp.int32, (nvec, leaf), 1) // rank
+
+    def coefficients(c):
+        kept = []
+        for g in range(c * per, (c + 1) * per):
+            rows = [xf[slot_ref[g * group + i]] for i in range(group)]
+            rows = jnp.concatenate(rows, axis=0).astype(jnp.bfloat16)
+            u = u_ref[g * group : (g + 1) * group].reshape(leaf, leaf)
+            kept.append(project(rows, u, owner, nvec, group))
+        return kept
+
     total = None
+    ahead = coefficients(0)
     for c in range(CHUNKS):
-        for g in range(c * per, (c + 1) * per):
-            u = u_ref[g * group : (g + 1) * group].reshape(leaf, leaf)
-            kept = project(picked[g], u, owner, nvec, group)
+        now, ahead = ahead, coefficients(c + 1) if c + 1 < CHUNKS else None
+        for g, kept in zip(range(c * per, (c + 1) * per), now):
             dest = jnp.full((nvec, leaf), dest_ref[g * group], jnp.int32)
             for i in range(1, group):
                 dest = jnp.where(owner == i, dest_ref[g * group + i], dest)
@@ -356,7 +363,6 @@
     few = slots <= 32
     if few:
         scratch = [
-            pltpu.VMEM((blocks * rank // leaf, leaf // rank * nvec, leaf), jnp.bfloat16),
             pltpu.VMEM((slots * nvec, blocks * rank), jnp.bfloat16),
         ]
     else:

time: 32.9 us -> 32.9 us (level)
  no operation moved by 1% of the time
where the time goes in v15:
time: 32.9 us; the launch traced here: 32.7 us
  blocking collectives  26.9 us (82%)
  Pallas kernels  4.95 us (15%)
  local copies, waits for them, and re-layouts  0.78 us (2%)
    all_to_all x1, blocking collectives, body(): lax.all_to_all(message, 'clus', split_axis=0, concat_axis=0, tiled=True)  15.9 us
    all_to_all x1, blocking collectives, body(): lax.all_to_all(returns, 'clus', split_axis=0, concat_axis=0, tiled=True)  11.1 us
    pallas_call x1, Pallas kernels, body(): pl.pallas_call(far_kernel if few else far_many_kernel, out_shape=(jax.Sha...  3.75 us
    pallas_call x1, Pallas kernels, body(): pl.pallas_call(sum_kernel, out_shape=jax.ShapeDtypeStruct((clusters, nvec...  0.82 us
    unnamed x16, local copies, waits for them, and re-layouts  0.78 us

profile of v15, /device:TPU:0, one launch (start us, length us, event | category | flops | bytes accessed | tf_op | source)
XLA Modules:
  0.0 32.7 jit_solution(9572234219927437943)
XLA Ops:
  0.0 0.0 copy-start.3
  0.0 0.0 copy-start.7
  0.0 0.0 copy-start.6
  0.0 0.7 %copy-done.3 = bf16[8,8,256]{2,1,0:T(8,128)(2,1)S(1)} copy-done((bf16[8,8,256]{2,1,0:T(8,128)(2,1)S(1)}, bf16[8,8,256]{2,1,0:T(8,128)(2,1)}, u32[]{:S(2)}) %copy-start.3) | copy-done | bytes 32792
  0.8 0.0 copy-done.7
  0.8 0.0 copy-done.6
  0.8 0.0 copy-start
  0.8 0.0 copy-start.1
  0.8 0.0 copy-start.2
  0.8 0.0 copy-start.4
  0.8 0.0 copy-start.5
  0.8 0.4 %pack.1 = bf16[16,40,128]{2,1,0:T(8,128)(2,1)S(1)} custom-call(s32[2,16]{1,0:T(2,128)S(1)} %bitcast.6, s32[2,16]{1,0:T(2,128)S(1)} %bitcast.7, bf16[8,8,256]{2,1,0:T(8,128)(2,1)S(1)} %copy-done.3, f32[8,128]{1,0:T(8,128)S(1)} %pattern.1.pattern_ref), custom_call_target="tpu_custom_call" | custom-call | flops 10000000000 | bytes 163840 | tf_op jit(solution)/shard_map/pack/pallas_call | solution.py:353
  1.2 15.9 %all_to_all.10.x_ref = bf16[16,40,128]{2,1,0:T(8,128)(2,1)S(1)} all-to-all(bf16[16,40,128]{2,1,0:T(8,128)(2,1)S(1)} %pack.1), channel_id=1, replica_groups=mesh['groups'=2,'clus'=16] {'clus'}, dimensions={0} | all-to-all | bytes 327680 | tf_op jit(solution)/shard_map/all_to_all | solution.py:362
  17.1 0.0 copy-done
  17.1 0.0 copy-done.1
  17.1 0.0 copy-done.2
  17.1 0.0 copy-done.4
  17.1 0.0 copy-done.5
  17.1 3.8 %far.1 = (bf16[16,40,128]{2,1,0:T(8,128)(2,1)S(1)}, f32[64,256]{1,0:T(8,128)S(1)}, bf16[64,256]{1,0:T(8,128)(2,1)S(1)}) custom-call(s32[256]{0:T(256)S(1)} %copy-done.4, s32[256]{0:T(256)S(1)} %copy-done.5, bf16[16,40,128]{2,1,0:T(8,128)(2,1)S(1)} %all_to_all.10.x_ref, bf16[256,32,256]{2,1,0:T(8,128)(2,1)S(1)} %copy-done.1, ...), custom_call_target="tpu_custom_call" | custom-call | flops 536870912 | bytes 8388608 | tf_op jit(solution)/shard_map/far/pallas_call | solution.py:373
  20.9 11.1 %all_to_all.11.back_ref = bf16[16,40,128]{2,1,0:T(8,128)(2,1)S(1)} all-to-all(bf16[16,40,128]{2,1,0:T(8,128)(2,1)S(1)} %get-tuple-element.8), channel_id=1, replica_groups=mesh['groups'=2,'clus'=16] {'clus'}, dimensions={0} | all-to-all | bytes 327680 | tf_op jit(solution)/shard_map/all_to_all | solution.py:394
  31.9 0.8 %sum.1 = f32[8,8,256]{2,1,0:T(8,128)} custom-call(bf16[16,40,128]{2,1,0:T(8,128)(2,1)S(1)} %all_to_all.11.back_ref, f32[64,256]{1,0:T(8,128)S(1)} %get-tuple-element.9.near_out_ref, bf16[64,256]{1,0:T(8,128)(2,1)S(1)} %get-tuple-element.10.place_ref, bf16[8,3,256,256]{3,2,1,0:T(8,128)(2,1)S(1)} %copy-done), custom_call_target="tpu_custom_call" | custom-call | flops 8388608 | bytes 131072 | tf_op jit(solution)/shard_map/sum/pallas_call | solution.py:395
  (1 shorter events, 0.0 us)
Async XLA Ops:
  0.0 0.8 %copy-start.3 = (bf16[8,8,256]{2,1,0:T(8,128)(2,1)S(1)}, bf16[8,8,256]{2,1,0:T(8,128)(2,1)}, u32[]{:S(2)}) copy-start(bf16[8,8,256]{2,1,0:T(8,128)(2,1)} %src_ref.3) | copy-start | bytes 98308
  0.0 0.8 %copy-start.7 = (s32[1,16,2]{1,2,0:T(2,128)S(1)}, s32[1,16,2]{1,2,0:T(2,128)}, u32[]{:S(2)}) copy-start(s32[1,16,2]{1,2,0:T(2,128)} %param.14) | copy-start | bytes 388
  0.0 0.8 %copy-start.6 = (s32[1,16,2]{1,2,0:T(2,128)S(1)}, s32[1,16,2]{1,2,0:T(2,128)}, u32[]{:S(2)}) copy-start(s32[1,16,2]{1,2,0:T(2,128)} %param.12) | copy-start | bytes 388
  0.8 16.3 %copy-start = (bf16[8,3,256,256]{3,2,1,0:T(8,128)(2,1)S(1)}, bf16[8,3,256,256]{3,2,1,0:T(8,128)(2,1)}, u32[]{:S(2)}) copy-start(bf16[8,3,256,256]{3,2,1,0:T(8,128)(2,1)} %near_ref.3) | copy-start | bytes 9437188
  0.8 16.3 %copy-start.1 = (bf16[256,32,256]{2,1,0:T(8,128)(2,1)S(1)}, bf16[256,32,256]{2,1,0:T(8,128)(2,1)}, u32[]{:S(2)}) copy-start(bf16[256,32,256]{2,1,0:T(8,128)(2,1)} %u_ref.1) | copy-start | bytes 12582916
  0.8 16.3 %copy-start.2 = (bf16[256,32,256]{2,1,0:T(8,128)(2,1)S(1)}, bf16[256,32,256]{2,1,0:T(8,128)(2,1)}, u32[]{:S(2)}) copy-start(bf16[256,32,256]{2,1,0:T(8,128)(2,1)} %v_ref.1) | copy-start | bytes 12582916
  0.8 16.3 %copy-start.4 = (s32[256]{0:T(256)S(1)}, s32[256]{0:T(256)}, u32[]{:S(2)}) copy-start(s32[256]{0:T(256)} %slots_any.1) | copy-start | bytes 3076
  0.8 16.3 %copy-start.5 = (s32[256]{0:T(256)S(1)}, s32[256]{0:T(256)}, u32[]{:S(2)}) copy-start(s32[256]{0:T(256)} %dests_any.1) | copy-start | bytes 3076

commit v16 on v14

--- a/solution.py
+++ b/solution.py
@@ -178,7 +178,8 @@
     sems,
     place,
     xf,
-    picked, wide,
+    picked,
+    acc,
 ):
     peers = x_ref.shape[0]
     slots, nvec, leaf = xf.shape
@@ -209,27 +210,26 @@
             for g in range(c * per, (c + 1) * per)
         ]
 
-    total = None
+    acc[...] = jnp.zeros_like(acc)
     ahead = coefficients(0)
     for c in range(CHUNKS):
         now, ahead = ahead, coefficients(c + 1) if c + 1 < CHUNKS else None
         for g, kept in zip(range(c * per, (c + 1) * per), now):
-            dest = jnp.full((nvec, leaf), dest_ref[g * group], jnp.int32)
+            ats = [dest_ref[g * group + i] for i in range(group)]
+            dest = jnp.full((nvec, leaf), ats[0], jnp.int32)
             for i in range(1, group):
-                dest = jnp.where(owner == i, dest_ref[g * group + i], dest)
-            dest = dest.astype(jnp.float32)
-            kept = jnp.concatenate([kept, kept], axis=0).astype(jnp.bfloat16)
-            dest = jnp.concatenate([dest, dest - 1.0], axis=0).astype(jnp.bfloat16)
-            for o in range(0, slots, 2):
-                wide[o * nvec : (o + 2) * nvec, g * leaf : (g + 1) * leaf] = jnp.where(
-                    dest == jnp.bfloat16(o), kept, jnp.bfloat16(0)
-                )
-        v = v_ref[c * per * group : (c + 1) * per * group].reshape(per * leaf, leaf)
-        part = jnp.dot(
-            wide[:, c * per * leaf : (c + 1) * per * leaf], v, preferred_element_type=jnp.float32
-        )
-        total = part if total is None else total + part
-    put_returns(total, x_ref, src_ref, out_ref)
+                dest = jnp.where(owner == i, ats[i], dest)
+            same = [jnp.where(dest == at, kept, 0.0) for at in ats]
+            v = v_ref[g * group : (g + 1) * group].reshape(leaf, leaf)
+            terms = jnp.dot(
+                jnp.concatenate(same, axis=0).astype(jnp.bfloat16),
+                v,
+                preferred_element_type=jnp.float32,
+            )
+            sums = [acc[at] + terms[i * nvec : (i + 1) * nvec] for i, at in enumerate(ats)]
+            for at, value in zip(ats, sums):
+                acc[at] = value
+    put_returns(acc[...].reshape(slots * nvec, leaf), x_ref, src_ref, out_ref)
 
 
 def far_many_kernel(
@@ -249,7 +249,8 @@
     sems,
     place,
     xf,
-    coef, acc,
+    coef,
+    acc,
 ):
     slots, nvec, leaf = xf.shape
     blocks, rank, _ = u_ref.shape
@@ -370,7 +371,7 @@
     if few:
         scratch = [
             pltpu.VMEM((blocks * rank // leaf, leaf // rank * nvec, leaf), jnp.bfloat16),
-            pltpu.VMEM((slots * nvec, blocks * rank), jnp.bfloat16),
+            pltpu.VMEM((slots, nvec, leaf), jnp.float32),
         ]
     else:
         scratch = [

time: 32.9 us -> 32.6 us (level)
  Pallas kernels: 4.95 us -> 4.56 us
    pallas_call x1, Pallas kernels: 3.75 us -> 3.36 us  [body(): pl.pallas_call(far_kernel if few else far_many_kernel, out_shape=(jax.Sha...]
where the time goes in v16:
time: 32.6 us; the launch traced here: 32.3 us
  blocking collectives  26.9 us (83%)
  Pallas kernels  4.56 us (14%)
  local copies, waits for them, and re-layouts  0.78 us (2%)
    all_to_all x1, blocking collectives, body(): lax.all_to_all(message, 'clus', split_axis=0, concat_axis=0, tiled=True)  15.9 us
    all_to_all x1, blocking collectives, body(): lax.all_to_all(returns, 'clus', split_axis=0, concat_axis=0, tiled=True)  11.1 us
    pallas_call x1, Pallas kernels, body(): pl.pallas_call(far_kernel if few else far_many_kernel, out_shape=(jax.Sha...  3.36 us
    pallas_call x1, Pallas kernels, body(): pl.pallas_call(sum_kernel, out_shape=jax.ShapeDtypeStruct((clusters, nvec...  0.82 us
    unnamed x16, local copies, waits for them, and re-layouts  0.78 us

profile of v16, /device:TPU:0, one launch (start us, length us, event | category | flops | bytes accessed | tf_op | source)
XLA Modules:
  0.0 32.3 jit_solution(16956625615134068809)
XLA Ops:
  0.0 0.0 copy-start.3
  0.0 0.0 copy-start.7
  0.0 0.0 copy-start.6
  0.0 0.7 %copy-done.3 = bf16[8,8,256]{2,1,0:T(8,128)(2,1)S(1)} copy-done((bf16[8,8,256]{2,1,0:T(8,128)(2,1)S(1)}, bf16[8,8,256]{2,1,0:T(8,128)(2,1)}, u32[]{:S(2)}) %copy-start.3) | copy-done | bytes 32792
  0.8 0.0 copy-done.7
  0.8 0.0 copy-done.6
  0.8 0.0 copy-start
  0.8 0.0 copy-start.1
  0.8 0.0 copy-start.2
  0.8 0.0 copy-start.4
  0.8 0.0 copy-start.5
  0.8 0.4 %pack.1 = bf16[16,40,128]{2,1,0:T(8,128)(2,1)S(1)} custom-call(s32[2,16]{1,0:T(2,128)S(1)} %bitcast.6, s32[2,16]{1,0:T(2,128)S(1)} %bitcast.7, bf16[8,8,256]{2,1,0:T(8,128)(2,1)S(1)} %copy-done.3, f32[8,128]{1,0:T(8,128)S(1)} %pattern.1.pattern_ref), custom_call_target="tpu_custom_call" | custom-call | flops 10000000000 | bytes 163840 | tf_op jit(solution)/shard_map/pack/pallas_call | solution.py:360
  1.2 15.9 %all_to_all.10.x_ref = bf16[16,40,128]{2,1,0:T(8,128)(2,1)S(1)} all-to-all(bf16[16,40,128]{2,1,0:T(8,128)(2,1)S(1)} %pack.1), channel_id=1, replica_groups=mesh['groups'=2,'clus'=16] {'clus'}, dimensions={0} | all-to-all | bytes 327680 | tf_op jit(solution)/shard_map/all_to_all | solution.py:369
  17.1 0.0 copy-done
  17.1 0.0 copy-done.1
  17.1 0.0 copy-done.2
  17.1 0.0 copy-done.4
  17.1 0.0 copy-done.5
  17.1 3.4 %far.1 = (bf16[16,40,128]{2,1,0:T(8,128)(2,1)S(1)}, f32[64,256]{1,0:T(8,128)S(1)}, bf16[64,256]{1,0:T(8,128)(2,1)S(1)}) custom-call(s32[256]{0:T(256)S(1)} %copy-done.4, s32[256]{0:T(256)S(1)} %copy-done.5, bf16[16,40,128]{2,1,0:T(8,128)(2,1)S(1)} %all_to_all.10.x_ref, bf16[256,32,256]{2,1,0:T(8,128)(2,1)S(1)} %copy-done.1, ...), custom_call_target="tpu_custom_call" | custom-call | flops 536870912 | bytes 8388608 | tf_op jit(solution)/shard_map/far/pallas_call | solution.py:381
  20.5 11.1 %all_to_all.11.back_ref = bf16[16,40,128]{2,1,0:T(8,128)(2,1)S(1)} all-to-all(bf16[16,40,128]{2,1,0:T(8,128)(2,1)S(1)} %get-tuple-element.8), channel_id=1, replica_groups=mesh['groups'=2,'clus'=16] {'clus'}, dimensions={0} | all-to-all | bytes 327680 | tf_op jit(solution)/shard_map/all_to_all | solution.py:402
  31.5 0.8 %sum.1 = f32[8,8,256]{2,1,0:T(8,128)} custom-call(bf16[16,40,128]{2,1,0:T(8,128)(2,1)S(1)} %all_to_all.11.back_ref, f32[64,256]{1,0:T(8,128)S(1)} %get-tuple-element.9.near_out_ref, bf16[64,256]{1,0:T(8,128)(2,1)S(1)} %get-tuple-element.10.place_ref, bf16[8,3,256,256]{3,2,1,0:T(8,128)(2,1)S(1)} %copy-done), custom_call_target="tpu_custom_call" | custom-call | flops 8388608 | bytes 131072 | tf_op jit(solution)/shard_map/sum/pallas_call | solution.py:403
  (1 shorter events, 0.0 us)
Async XLA Ops:
  0.0 0.8 %copy-start.3 = (bf16[8,8,256]{2,1,0:T(8,128)(2,1)S(1)}, bf16[8,8,256]{2,1,0:T(8,128)(2,1)}, u32[]{:S(2)}) copy-start(bf16[8,8,256]{2,1,0:T(8,128)(2,1)} %src_ref.3) | copy-start | bytes 98308
  0.0 0.8 %copy-start.7 = (s32[1,16,2]{1,2,0:T(2,128)S(1)}, s32[1,16,2]{1,2,0:T(2,128)}, u32[]{:S(2)}) copy-start(s32[1,16,2]{1,2,0:T(2,128)} %param.14) | copy-start | bytes 388
  0.0 0.8 %copy-start.6 = (s32[1,16,2]{1,2,0:T(2,128)S(1)}, s32[1,16,2]{1,2,0:T(2,128)}, u32[]{:S(2)}) copy-start(s32[1,16,2]{1,2,0:T(2,128)} %param.12) | copy-start | bytes 388
  0.8 16.3 %copy-start = (bf16[8,3,256,256]{3,2,1,0:T(8,128)(2,1)S(1)}, bf16[8,3,256,256]{3,2,1,0:T(8,128)(2,1)}, u32[]{:S(2)}) copy-start(bf16[8,3,256,256]{3,2,1,0:T(8,128)(2,1)} %near_ref.3) | copy-start | bytes 9437188
  0.8 16.3 %copy-start.1 = (bf16[256,32,256]{2,1,0:T(8,128)(2,1)S(1)}, bf16[256,32,256]{2,1,0:T(8,128)(2,1)}, u32[]{:S(2)}) copy-start(bf16[256,32,256]{2,1,0:T(8,128)(2,1)} %u_ref.1) | copy-start | bytes 12582916
  0.8 16.3 %copy-start.2 = (bf16[256,32,256]{2,1,0:T(8,128)(2,1)S(1)}, bf16[256,32,256]{2,1,0:T(8,128)(2,1)}, u32[]{:S(2)}) copy-start(bf16[256,32,256]{2,1,0:T(8,128)(2,1)} %v_ref.1) | copy-start | bytes 12582916
  0.8 16.3 %copy-start.4 = (s32[256]{0:T(256)S(1)}, s32[256]{0:T(256)}, u32[]{:S(2)}) copy-start(s32[256]{0:T(256)} %slots_any.1) | copy-start | bytes 3076
  0.8 16.3 %copy-start.5 = (s32[256]{0:T(256)S(1)}, s32[256]{0:T(256)}, u32[]{:S(2)}) copy-start(s32[256]{0:T(256)} %dests_any.1) | copy-start | bytes 3076

commit v17 on v13

--- a/solution.py
+++ b/solution.py
@@ -7,7 +7,6 @@
 
 VMEM = pl.BlockSpec(memory_space=pltpu.VMEM)
 ANY = pl.BlockSpec(memory_space=pl.ANY)
-CHUNKS = 16
 
 
 def halves(x):
@@ -178,14 +177,14 @@
     sems,
     place,
     xf,
-    picked, wide,
+    picked,
+    acc,
 ):
     peers = x_ref.shape[0]
     slots, nvec, leaf = xf.shape
     blocks, rank, _ = u_ref.shape
     group = leaf // rank
     groups = blocks // group
-    per = groups // CHUNKS
     copies = load_slots(slots_any, dests_any, slot_ref, dest_ref, sems)
     widen_sources(x_ref, xf)
     placement(x_ref, pattern_ref, place, place_out)
@@ -196,80 +195,37 @@
         rows = [xf[slot_ref[g * group + i]] for i in range(group)]
         picked[g] = jnp.concatenate(rows, axis=0).astype(jnp.bfloat16)
     owner = lax.broadcasted_iota(jnp.int32, (nvec, leaf), 1) // rank
-    total = None
-    for c in range(CHUNKS):
-        for g in range(c * per, (c + 1) * per):
-            u = u_ref[g * group : (g + 1) * group].reshape(leaf, leaf)
-            kept = project(picked[g], u, owner, nvec, group)
-            dest = jnp.full((nvec, leaf), dest_ref[g * group], jnp.int32)
-            for i in range(1, group):
-                dest = jnp.where(owner == i, dest_ref[g * group + i], dest)
-            dest = dest.astype(jnp.float32)
-            kept = jnp.concatenate([kept, kept], axis=0).astype(jnp.bfloat16)
-            dest = jnp.concatenate([dest, dest - 1.0], axis=0).astype(jnp.bfloat16)
-            for o in range(0, slots, 2):
-                wide[o * nvec : (o + 2) * nvec, g * leaf : (g + 1) * leaf] = jnp.where(
-                    dest == jnp.bfloat16(o), kept, jnp.bfloat16(0)
-                )
-        v = v_ref[c * per * group : (c + 1) * per * group].reshape(per * leaf, leaf)
-        part = jnp.dot(
-            wide[:, c * per * leaf : (c + 1) * per * leaf], v, preferred_element_type=jnp.float32
+
+    def coefficients(g):
+        u = u_ref[g * group : (g + 1) * group].reshape(leaf, leaf)
+        return project(picked[g], u, owner, nvec, group)
+
+    def contributions(g, kept, ats):
+        dest = jnp.full((nvec, leaf), ats[0], jnp.int32)
+        for i in range(1, group):
+            dest = jnp.where(owner == i, ats[i], dest)
+        same = [jnp.where(dest == at, kept, 0.0) for at in ats]
+        return jnp.dot(
+            jnp.concatenate(same, axis=0).astype(jnp.bfloat16),
+            v_ref[g * group : (g + 1) * group].reshape(leaf, leaf),
+            preferred_element_type=jnp.float32,
         )
-        total = part if total is None else total + part
-    put_returns(total, x_ref, src_ref, out_ref)
-
-
-def far_many_kernel(
-    slots_any,
-    dests_any,
-    x_ref,
-    u_ref,
-    v_ref,
-    src_ref,
-    near_ref,
-    pattern_ref,
-    out_ref,
-    near_out,
-    place_out,
-    slot_ref,
-    dest_ref,
-    sems,
-    place,
-    xf,
-    coef, acc,
-):
-    slots, nvec, leaf = xf.shape
-    blocks, rank, _ = u_ref.shape
-    group = leaf // rank
-    copies = load_slots(slots_any, dests_any, slot_ref, dest_ref, sems)
-    widen_sources(x_ref, xf)
-    placement(x_ref, pattern_ref, place, place_out)
-    for copy in copies:
-        copy.wait()
-    near_product(src_ref, near_ref, x_ref, near_out)
+
+    def accumulate(terms, ats):
+        sums = [acc[at] + terms[i * nvec : (i + 1) * nvec] for i, at in enumerate(ats)]
+        for at, value in zip(ats, sums):
+            acc[at] = value
+
     acc[...] = jnp.zeros_like(acc)
-    owner = lax.broadcasted_iota(jnp.int32, (nvec, leaf), 1) // rank
-
-    def forward(g, carry):
-        rows = [xf[slot_ref[g * group + i]] for i in range(group)]
-        picked = jnp.concatenate(rows, axis=0).astype(jnp.bfloat16)
-        u = u_ref[pl.ds(g * group, group)].reshape(leaf, leaf)
-        coef[g] = project(picked, u, owner, nvec, group)
-        return carry
-
-    def backward(g, carry):
-        kept = coef[g]
-        spread = jnp.concatenate(
-            [jnp.where(owner == i, kept, 0.0) for i in range(group)], axis=0
-        ).astype(jnp.bfloat16)
-        v = v_ref[pl.ds(g * group, group)].reshape(leaf, leaf)
-        terms = jnp.dot(spread, v, preferred_element_type=jnp.float32)
-        for i in range(group):
-            acc[dest_ref[g * group + i]] += terms[i * nvec : (i + 1) * nvec]
-        return carry
-
-    lax.fori_loop(0, blocks // group, forward, 0, unroll=4)
-    lax.fori_loop(0, blocks // group, backward, 0, unroll=4)
+    kept, late = coefficients(0), None
+    for g in range(groups):
+        ahead = coefficients(g + 1) if g + 1 < groups else None
+        ats = [dest_ref[g * group + i] for i in range(group)]
+        terms = contributions(g, kept, ats)
+        if late is not None:
+            accumulate(*late)
+        kept, late = ahead, (terms, ats)
+    accumulate(*late)
     put_returns(acc[...].reshape(slots * nvec, leaf), x_ref, src_ref, out_ref)
 
 
@@ -353,19 +309,8 @@
         name="pack",
     )(send_list[0].T, ret_list[0].T, sources, pattern)
     incoming = lax.all_to_all(message, "clus", split_axis=0, concat_axis=0, tiled=True)
-    few = slots <= 32
-    if few:
-        scratch = [
-            pltpu.VMEM((blocks * rank // leaf, leaf // rank * nvec, leaf), jnp.bfloat16),
-            pltpu.VMEM((slots * nvec, blocks * rank), jnp.bfloat16),
-        ]
-    else:
-        scratch = [
-            pltpu.VMEM((blocks * rank // leaf, nvec, leaf), jnp.float32),
-            pltpu.VMEM((slots, nvec, leaf), jnp.float32),
-        ]
     returns, near_part, place = pl.pallas_call(
-        far_kernel if few else far_many_kernel,
+        far_kernel,
         out_shape=(
             jax.ShapeDtypeStruct((peers, rows, leaf // 2), jnp.bfloat16),
             jax.ShapeDtypeStruct((clusters * nvec, leaf), jnp.float32),
@@ -379,8 +324,9 @@
             pltpu.SemaphoreType.DMA((2,)),
             pltpu.VMEM((slots * nvec, leaf // 2), jnp.float32),
             pltpu.VMEM((slots, nvec, leaf), jnp.float32),
-        ]
-        + scratch,
+            pltpu.VMEM((blocks * rank // leaf, leaf // rank * nvec, leaf), jnp.bfloat16),
+            pltpu.VMEM((slots, nvec, leaf), jnp.float32),
+        ],
         compiler_params=pltpu.CompilerParams(vmem_limit_bytes=16 * 2**20),
         cost_estimate=cost(4 * blocks * 8 * nvec * leaf * rank, 4 * blocks * rank * leaf),
         name="far",

time: 32.9 us -> 33.7 us (1.024)
  Pallas kernels: 4.95 us -> 5.67 us
    pallas_call x1, Pallas kernels: 3.75 us -> 4.47 us  [body(): pl.pallas_call(far_kernel, out_shape=(jax.ShapeDtypeStruct((peers, rows,...]
where the time goes in v17:
time: 33.7 us; the launch traced here: 33.4 us
  blocking collectives  26.9 us (80%)
  Pallas kernels  5.67 us (17%)
  local copies, waits for them, and re-layouts  0.78 us (2%)
    all_to_all x1, blocking collectives, body(): lax.all_to_all(message, 'clus', split_axis=0, concat_axis=0, tiled=True)  15.9 us
    all_to_all x1, blocking collectives, body(): lax.all_to_all(returns, 'clus', split_axis=0, concat_axis=0, tiled=True)  11.1 us
    pallas_call x1, Pallas kernels, body(): pl.pallas_call(far_kernel, out_shape=(jax.ShapeDtypeStruct((peers, rows,...  4.47 us
    pallas_call x1, Pallas kernels, body(): pl.pallas_call(sum_kernel, out_shape=jax.ShapeDtypeStruct((clusters, nvec...  0.82 us
    unnamed x16, local copies, waits for them, and re-layouts  0.78 us

profile of v17, /device:TPU:0, one launch (start us, length us, event | category | flops | bytes accessed | tf_op | source)
XLA Modules:
  0.0 33.4 jit_solution(4954907457167718349)
XLA Ops:
  0.0 0.0 copy-start.3
  0.0 0.0 copy-start.7
  0.0 0.0 copy-start.6
  0.0 0.7 %copy-done.3 = bf16[8,8,256]{2,1,0:T(8,128)(2,1)S(1)} copy-done((bf16[8,8,256]{2,1,0:T(8,128)(2,1)S(1)}, bf16[8,8,256]{2,1,0:T(8,128)(2,1)}, u32[]{:S(2)}) %copy-start.3) | copy-done | bytes 32792
  0.8 0.0 copy-done.7
  0.8 0.0 copy-done.6
  0.8 0.0 copy-start
  0.8 0.0 copy-start.1
  0.8 0.0 copy-start.2
  0.8 0.0 copy-start.4
  0.8 0.0 copy-start.5
  0.8 0.4 %pack.1 = bf16[16,40,128]{2,1,0:T(8,128)(2,1)S(1)} custom-call(s32[2,16]{1,0:T(2,128)S(1)} %bitcast.6, s32[2,16]{1,0:T(2,128)S(1)} %bitcast.7, bf16[8,8,256]{2,1,0:T(8,128)(2,1)S(1)} %copy-done.3, f32[8,128]{1,0:T(8,128)S(1)} %pattern.1.pattern_ref), custom_call_target="tpu_custom_call" | custom-call | flops 10000000000 | bytes 163840 | tf_op jit(solution)/shard_map/pack/pallas_call | solution.py:302
  1.2 15.9 %all_to_all.10.x_ref = bf16[16,40,128]{2,1,0:T(8,128)(2,1)S(1)} all-to-all(bf16[16,40,128]{2,1,0:T(8,128)(2,1)S(1)} %pack.1), channel_id=1, replica_groups=mesh['groups'=2,'clus'=16] {'clus'}, dimensions={0} | all-to-all | bytes 327680 | tf_op jit(solution)/shard_map/all_to_all | solution.py:311
  17.1 0.0 copy-done
  17.1 0.0 copy-done.1
  17.1 0.0 copy-done.2
  17.1 0.0 copy-done.4
  17.1 0.0 copy-done.5
  17.1 4.5 %far.1 = (bf16[16,40,128]{2,1,0:T(8,128)(2,1)S(1)}, f32[64,256]{1,0:T(8,128)S(1)}, bf16[64,256]{1,0:T(8,128)(2,1)S(1)}) custom-call(s32[256]{0:T(256)S(1)} %copy-done.4, s32[256]{0:T(256)S(1)} %copy-done.5, bf16[16,40,128]{2,1,0:T(8,128)(2,1)S(1)} %all_to_all.10.x_ref, bf16[256,32,256]{2,1,0:T(8,128)(2,1)S(1)} %copy-done.1, ...), custom_call_target="tpu_custom_call" | custom-call | flops 536870912 | bytes 8388608 | tf_op jit(solution)/shard_map/far/pallas_call | solution.py:312
  21.6 11.1 %all_to_all.11.back_ref = bf16[16,40,128]{2,1,0:T(8,128)(2,1)S(1)} all-to-all(bf16[16,40,128]{2,1,0:T(8,128)(2,1)S(1)} %get-tuple-element.8), channel_id=1, replica_groups=mesh['groups'=2,'clus'=16] {'clus'}, dimensions={0} | all-to-all | bytes 327680 | tf_op jit(solution)/shard_map/all_to_all | solution.py:334
  32.6 0.8 %sum.1 = f32[8,8,256]{2,1,0:T(8,128)} custom-call(bf16[16,40,128]{2,1,0:T(8,128)(2,1)S(1)} %all_to_all.11.back_ref, f32[64,256]{1,0:T(8,128)S(1)} %get-tuple-element.9.near_out_ref, bf16[64,256]{1,0:T(8,128)(2,1)S(1)} %get-tuple-element.10.place_ref, bf16[8,3,256,256]{3,2,1,0:T(8,128)(2,1)S(1)} %copy-done), custom_call_target="tpu_custom_call" | custom-call | flops 8388608 | bytes 131072 | tf_op jit(solution)/shard_map/sum/pallas_call | solution.py:335
  (1 shorter events, 0.0 us)
Async XLA Ops:
  0.0 0.8 %copy-start.3 = (bf16[8,8,256]{2,1,0:T(8,128)(2,1)S(1)}, bf16[8,8,256]{2,1,0:T(8,128)(2,1)}, u32[]{:S(2)}) copy-start(bf16[8,8,256]{2,1,0:T(8,128)(2,1)} %src_ref.3) | copy-start | bytes 98308
  0.0 0.8 %copy-start.7 = (s32[1,16,2]{1,2,0:T(2,128)S(1)}, s32[1,16,2]{1,2,0:T(2,128)}, u32[]{:S(2)}) copy-start(s32[1,16,2]{1,2,0:T(2,128)} %param.14) | copy-start | bytes 388
  0.0 0.8 %copy-start.6 = (s32[1,16,2]{1,2,0:T(2,128)S(1)}, s32[1,16,2]{1,2,0:T(2,128)}, u32[]{:S(2)}) copy-start(s32[1,16,2]{1,2,0:T(2,128)} %param.12) | copy-start | bytes 388
  0.8 16.3 %copy-start = (bf16[8,3,256,256]{3,2,1,0:T(8,128)(2,1)S(1)}, bf16[8,3,256,256]{3,2,1,0:T(8,128)(2,1)}, u32[]{:S(2)}) copy-start(bf16[8,3,256,256]{3,2,1,0:T(8,128)(2,1)} %near_ref.3) | copy-start | bytes 9437188
  0.8 16.3 %copy-start.1 = (bf16[256,32,256]{2,1,0:T(8,128)(2,1)S(1)}, bf16[256,32,256]{2,1,0:T(8,128)(2,1)}, u32[]{:S(2)}) copy-start(bf16[256,32,256]{2,1,0:T(8,128)(2,1)} %u_ref.1) | copy-start | bytes 12582916
  0.8 16.3 %copy-start.2 = (bf16[256,32,256]{2,1,0:T(8,128)(2,1)S(1)}, bf16[256,32,256]{2,1,0:T(8,128)(2,1)}, u32[]{:S(2)}) copy-start(bf16[256,32,256]{2,1,0:T(8,128)(2,1)} %v_ref.1) | copy-start | bytes 12582916
  0.8 16.3 %copy-start.4 = (s32[256]{0:T(256)S(1)}, s32[256]{0:T(256)}, u32[]{:S(2)}) copy-start(s32[256]{0:T(256)} %slots_any.1) | copy-start | bytes 3076
  0.8 16.3 %copy-start.5 = (s32[256]{0:T(256)S(1)}, s32[256]{0:T(256)}, u32[]{:S(2)}) copy-start(s32[256]{0:T(256)} %dests_any.1) | copy-start | bytes 3076

commit v18 on v17

--- a/solution.py
+++ b/solution.py
@@ -6,6 +6,7 @@
 from jax.sharding import PartitionSpec as P
 
 VMEM = pl.BlockSpec(memory_space=pltpu.VMEM)
+CHUNK = 4
 ANY = pl.BlockSpec(memory_space=pl.ANY)
 
 
@@ -217,15 +218,16 @@
             acc[at] = value
 
     acc[...] = jnp.zeros_like(acc)
-    kept, late = coefficients(0), None
-    for g in range(groups):
-        ahead = coefficients(g + 1) if g + 1 < groups else None
-        ats = [dest_ref[g * group + i] for i in range(group)]
-        terms = contributions(g, kept, ats)
-        if late is not None:
-            accumulate(*late)
-        kept, late = ahead, (terms, ats)
-    accumulate(*late)
+    chunks = [range(first, min(first + CHUNK, groups)) for first in range(0, groups, CHUNK)]
+    ahead = [coefficients(g) for g in chunks[0]]
+    for c, chunk in enumerate(chunks):
+        kept = ahead
+        if c + 1 < len(chunks):
+            ahead = [coefficients(g) for g in chunks[c + 1]]
+        ats = [[dest_ref[g * group + i] for i in range(group)] for g in chunk]
+        terms = [contributions(g, k, at) for g, k, at in zip(chunk, kept, ats)]
+        for term, at in zip(terms, ats):
+            accumulate(term, at)
     put_returns(acc[...].reshape(slots * nvec, leaf), x_ref, src_ref, out_ref)
 
 

time: 33.7 us -> 32.5 us (0.964)
  Pallas kernels: 5.67 us -> 4.47 us
    pallas_call x1, Pallas kernels: 4.47 us -> 3.27 us  [body(): pl.pallas_call(far_kernel, out_shape=(jax.ShapeDtypeStruct((peers, rows,...]
where the time goes in v18:
time: 32.5 us; the launch traced here: 32.2 us
  blocking collectives  26.9 us (83%)
  Pallas kernels  4.47 us (14%)
  local copies, waits for them, and re-layouts  0.78 us (2%)
    all_to_all x1, blocking collectives, body(): lax.all_to_all(message, 'clus', split_axis=0, concat_axis=0, tiled=True)  15.9 us
    all_to_all x1, blocking collectives, body(): lax.all_to_all(returns, 'clus', split_axis=0, concat_axis=0, tiled=True)  11.1 us
    pallas_call x1, Pallas kernels, body(): pl.pallas_call(far_kernel, out_shape=(jax.ShapeDtypeStruct((peers, rows,...  3.27 us
    pallas_call x1, Pallas kernels, body(): pl.pallas_call(sum_kernel, out_shape=jax.ShapeDtypeStruct((clusters, nvec...  0.82 us
    unnamed x16, local copies, waits for them, and re-layouts  0.78 us

profile of v18, /device:TPU:0, one launch (start us, length us, event | category | flops | bytes accessed | tf_op | source)
XLA Modules:
  0.0 32.2 jit_solution(15452563031950749125)
XLA Ops:
  0.0 0.0 copy-start.3
  0.0 0.0 copy-start.7
  0.0 0.0 copy-start.6
  0.0 0.7 %copy-done.3 = bf16[8,8,256]{2,1,0:T(8,128)(2,1)S(1)} copy-done((bf16[8,8,256]{2,1,0:T(8,128)(2,1)S(1)}, bf16[8,8,256]{2,1,0:T(8,128)(2,1)}, u32[]{:S(2)}) %copy-start.3) | copy-done | bytes 32792
  0.8 0.0 copy-done.7
  0.8 0.0 copy-done.6
  0.8 0.0 copy-start
  0.8 0.0 copy-start.1
  0.8 0.0 copy-start.2
  0.8 0.0 copy-start.4
  0.8 0.0 copy-start.5
  0.8 0.4 %pack.1 = bf16[16,40,128]{2,1,0:T(8,128)(2,1)S(1)} custom-call(s32[2,16]{1,0:T(2,128)S(1)} %bitcast.6, s32[2,16]{1,0:T(2,128)S(1)} %bitcast.7, bf16[8,8,256]{2,1,0:T(8,128)(2,1)S(1)} %copy-done.3, f32[8,128]{1,0:T(8,128)S(1)} %pattern.1.pattern_ref), custom_call_target="tpu_custom_call" | custom-call | flops 10000000000 | bytes 163840 | tf_op jit(solution)/shard_map/pack/pallas_call | solution.py:304
  1.2 15.9 %all_to_all.10.x_ref = bf16[16,40,128]{2,1,0:T(8,128)(2,1)S(1)} all-to-all(bf16[16,40,128]{2,1,0:T(8,128)(2,1)S(1)} %pack.1), channel_id=1, replica_groups=mesh['groups'=2,'clus'=16] {'clus'}, dimensions={0} | all-to-all | bytes 327680 | tf_op jit(solution)/shard_map/all_to_all | solution.py:313
  17.1 0.0 copy-done
  17.1 0.0 copy-done.1
  17.1 0.0 copy-done.2
  17.1 0.0 copy-done.4
  17.1 0.0 copy-done.5
  17.1 3.3 %far.1 = (bf16[16,40,128]{2,1,0:T(8,128)(2,1)S(1)}, f32[64,256]{1,0:T(8,128)S(1)}, bf16[64,256]{1,0:T(8,128)(2,1)S(1)}) custom-call(s32[256]{0:T(256)S(1)} %copy-done.4, s32[256]{0:T(256)S(1)} %copy-done.5, bf16[16,40,128]{2,1,0:T(8,128)(2,1)S(1)} %all_to_all.10.x_ref, bf16[256,32,256]{2,1,0:T(8,128)(2,1)S(1)} %copy-done.1, ...), custom_call_target="tpu_custom_call" | custom-call | flops 536870912 | bytes 8388608 | tf_op jit(solution)/shard_map/far/pallas_call | solution.py:314
  20.4 11.1 %all_to_all.11.back_ref = bf16[16,40,128]{2,1,0:T(8,128)(2,1)S(1)} all-to-all(bf16[16,40,128]{2,1,0:T(8,128)(2,1)S(1)} %get-tuple-element.8), channel_id=1, replica_groups=mesh['groups'=2,'clus'=16] {'clus'}, dimensions={0} | all-to-all | bytes 327680 | tf_op jit(solution)/shard_map/all_to_all | solution.py:336
  31.4 0.8 %sum.1 = f32[8,8,256]{2,1,0:T(8,128)} custom-call(bf16[16,40,128]{2,1,0:T(8,128)(2,1)S(1)} %all_to_all.11.back_ref, f32[64,256]{1,0:T(8,128)S(1)} %get-tuple-element.9.near_out_ref, bf16[64,256]{1,0:T(8,128)(2,1)S(1)} %get-tuple-element.10.place_ref, bf16[8,3,256,256]{3,2,1,0:T(8,128)(2,1)S(1)} %copy-done), custom_call_target="tpu_custom_call" | custom-call | flops 8388608 | bytes 131072 | tf_op jit(solution)/shard_map/sum/pallas_call | solution.py:337
  (1 shorter events, 0.0 us)
Async XLA Ops:
  0.0 0.8 %copy-start.3 = (bf16[8,8,256]{2,1,0:T(8,128)(2,1)S(1)}, bf16[8,8,256]{2,1,0:T(8,128)(2,1)}, u32[]{:S(2)}) copy-start(bf16[8,8,256]{2,1,0:T(8,128)(2,1)} %src_ref.3) | copy-start | bytes 98308
  0.0 0.8 %copy-start.7 = (s32[1,16,2]{1,2,0:T(2,128)S(1)}, s32[1,16,2]{1,2,0:T(2,128)}, u32[]{:S(2)}) copy-start(s32[1,16,2]{1,2,0:T(2,128)} %param.14) | copy-start | bytes 388
  0.0 0.8 %copy-start.6 = (s32[1,16,2]{1,2,0:T(2,128)S(1)}, s32[1,16,2]{1,2,0:T(2,128)}, u32[]{:S(2)}) copy-start(s32[1,16,2]{1,2,0:T(2,128)} %param.12) | copy-start | bytes 388
  0.8 16.3 %copy-start = (bf16[8,3,256,256]{3,2,1,0:T(8,128)(2,1)S(1)}, bf16[8,3,256,256]{3,2,1,0:T(8,128)(2,1)}, u32[]{:S(2)}) copy-start(bf16[8,3,256,256]{3,2,1,0:T(8,128)(2,1)} %near_ref.3) | copy-start | bytes 9437188
  0.8 16.3 %copy-start.1 = (bf16[256,32,256]{2,1,0:T(8,128)(2,1)S(1)}, bf16[256,32,256]{2,1,0:T(8,128)(2,1)}, u32[]{:S(2)}) copy-start(bf16[256,32,256]{2,1,0:T(8,128)(2,1)} %u_ref.1) | copy-start | bytes 12582916
  0.8 16.3 %copy-start.2 = (bf16[256,32,256]{2,1,0:T(8,128)(2,1)S(1)}, bf16[256,32,256]{2,1,0:T(8,128)(2,1)}, u32[]{:S(2)}) copy-start(bf16[256,32,256]{2,1,0:T(8,128)(2,1)} %v_ref.1) | copy-start | bytes 12582916
  0.8 16.3 %copy-start.4 = (s32[256]{0:T(256)S(1)}, s32[256]{0:T(256)}, u32[]{:S(2)}) copy-start(s32[256]{0:T(256)} %slots_any.1) | copy-start | bytes 3076
  0.8 16.3 %copy-start.5 = (s32[256]{0:T(256)S(1)}, s32[256]{0:T(256)}, u32[]{:S(2)}) copy-start(s32[256]{0:T(256)} %dests_any.1) | copy-start | bytes 3076

commit v19 on v18

--- a/solution.py
+++ b/solution.py
@@ -6,7 +6,7 @@
 from jax.sharding import PartitionSpec as P
 
 VMEM = pl.BlockSpec(memory_space=pltpu.VMEM)
-CHUNK = 4
+CHUNK = 8
 ANY = pl.BlockSpec(memory_space=pl.ANY)
 
 

time: 32.5 us -> 32.4 us (level)
  no operation moved by 1% of the time
where the time goes in v19:
time: 32.4 us; the launch traced here: 32.2 us
  blocking collectives  26.9 us (83%)
  Pallas kernels  4.45 us (14%)
  local copies, waits for them, and re-layouts  0.78 us (2%)
    all_to_all x1, blocking collectives, body(): lax.all_to_all(message, 'clus', split_axis=0, concat_axis=0, tiled=True)  15.9 us
    all_to_all x1, blocking collectives, body(): lax.all_to_all(returns, 'clus', split_axis=0, concat_axis=0, tiled=True)  11.1 us
    pallas_call x1, Pallas kernels, body(): pl.pallas_call(far_kernel, out_shape=(jax.ShapeDtypeStruct((peers, rows,...  3.25 us
    pallas_call x1, Pallas kernels, body(): pl.pallas_call(sum_kernel, out_shape=jax.ShapeDtypeStruct((clusters, nvec...  0.82 us
    unnamed x16, local copies, waits for them, and re-layouts  0.78 us

profile of v19, /device:TPU:0, one launch (start us, length us, event | category | flops | bytes accessed | tf_op | source)
XLA Modules:
  0.0 32.2 jit_solution(16186234300578390266)
XLA Ops:
  0.0 0.0 copy-start.3
  0.0 0.0 copy-start.7
  0.0 0.0 copy-start.6
  0.0 0.7 %copy-done.3 = bf16[8,8,256]{2,1,0:T(8,128)(2,1)S(1)} copy-done((bf16[8,8,256]{2,1,0:T(8,128)(2,1)S(1)}, bf16[8,8,256]{2,1,0:T(8,128)(2,1)}, u32[]{:S(2)}) %copy-start.3) | copy-done | bytes 32792
  0.8 0.0 copy-done.7
  0.8 0.0 copy-done.6
  0.8 0.0 copy-start
  0.8 0.0 copy-start.1
  0.8 0.0 copy-start.2
  0.8 0.0 copy-start.4
  0.8 0.0 copy-start.5
  0.8 0.4 %pack.1 = bf16[16,40,128]{2,1,0:T(8,128)(2,1)S(1)} custom-call(s32[2,16]{1,0:T(2,128)S(1)} %bitcast.6, s32[2,16]{1,0:T(2,128)S(1)} %bitcast.7, bf16[8,8,256]{2,1,0:T(8,128)(2,1)S(1)} %copy-done.3, f32[8,128]{1,0:T(8,128)S(1)} %pattern.1.pattern_ref), custom_call_target="tpu_custom_call" | custom-call | flops 10000000000 | bytes 163840 | tf_op jit(solution)/shard_map/pack/pallas_call | solution.py:304
  1.2 15.9 %all_to_all.10.x_ref = bf16[16,40,128]{2,1,0:T(8,128)(2,1)S(1)} all-to-all(bf16[16,40,128]{2,1,0:T(8,128)(2,1)S(1)} %pack.1), channel_id=1, replica_groups=mesh['groups'=2,'clus'=16] {'clus'}, dimensions={0} | all-to-all | bytes 327680 | tf_op jit(solution)/shard_map/all_to_all | solution.py:313
  17.1 0.0 copy-done
  17.1 0.0 copy-done.1
  17.1 0.0 copy-done.2
  17.1 0.0 copy-done.4
  17.1 0.0 copy-done.5
  17.1 3.2 %far.1 = (bf16[16,40,128]{2,1,0:T(8,128)(2,1)S(1)}, f32[64,256]{1,0:T(8,128)S(1)}, bf16[64,256]{1,0:T(8,128)(2,1)S(1)}) custom-call(s32[256]{0:T(256)S(1)} %copy-done.4, s32[256]{0:T(256)S(1)} %copy-done.5, bf16[16,40,128]{2,1,0:T(8,128)(2,1)S(1)} %all_to_all.10.x_ref, bf16[256,32,256]{2,1,0:T(8,128)(2,1)S(1)} %copy-done.1, ...), custom_call_target="tpu_custom_call" | custom-call | flops 536870912 | bytes 8388608 | tf_op jit(solution)/shard_map/far/pallas_call | solution.py:314
  20.4 11.1 %all_to_all.11.back_ref = bf16[16,40,128]{2,1,0:T(8,128)(2,1)S(1)} all-to-all(bf16[16,40,128]{2,1,0:T(8,128)(2,1)S(1)} %get-tuple-element.8), channel_id=1, replica_groups=mesh['groups'=2,'clus'=16] {'clus'}, dimensions={0} | all-to-all | bytes 327680 | tf_op jit(solution)/shard_map/all_to_all | solution.py:336
  31.4 0.8 %sum.1 = f32[8,8,256]{2,1,0:T(8,128)} custom-call(bf16[16,40,128]{2,1,0:T(8,128)(2,1)S(1)} %all_to_all.11.back_ref, f32[64,256]{1,0:T(8,128)S(1)} %get-tuple-element.9.near_out_ref, bf16[64,256]{1,0:T(8,128)(2,1)S(1)} %get-tuple-element.10.place_ref, bf16[8,3,256,256]{3,2,1,0:T(8,128)(2,1)S(1)} %copy-done), custom_call_target="tpu_custom_call" | custom-call | flops 8388608 | bytes 131072 | tf_op jit(solution)/shard_map/sum/pallas_call | solution.py:337
  (1 shorter events, 0.0 us)
Async XLA Ops:
  0.0 0.8 %copy-start.3 = (bf16[8,8,256]{2,1,0:T(8,128)(2,1)S(1)}, bf16[8,8,256]{2,1,0:T(8,128)(2,1)}, u32[]{:S(2)}) copy-start(bf16[8,8,256]{2,1,0:T(8,128)(2,1)} %src_ref.3) | copy-start | bytes 98308
  0.0 0.8 %copy-start.7 = (s32[1,16,2]{1,2,0:T(2,128)S(1)}, s32[1,16,2]{1,2,0:T(2,128)}, u32[]{:S(2)}) copy-start(s32[1,16,2]{1,2,0:T(2,128)} %param.14) | copy-start | bytes 388
  0.0 0.8 %copy-start.6 = (s32[1,16,2]{1,2,0:T(2,128)S(1)}, s32[1,16,2]{1,2,0:T(2,128)}, u32[]{:S(2)}) copy-start(s32[1,16,2]{1,2,0:T(2,128)} %param.12) | copy-start | bytes 388
  0.8 16.3 %copy-start = (bf16[8,3,256,256]{3,2,1,0:T(8,128)(2,1)S(1)}, bf16[8,3,256,256]{3,2,1,0:T(8,128)(2,1)}, u32[]{:S(2)}) copy-start(bf16[8,3,256,256]{3,2,1,0:T(8,128)(2,1)} %near_ref.3) | copy-start | bytes 9437188
  0.8 16.3 %copy-start.1 = (bf16[256,32,256]{2,1,0:T(8,128)(2,1)S(1)}, bf16[256,32,256]{2,1,0:T(8,128)(2,1)}, u32[]{:S(2)}) copy-start(bf16[256,32,256]{2,1,0:T(8,128)(2,1)} %u_ref.1) | copy-start | bytes 12582916
  0.8 16.3 %copy-start.2 = (bf16[256,32,256]{2,1,0:T(8,128)(2,1)S(1)}, bf16[256,32,256]{2,1,0:T(8,128)(2,1)}, u32[]{:S(2)}) copy-start(bf16[256,32,256]{2,1,0:T(8,128)(2,1)} %v_ref.1) | copy-start | bytes 12582916
  0.8 16.3 %copy-start.4 = (s32[256]{0:T(256)S(1)}, s32[256]{0:T(256)}, u32[]{:S(2)}) copy-start(s32[256]{0:T(256)} %slots_any.1) | copy-start | bytes 3076
  0.8 16.3 %copy-start.5 = (s32[256]{0:T(256)S(1)}, s32[256]{0:T(256)}, u32[]{:S(2)}) copy-start(s32[256]{0:T(256)} %dests_any.1) | copy-start | bytes 3076

commit v20 on v18

--- a/solution.py
+++ b/solution.py
@@ -93,12 +93,15 @@
         for x in (before, after)
     ]
     sources = [before] + [src_ref[s] for s in range(clusters)] + [after]
-    for s in range(clusters):
+
+    def product(s):
         near_out[s * nvec : (s + 1) * nvec] = jnp.dot(
             jnp.concatenate(sources[s : s + 3], axis=1),
             near_ref[s].reshape(3 * leaf, leaf),
             preferred_element_type=jnp.float32,
         )
+
+    return product
 
 
 def placement(x_ref, pattern_ref, place, place_out):
@@ -191,7 +194,8 @@
     placement(x_ref, pattern_ref, place, place_out)
     for copy in copies:
         copy.wait()
-    near_product(src_ref, near_ref, x_ref, near_out)
+    near = near_product(src_ref, near_ref, x_ref, near_out)
+    clusters = src_ref.shape[0]
     for g in range(groups):
         rows = [xf[slot_ref[g * group + i]] for i in range(group)]
         picked[g] = jnp.concatenate(rows, axis=0).astype(jnp.bfloat16)
@@ -226,6 +230,8 @@
             ahead = [coefficients(g) for g in chunks[c + 1]]
         ats = [[dest_ref[g * group + i] for i in range(group)] for g in chunk]
         terms = [contributions(g, k, at) for g, k, at in zip(chunk, kept, ats)]
+        for s in range(c * clusters // len(chunks), (c + 1) * clusters // len(chunks)):
+            near(s)
         for term, at in zip(terms, ats):
             accumulate(term, at)
     put_returns(acc[...].reshape(slots * nvec, leaf), x_ref, src_ref, out_ref)

time: 32.5 us -> 32.4 us (level)
  no operation moved by 1% of the time
where the time goes in v20:
time: 32.4 us; the launch traced here: 32.1 us
  blocking collectives  26.9 us (83%)
  Pallas kernels  4.37 us (13%)
  local copies, waits for them, and re-layouts  0.78 us (2%)
    all_to_all x1, blocking collectives, body(): lax.all_to_all(message, 'clus', split_axis=0, concat_axis=0, tiled=True)  15.9 us
    all_to_all x1, blocking collectives, body(): lax.all_to_all(returns, 'clus', split_axis=0, concat_axis=0, tiled=True)  11.1 us
    pallas_call x1, Pallas kernels, body(): pl.pallas_call(far_kernel, out_shape=(jax.ShapeDtypeStruct((peers, rows,...  3.17 us
    pallas_call x1, Pallas kernels, body(): pl.pallas_call(sum_kernel, out_shape=jax.ShapeDtypeStruct((clusters, nvec...  0.82 us
    unnamed x16, local copies, waits for them, and re-layouts  0.78 us

profile of v20, /device:TPU:0, one launch (start us, length us, event | category | flops | bytes accessed | tf_op | source)
XLA Modules:
  0.0 32.1 jit_solution(11347698792187533668)
XLA Ops:
  0.0 0.0 copy-start.3
  0.0 0.0 copy-start.7
  0.0 0.0 copy-start.6
  0.0 0.7 %copy-done.3 = bf16[8,8,256]{2,1,0:T(8,128)(2,1)S(1)} copy-done((bf16[8,8,256]{2,1,0:T(8,128)(2,1)S(1)}, bf16[8,8,256]{2,1,0:T(8,128)(2,1)}, u32[]{:S(2)}) %copy-start.3) | copy-done | bytes 32792
  0.8 0.0 copy-done.7
  0.8 0.0 copy-done.6
  0.8 0.0 copy-start
  0.8 0.0 copy-start.1
  0.8 0.0 copy-start.2
  0.8 0.0 copy-start.4
  0.8 0.0 copy-start.5
  0.8 0.4 %pack.1 = bf16[16,40,128]{2,1,0:T(8,128)(2,1)S(1)} custom-call(s32[2,16]{1,0:T(2,128)S(1)} %bitcast.6, s32[2,16]{1,0:T(2,128)S(1)} %bitcast.7, bf16[8,8,256]{2,1,0:T(8,128)(2,1)S(1)} %copy-done.3, f32[8,128]{1,0:T(8,128)S(1)} %pattern.1.pattern_ref), custom_call_target="tpu_custom_call" | custom-call | flops 10000000000 | bytes 163840 | tf_op jit(solution)/shard_map/pack/pallas_call | solution.py:310
  1.2 15.9 %all_to_all.10.x_ref = bf16[16,40,128]{2,1,0:T(8,128)(2,1)S(1)} all-to-all(bf16[16,40,128]{2,1,0:T(8,128)(2,1)S(1)} %pack.1), channel_id=1, replica_groups=mesh['groups'=2,'clus'=16] {'clus'}, dimensions={0} | all-to-all | bytes 327680 | tf_op jit(solution)/shard_map/all_to_all | solution.py:319
  17.1 0.0 copy-done
  17.1 0.0 copy-done.1
  17.1 0.0 copy-done.2
  17.1 0.0 copy-done.4
  17.1 0.0 copy-done.5
  17.1 3.2 %far.1 = (bf16[16,40,128]{2,1,0:T(8,128)(2,1)S(1)}, f32[64,256]{1,0:T(8,128)S(1)}, bf16[64,256]{1,0:T(8,128)(2,1)S(1)}) custom-call(s32[256]{0:T(256)S(1)} %copy-done.4, s32[256]{0:T(256)S(1)} %copy-done.5, bf16[16,40,128]{2,1,0:T(8,128)(2,1)S(1)} %all_to_all.10.x_ref, bf16[256,32,256]{2,1,0:T(8,128)(2,1)S(1)} %copy-done.1, ...), custom_call_target="tpu_custom_call" | custom-call | flops 536870912 | bytes 8388608 | tf_op jit(solution)/shard_map/far/pallas_call | solution.py:320
  20.3 11.1 %all_to_all.11.back_ref = bf16[16,40,128]{2,1,0:T(8,128)(2,1)S(1)} all-to-all(bf16[16,40,128]{2,1,0:T(8,128)(2,1)S(1)} %get-tuple-element.8), channel_id=1, replica_groups=mesh['groups'=2,'clus'=16] {'clus'}, dimensions={0} | all-to-all | bytes 327680 | tf_op jit(solution)/shard_map/all_to_all | solution.py:342
  31.3 0.8 %sum.1 = f32[8,8,256]{2,1,0:T(8,128)} custom-call(bf16[16,40,128]{2,1,0:T(8,128)(2,1)S(1)} %all_to_all.11.back_ref, f32[64,256]{1,0:T(8,128)S(1)} %get-tuple-element.9.near_out_ref, bf16[64,256]{1,0:T(8,128)(2,1)S(1)} %get-tuple-element.10.place_ref, bf16[8,3,256,256]{3,2,1,0:T(8,128)(2,1)S(1)} %copy-done), custom_call_target="tpu_custom_call" | custom-call | flops 8388608 | bytes 131072 | tf_op jit(solution)/shard_map/sum/pallas_call | solution.py:343
  (1 shorter events, 0.0 us)
Async XLA Ops:
  0.0 0.8 %copy-start.3 = (bf16[8,8,256]{2,1,0:T(8,128)(2,1)S(1)}, bf16[8,8,256]{2,1,0:T(8,128)(2,1)}, u32[]{:S(2)}) copy-start(bf16[8,8,256]{2,1,0:T(8,128)(2,1)} %src_ref.3) | copy-start | bytes 98308
  0.0 0.8 %copy-start.7 = (s32[1,16,2]{1,2,0:T(2,128)S(1)}, s32[1,16,2]{1,2,0:T(2,128)}, u32[]{:S(2)}) copy-start(s32[1,16,2]{1,2,0:T(2,128)} %param.14) | copy-start | bytes 388
  0.0 0.8 %copy-start.6 = (s32[1,16,2]{1,2,0:T(2,128)S(1)}, s32[1,16,2]{1,2,0:T(2,128)}, u32[]{:S(2)}) copy-start(s32[1,16,2]{1,2,0:T(2,128)} %param.12) | copy-start | bytes 388
  0.8 16.3 %copy-start = (bf16[8,3,256,256]{3,2,1,0:T(8,128)(2,1)S(1)}, bf16[8,3,256,256]{3,2,1,0:T(8,128)(2,1)}, u32[]{:S(2)}) copy-start(bf16[8,3,256,256]{3,2,1,0:T(8,128)(2,1)} %near_ref.3) | copy-start | bytes 9437188
  0.8 16.3 %copy-start.1 = (bf16[256,32,256]{2,1,0:T(8,128)(2,1)S(1)}, bf16[256,32,256]{2,1,0:T(8,128)(2,1)}, u32[]{:S(2)}) copy-start(bf16[256,32,256]{2,1,0:T(8,128)(2,1)} %u_ref.1) | copy-start | bytes 12582916
  0.8 16.3 %copy-start.2 = (bf16[256,32,256]{2,1,0:T(8,128)(2,1)S(1)}, bf16[256,32,256]{2,1,0:T(8,128)(2,1)}, u32[]{:S(2)}) copy-start(bf16[256,32,256]{2,1,0:T(8,128)(2,1)} %v_ref.1) | copy-start | bytes 12582916
  0.8 16.3 %copy-start.4 = (s32[256]{0:T(256)S(1)}, s32[256]{0:T(256)}, u32[]{:S(2)}) copy-start(s32[256]{0:T(256)} %slots_any.1) | copy-start | bytes 3076
  0.8 16.3 %copy-start.5 = (s32[256]{0:T(256)S(1)}, s32[256]{0:T(256)}, u32[]{:S(2)}) copy-start(s32[256]{0:T(256)} %dests_any.1) | copy-start | bytes 3076

commit v21 on v20

--- a/solution.py
+++ b/solution.py
@@ -182,7 +182,7 @@
     place,
     xf,
     picked,
-    acc,
+    *accs,
 ):
     peers = x_ref.shape[0]
     slots, nvec, leaf = xf.shape
@@ -216,12 +216,13 @@
             preferred_element_type=jnp.float32,
         )
 
-    def accumulate(terms, ats):
+    def accumulate(acc, terms, ats):
         sums = [acc[at] + terms[i * nvec : (i + 1) * nvec] for i, at in enumerate(ats)]
         for at, value in zip(ats, sums):
             acc[at] = value
 
-    acc[...] = jnp.zeros_like(acc)
+    for acc in accs:
+        acc[...] = jnp.zeros_like(acc)
     chunks = [range(first, min(first + CHUNK, groups)) for first in range(0, groups, CHUNK)]
     ahead = [coefficients(g) for g in chunks[0]]
     for c, chunk in enumerate(chunks):
@@ -232,9 +233,10 @@
         terms = [contributions(g, k, at) for g, k, at in zip(chunk, kept, ats)]
         for s in range(c * clusters // len(chunks), (c + 1) * clusters // len(chunks)):
             near(s)
-        for term, at in zip(terms, ats):
-            accumulate(term, at)
-    put_returns(acc[...].reshape(slots * nvec, leaf), x_ref, src_ref, out_ref)
+        for g, term, at in zip(chunk, terms, ats):
+            accumulate(accs[g % len(accs)], term, at)
+    total = accs[0][...] + accs[1][...]
+    put_returns(total.reshape(slots * nvec, leaf), x_ref, src_ref, out_ref)
 
 
 def sum_kernel(back_ref, near_out_ref, place_ref, near_ref, out_ref):
@@ -334,6 +336,7 @@
             pltpu.VMEM((slots, nvec, leaf), jnp.float32),
             pltpu.VMEM((blocks * rank // leaf, leaf // rank * nvec, leaf), jnp.bfloat16),
             pltpu.VMEM((slots, nvec, leaf), jnp.float32),
+            pltpu.VMEM((slots, nvec, leaf), jnp.float32),
         ],
         compiler_params=pltpu.CompilerParams(vmem_limit_bytes=16 * 2**20),
         cost_estimate=cost(4 * blocks * 8 * nvec * leaf * rank, 4 * blocks * rank * leaf),

time: 32.4 us -> 32.4 us (level)
  no operation moved by 1% of the time
where the time goes in v21:
time: 32.4 us; the launch traced here: 32.2 us
  blocking collectives  26.9 us (83%)
  Pallas kernels  4.41 us (14%)
  local copies, waits for them, and re-layouts  0.78 us (2%)
    all_to_all x1, blocking collectives, body(): lax.all_to_all(message, 'clus', split_axis=0, concat_axis=0, tiled=True)  15.9 us
    all_to_all x1, blocking collectives, body(): lax.all_to_all(returns, 'clus', split_axis=0, concat_axis=0, tiled=True)  11.1 us
    pallas_call x1, Pallas kernels, body(): pl.pallas_call(far_kernel, out_shape=(jax.ShapeDtypeStruct((peers, rows,...  3.21 us
    pallas_call x1, Pallas kernels, body(): pl.pallas_call(sum_kernel, out_shape=jax.ShapeDtypeStruct((clusters, nvec...  0.82 us
    unnamed x16, local copies, waits for them, and re-layouts  0.78 us

profile of v21, /device:TPU:0, one launch (start us, length us, event | category | flops | bytes accessed | tf_op | source)
XLA Modules:
  0.0 32.2 jit_solution(2793622286157336723)
XLA Ops:
  0.0 0.0 copy-start.3
  0.0 0.0 copy-start.7
  0.0 0.0 copy-start.6
  0.0 0.7 %copy-done.3 = bf16[8,8,256]{2,1,0:T(8,128)(2,1)S(1)} copy-done((bf16[8,8,256]{2,1,0:T(8,128)(2,1)S(1)}, bf16[8,8,256]{2,1,0:T(8,128)(2,1)}, u32[]{:S(2)}) %copy-start.3) | copy-done | bytes 32792
  0.8 0.0 copy-done.7
  0.8 0.0 copy-done.6
  0.8 0.0 copy-start
  0.8 0.0 copy-start.1
  0.8 0.0 copy-start.2
  0.8 0.0 copy-start.4
  0.8 0.0 copy-start.5
  0.8 0.4 %pack.1 = bf16[16,40,128]{2,1,0:T(8,128)(2,1)S(1)} custom-call(s32[2,16]{1,0:T(2,128)S(1)} %bitcast.6, s32[2,16]{1,0:T(2,128)S(1)} %bitcast.7, bf16[8,8,256]{2,1,0:T(8,128)(2,1)S(1)} %copy-done.3, f32[8,128]{1,0:T(8,128)S(1)} %pattern.1.pattern_ref), custom_call_target="tpu_custom_call" | custom-call | flops 10000000000 | bytes 163840 | tf_op jit(solution)/shard_map/pack/pallas_call | solution.py:312
  1.2 15.9 %all_to_all.10.x_ref = bf16[16,40,128]{2,1,0:T(8,128)(2,1)S(1)} all-to-all(bf16[16,40,128]{2,1,0:T(8,128)(2,1)S(1)} %pack.1), channel_id=1, replica_groups=mesh['groups'=2,'clus'=16] {'clus'}, dimensions={0} | all-to-all | bytes 327680 | tf_op jit(solution)/shard_map/all_to_all | solution.py:321
  17.1 0.0 copy-done
  17.1 0.0 copy-done.1
  17.1 0.0 copy-done.2
  17.1 0.0 copy-done.4
  17.1 0.0 copy-done.5
  17.1 3.2 %far.1 = (bf16[16,40,128]{2,1,0:T(8,128)(2,1)S(1)}, f32[64,256]{1,0:T(8,128)S(1)}, bf16[64,256]{1,0:T(8,128)(2,1)S(1)}) custom-call(s32[256]{0:T(256)S(1)} %copy-done.4, s32[256]{0:T(256)S(1)} %copy-done.5, bf16[16,40,128]{2,1,0:T(8,128)(2,1)S(1)} %all_to_all.10.x_ref, bf16[256,32,256]{2,1,0:T(8,128)(2,1)S(1)} %copy-done.1, ...), custom_call_target="tpu_custom_call" | custom-call | flops 536870912 | bytes 8388608 | tf_op jit(solution)/shard_map/far/pallas_call | solution.py:322
  20.3 11.1 %all_to_all.11.back_ref = bf16[16,40,128]{2,1,0:T(8,128)(2,1)S(1)} all-to-all(bf16[16,40,128]{2,1,0:T(8,128)(2,1)S(1)} %get-tuple-element.8), channel_id=1, replica_groups=mesh['groups'=2,'clus'=16] {'clus'}, dimensions={0} | all-to-all | bytes 327680 | tf_op jit(solution)/shard_map/all_to_all | solution.py:345
  31.4 0.8 %sum.1 = f32[8,8,256]{2,1,0:T(8,128)} custom-call(bf16[16,40,128]{2,1,0:T(8,128)(2,1)S(1)} %all_to_all.11.back_ref, f32[64,256]{1,0:T(8,128)S(1)} %get-tuple-element.9.near_out_ref, bf16[64,256]{1,0:T(8,128)(2,1)S(1)} %get-tuple-element.10.place_ref, bf16[8,3,256,256]{3,2,1,0:T(8,128)(2,1)S(1)} %copy-done), custom_call_target="tpu_custom_call" | custom-call | flops 8388608 | bytes 131072 | tf_op jit(solution)/shard_map/sum/pallas_call | solution.py:346
  (1 shorter events, 0.0 us)
Async XLA Ops:
  0.0 0.8 %copy-start.3 = (bf16[8,8,256]{2,1,0:T(8,128)(2,1)S(1)}, bf16[8,8,256]{2,1,0:T(8,128)(2,1)}, u32[]{:S(2)}) copy-start(bf16[8,8,256]{2,1,0:T(8,128)(2,1)} %src_ref.3) | copy-start | bytes 98308
  0.0 0.8 %copy-start.7 = (s32[1,16,2]{1,2,0:T(2,128)S(1)}, s32[1,16,2]{1,2,0:T(2,128)}, u32[]{:S(2)}) copy-start(s32[1,16,2]{1,2,0:T(2,128)} %param.14) | copy-start | bytes 388
  0.0 0.8 %copy-start.6 = (s32[1,16,2]{1,2,0:T(2,128)S(1)}, s32[1,16,2]{1,2,0:T(2,128)}, u32[]{:S(2)}) copy-start(s32[1,16,2]{1,2,0:T(2,128)} %param.12) | copy-start | bytes 388
  0.8 16.3 %copy-start = (bf16[8,3,256,256]{3,2,1,0:T(8,128)(2,1)S(1)}, bf16[8,3,256,256]{3,2,1,0:T(8,128)(2,1)}, u32[]{:S(2)}) copy-start(bf16[8,3,256,256]{3,2,1,0:T(8,128)(2,1)} %near_ref.3) | copy-start | bytes 9437188
  0.8 16.3 %copy-start.1 = (bf16[256,32,256]{2,1,0:T(8,128)(2,1)S(1)}, bf16[256,32,256]{2,1,0:T(8,128)(2,1)}, u32[]{:S(2)}) copy-start(bf16[256,32,256]{2,1,0:T(8,128)(2,1)} %u_ref.1) | copy-start | bytes 12582916
  0.8 16.3 %copy-start.2 = (bf16[256,32,256]{2,1,0:T(8,128)(2,1)S(1)}, bf16[256,32,256]{2,1,0:T(8,128)(2,1)}, u32[]{:S(2)}) copy-start(bf16[256,32,256]{2,1,0:T(8,128)(2,1)} %v_ref.1) | copy-start | bytes 12582916
  0.8 16.3 %copy-start.4 = (s32[256]{0:T(256)S(1)}, s32[256]{0:T(256)}, u32[]{:S(2)}) copy-start(s32[256]{0:T(256)} %slots_any.1) | copy-start | bytes 3076
  0.8 16.3 %copy-start.5 = (s32[256]{0:T(256)S(1)}, s32[256]{0:T(256)}, u32[]{:S(2)}) copy-start(s32[256]{0:T(256)} %dests_any.1) | copy-start | bytes 3076

commit v22 on v20

--- a/solution.py
+++ b/solution.py
@@ -191,7 +191,6 @@
     groups = blocks // group
     copies = load_slots(slots_any, dests_any, slot_ref, dest_ref, sems)
     widen_sources(x_ref, xf)
-    placement(x_ref, pattern_ref, place, place_out)
     for copy in copies:
         copy.wait()
     near = near_product(src_ref, near_ref, x_ref, near_out)
@@ -232,6 +231,8 @@
         terms = [contributions(g, k, at) for g, k, at in zip(chunk, kept, ats)]
         for s in range(c * clusters // len(chunks), (c + 1) * clusters // len(chunks)):
             near(s)
+        if c == 0:
+            placement(x_ref, pattern_ref, place, place_out)
         for term, at in zip(terms, ats):
             accumulate(term, at)
     put_returns(acc[...].reshape(slots * nvec, leaf), x_ref, src_ref, out_ref)

time: 32.4 us -> 32.3 us (level)
  no operation moved by 1% of the time
where the time goes in v22:
time: 32.3 us; the launch traced here: 32.1 us
  blocking collectives  26.9 us (83%)
  Pallas kernels  4.35 us (13%)
  local copies, waits for them, and re-layouts  0.78 us (2%)
    all_to_all x1, blocking collectives, body(): lax.all_to_all(message, 'clus', split_axis=0, concat_axis=0, tiled=True)  15.9 us
    all_to_all x1, blocking collectives, body(): lax.all_to_all(returns, 'clus', split_axis=0, concat_axis=0, tiled=True)  11.1 us
    pallas_call x1, Pallas kernels, body(): pl.pallas_call(far_kernel, out_shape=(jax.ShapeDtypeStruct((peers, rows,...  3.15 us
    pallas_call x1, Pallas kernels, body(): pl.pallas_call(sum_kernel, out_shape=jax.ShapeDtypeStruct((clusters, nvec...  0.82 us
    unnamed x16, local copies, waits for them, and re-layouts  0.78 us

profile of v22, /device:TPU:0, one launch (start us, length us, event | category | flops | bytes accessed | tf_op | source)
XLA Modules:
  0.0 32.1 jit_solution(7735021561942535285)
XLA Ops:
  0.0 0.0 copy-start.3
  0.0 0.0 copy-start.7
  0.0 0.0 copy-start.6
  0.0 0.7 %copy-done.3 = bf16[8,8,256]{2,1,0:T(8,128)(2,1)S(1)} copy-done((bf16[8,8,256]{2,1,0:T(8,128)(2,1)S(1)}, bf16[8,8,256]{2,1,0:T(8,128)(2,1)}, u32[]{:S(2)}) %copy-start.3) | copy-done | bytes 32792
  0.8 0.0 copy-done.7
  0.8 0.0 copy-done.6
  0.8 0.0 copy-start
  0.8 0.0 copy-start.1
  0.8 0.0 copy-start.2
  0.8 0.0 copy-start.4
  0.8 0.0 copy-start.5
  0.8 0.4 %pack.1 = bf16[16,40,128]{2,1,0:T(8,128)(2,1)S(1)} custom-call(s32[2,16]{1,0:T(2,128)S(1)} %bitcast.6, s32[2,16]{1,0:T(2,128)S(1)} %bitcast.7, bf16[8,8,256]{2,1,0:T(8,128)(2,1)S(1)} %copy-done.3, f32[8,128]{1,0:T(8,128)S(1)} %pattern.1.pattern_ref), custom_call_target="tpu_custom_call" | custom-call | flops 10000000000 | bytes 163840 | tf_op jit(solution)/shard_map/pack/pallas_call | solution.py:311
  1.2 15.9 %all_to_all.10.x_ref = bf16[16,40,128]{2,1,0:T(8,128)(2,1)S(1)} all-to-all(bf16[16,40,128]{2,1,0:T(8,128)(2,1)S(1)} %pack.1), channel_id=1, replica_groups=mesh['groups'=2,'clus'=16] {'clus'}, dimensions={0} | all-to-all | bytes 327680 | tf_op jit(solution)/shard_map/all_to_all | solution.py:320
  17.1 0.0 copy-done
  17.1 0.0 copy-done.1
  17.1 0.0 copy-done.2
  17.1 0.0 copy-done.4
  17.1 0.0 copy-done.5
  17.1 3.1 %far.1 = (bf16[16,40,128]{2,1,0:T(8,128)(2,1)S(1)}, f32[64,256]{1,0:T(8,128)S(1)}, bf16[64,256]{1,0:T(8,128)(2,1)S(1)}) custom-call(s32[256]{0:T(256)S(1)} %copy-done.4, s32[256]{0:T(256)S(1)} %copy-done.5, bf16[16,40,128]{2,1,0:T(8,128)(2,1)S(1)} %all_to_all.10.x_ref, bf16[256,32,256]{2,1,0:T(8,128)(2,1)S(1)} %copy-done.1, ...), custom_call_target="tpu_custom_call" | custom-call | flops 536870912 | bytes 8388608 | tf_op jit(solution)/shard_map/far/pallas_call | solution.py:321
  20.2 11.1 %all_to_all.11.back_ref = bf16[16,40,128]{2,1,0:T(8,128)(2,1)S(1)} all-to-all(bf16[16,40,128]{2,1,0:T(8,128)(2,1)S(1)} %get-tuple-element.8), channel_id=1, replica_groups=mesh['groups'=2,'clus'=16] {'clus'}, dimensions={0} | all-to-all | bytes 327680 | tf_op jit(solution)/shard_map/all_to_all | solution.py:343
  31.3 0.8 %sum.1 = f32[8,8,256]{2,1,0:T(8,128)} custom-call(bf16[16,40,128]{2,1,0:T(8,128)(2,1)S(1)} %all_to_all.11.back_ref, f32[64,256]{1,0:T(8,128)S(1)} %get-tuple-element.9.near_out_ref, bf16[64,256]{1,0:T(8,128)(2,1)S(1)} %get-tuple-element.10.place_ref, bf16[8,3,256,256]{3,2,1,0:T(8,128)(2,1)S(1)} %copy-done), custom_call_target="tpu_custom_call" | custom-call | flops 8388608 | bytes 131072 | tf_op jit(solution)/shard_map/sum/pallas_call | solution.py:344
  (1 shorter events, 0.0 us)
Async XLA Ops:
  0.0 0.8 %copy-start.3 = (bf16[8,8,256]{2,1,0:T(8,128)(2,1)S(1)}, bf16[8,8,256]{2,1,0:T(8,128)(2,1)}, u32[]{:S(2)}) copy-start(bf16[8,8,256]{2,1,0:T(8,128)(2,1)} %src_ref.3) | copy-start | bytes 98308
  0.0 0.8 %copy-start.7 = (s32[1,16,2]{1,2,0:T(2,128)S(1)}, s32[1,16,2]{1,2,0:T(2,128)}, u32[]{:S(2)}) copy-start(s32[1,16,2]{1,2,0:T(2,128)} %param.14) | copy-start | bytes 388
  0.0 0.8 %copy-start.6 = (s32[1,16,2]{1,2,0:T(2,128)S(1)}, s32[1,16,2]{1,2,0:T(2,128)}, u32[]{:S(2)}) copy-start(s32[1,16,2]{1,2,0:T(2,128)} %param.12) | copy-start | bytes 388
  0.8 16.3 %copy-start = (bf16[8,3,256,256]{3,2,1,0:T(8,128)(2,1)S(1)}, bf16[8,3,256,256]{3,2,1,0:T(8,128)(2,1)}, u32[]{:S(2)}) copy-start(bf16[8,3,256,256]{3,2,1,0:T(8,128)(2,1)} %near_ref.3) | copy-start | bytes 9437188
  0.8 16.3 %copy-start.1 = (bf16[256,32,256]{2,1,0:T(8,128)(2,1)S(1)}, bf16[256,32,256]{2,1,0:T(8,128)(2,1)}, u32[]{:S(2)}) copy-start(bf16[256,32,256]{2,1,0:T(8,128)(2,1)} %u_ref.1) | copy-start | bytes 12582916
  0.8 16.3 %copy-start.2 = (bf16[256,32,256]{2,1,0:T(8,128)(2,1)S(1)}, bf16[256,32,256]{2,1,0:T(8,128)(2,1)}, u32[]{:S(2)}) copy-start(bf16[256,32,256]{2,1,0:T(8,128)(2,1)} %v_ref.1) | copy-start | bytes 12582916
  0.8 16.3 %copy-start.4 = (s32[256]{0:T(256)S(1)}, s32[256]{0:T(256)}, u32[]{:S(2)}) copy-start(s32[256]{0:T(256)} %slots_any.1) | copy-start | bytes 3076
  0.8 16.3 %copy-start.5 = (s32[256]{0:T(256)S(1)}, s32[256]{0:T(256)}, u32[]{:S(2)}) copy-start(s32[256]{0:T(256)} %dests_any.1) | copy-start | bytes 3076

commit v23 on v20

--- a/solution.py
+++ b/solution.py
@@ -224,6 +224,7 @@
     acc[...] = jnp.zeros_like(acc)
     chunks = [range(first, min(first + CHUNK, groups)) for first in range(0, groups, CHUNK)]
     ahead = [coefficients(g) for g in chunks[0]]
+    late = []
     for c, chunk in enumerate(chunks):
         kept = ahead
         if c + 1 < len(chunks):
@@ -232,8 +233,11 @@
         terms = [contributions(g, k, at) for g, k, at in zip(chunk, kept, ats)]
         for s in range(c * clusters // len(chunks), (c + 1) * clusters // len(chunks)):
             near(s)
-        for term, at in zip(terms, ats):
+        for term, at in late:
             accumulate(term, at)
+        late = list(zip(terms, ats))
+    for term, at in late:
+        accumulate(term, at)
     put_returns(acc[...].reshape(slots * nvec, leaf), x_ref, src_ref, out_ref)
 
 

time: 32.4 us -> 32.4 us (level)
  no operation moved by 1% of the time
where the time goes in v23:
time: 32.4 us; the launch traced here: 32.2 us
  blocking collectives  26.9 us (83%)
  Pallas kernels  4.37 us (13%)
  local copies, waits for them, and re-layouts  0.78 us (2%)
    all_to_all x1, blocking collectives, body(): lax.all_to_all(message, 'clus', split_axis=0, concat_axis=0, tiled=True)  15.9 us
    all_to_all x1, blocking collectives, body(): lax.all_to_all(returns, 'clus', split_axis=0, concat_axis=0, tiled=True)  11.1 us
    pallas_call x1, Pallas kernels, body(): pl.pallas_call(far_kernel, out_shape=(jax.ShapeDtypeStruct((peers, rows,...  3.18 us
    pallas_call x1, Pallas kernels, body(): pl.pallas_call(sum_kernel, out_shape=jax.ShapeDtypeStruct((clusters, nvec...  0.82 us
    unnamed x16, local copies, waits for them, and re-layouts  0.78 us

profile of v23, /device:TPU:0, one launch (start us, length us, event | category | flops | bytes accessed | tf_op | source)
XLA Modules:
  0.0 32.2 jit_solution(11347698792187533668)
XLA Ops:
  0.0 0.0 copy-start.3
  0.0 0.0 copy-start.7
  0.0 0.0 copy-start.6
  0.0 0.7 %copy-done.3 = bf16[8,8,256]{2,1,0:T(8,128)(2,1)S(1)} copy-done((bf16[8,8,256]{2,1,0:T(8,128)(2,1)S(1)}, bf16[8,8,256]{2,1,0:T(8,128)(2,1)}, u32[]{:S(2)}) %copy-start.3) | copy-done | bytes 32792
  0.8 0.0 copy-done.7
  0.8 0.0 copy-done.6
  0.8 0.0 copy-start
  0.8 0.0 copy-start.1
  0.8 0.0 copy-start.2
  0.8 0.0 copy-start.4
  0.8 0.0 copy-start.5
  0.8 0.4 %pack.1 = bf16[16,40,128]{2,1,0:T(8,128)(2,1)S(1)} custom-call(s32[2,16]{1,0:T(2,128)S(1)} %bitcast.6, s32[2,16]{1,0:T(2,128)S(1)} %bitcast.7, bf16[8,8,256]{2,1,0:T(8,128)(2,1)S(1)} %copy-done.3, f32[8,128]{1,0:T(8,128)S(1)} %pattern.1.pattern_ref), custom_call_target="tpu_custom_call" | custom-call | flops 10000000000 | bytes 163840 | tf_op jit(solution)/shard_map/pack/pallas_call | solution.py:314
  1.2 15.9 %all_to_all.10.x_ref = bf16[16,40,128]{2,1,0:T(8,128)(2,1)S(1)} all-to-all(bf16[16,40,128]{2,1,0:T(8,128)(2,1)S(1)} %pack.1), channel_id=1, replica_groups=mesh['groups'=2,'clus'=16] {'clus'}, dimensions={0} | all-to-all | bytes 327680 | tf_op jit(solution)/shard_map/all_to_all | solution.py:323
  17.1 0.0 copy-done
  17.1 0.0 copy-done.1
  17.1 0.0 copy-done.2
  17.1 0.0 copy-done.4
  17.1 0.0 copy-done.5
  17.1 3.2 %far.1 = (bf16[16,40,128]{2,1,0:T(8,128)(2,1)S(1)}, f32[64,256]{1,0:T(8,128)S(1)}, bf16[64,256]{1,0:T(8,128)(2,1)S(1)}) custom-call(s32[256]{0:T(256)S(1)} %copy-done.4, s32[256]{0:T(256)S(1)} %copy-done.5, bf16[16,40,128]{2,1,0:T(8,128)(2,1)S(1)} %all_to_all.10.x_ref, bf16[256,32,256]{2,1,0:T(8,128)(2,1)S(1)} %copy-done.1, ...), custom_call_target="tpu_custom_call" | custom-call | flops 536870912 | bytes 8388608 | tf_op jit(solution)/shard_map/far/pallas_call | solution.py:324
  20.3 11.1 %all_to_all.11.back_ref = bf16[16,40,128]{2,1,0:T(8,128)(2,1)S(1)} all-to-all(bf16[16,40,128]{2,1,0:T(8,128)(2,1)S(1)} %get-tuple-element.8), channel_id=1, replica_groups=mesh['groups'=2,'clus'=16] {'clus'}, dimensions={0} | all-to-all | bytes 327680 | tf_op jit(solution)/shard_map/all_to_all | solution.py:346
  31.3 0.8 %sum.1 = f32[8,8,256]{2,1,0:T(8,128)} custom-call(bf16[16,40,128]{2,1,0:T(8,128)(2,1)S(1)} %all_to_all.11.back_ref, f32[64,256]{1,0:T(8,128)S(1)} %get-tuple-element.9.near_out_ref, bf16[64,256]{1,0:T(8,128)(2,1)S(1)} %get-tuple-element.10.place_ref, bf16[8,3,256,256]{3,2,1,0:T(8,128)(2,1)S(1)} %copy-done), custom_call_target="tpu_custom_call" | custom-call | flops 8388608 | bytes 131072 | tf_op jit(solution)/shard_map/sum/pallas_call | solution.py:347
  (1 shorter events, 0.0 us)
Async XLA Ops:
  0.0 0.8 %copy-start.3 = (bf16[8,8,256]{2,1,0:T(8,128)(2,1)S(1)}, bf16[8,8,256]{2,1,0:T(8,128)(2,1)}, u32[]{:S(2)}) copy-start(bf16[8,8,256]{2,1,0:T(8,128)(2,1)} %src_ref.3) | copy-start | bytes 98308
  0.0 0.8 %copy-start.7 = (s32[1,16,2]{1,2,0:T(2,128)S(1)}, s32[1,16,2]{1,2,0:T(2,128)}, u32[]{:S(2)}) copy-start(s32[1,16,2]{1,2,0:T(2,128)} %param.14) | copy-start | bytes 388
  0.0 0.8 %copy-start.6 = (s32[1,16,2]{1,2,0:T(2,128)S(1)}, s32[1,16,2]{1,2,0:T(2,128)}, u32[]{:S(2)}) copy-start(s32[1,16,2]{1,2,0:T(2,128)} %param.12) | copy-start | bytes 388
  0.8 16.3 %copy-start = (bf16[8,3,256,256]{3,2,1,0:T(8,128)(2,1)S(1)}, bf16[8,3,256,256]{3,2,1,0:T(8,128)(2,1)}, u32[]{:S(2)}) copy-start(bf16[8,3,256,256]{3,2,1,0:T(8,128)(2,1)} %near_ref.3) | copy-start | bytes 9437188
  0.8 16.3 %copy-start.1 = (bf16[256,32,256]{2,1,0:T(8,128)(2,1)S(1)}, bf16[256,32,256]{2,1,0:T(8,128)(2,1)}, u32[]{:S(2)}) copy-start(bf16[256,32,256]{2,1,0:T(8,128)(2,1)} %u_ref.1) | copy-start | bytes 12582916
  0.8 16.3 %copy-start.2 = (bf16[256,32,256]{2,1,0:T(8,128)(2,1)S(1)}, bf16[256,32,256]{2,1,0:T(8,128)(2,1)}, u32[]{:S(2)}) copy-start(bf16[256,32,256]{2,1,0:T(8,128)(2,1)} %v_ref.1) | copy-start | bytes 12582916
  0.8 16.3 %copy-start.4 = (s32[256]{0:T(256)S(1)}, s32[256]{0:T(256)}, u32[]{:S(2)}) copy-start(s32[256]{0:T(256)} %slots_any.1) | copy-start | bytes 3076
  0.8 16.3 %copy-start.5 = (s32[256]{0:T(256)S(1)}, s32[256]{0:T(256)}, u32[]{:S(2)}) copy-start(s32[256]{0:T(256)} %dests_any.1) | copy-start | bytes 3076

commit v24 on v20

--- a/solution.py
+++ b/solution.py
@@ -192,10 +192,13 @@
     copies = load_slots(slots_any, dests_any, slot_ref, dest_ref, sems)
     widen_sources(x_ref, xf)
     placement(x_ref, pattern_ref, place, place_out)
+    near = near_product(src_ref, near_ref, x_ref, near_out)
+    clusters = src_ref.shape[0]
+    early = clusters * 3 // 8
+    for s in range(early):
+        near(s)
     for copy in copies:
         copy.wait()
-    near = near_product(src_ref, near_ref, x_ref, near_out)
-    clusters = src_ref.shape[0]
     for g in range(groups):
         rows = [xf[slot_ref[g * group + i]] for i in range(group)]
         picked[g] = jnp.concatenate(rows, axis=0).astype(jnp.bfloat16)
@@ -230,7 +233,8 @@
             ahead = [coefficients(g) for g in chunks[c + 1]]
         ats = [[dest_ref[g * group + i] for i in range(group)] for g in chunk]
         terms = [contributions(g, k, at) for g, k, at in zip(chunk, kept, ats)]
-        for s in range(c * clusters // len(chunks), (c + 1) * clusters // len(chunks)):
+        share = [early + (clusters - early) * i // len(chunks) for i in (c, c + 1)]
+        for s in range(*share):
             near(s)
         for term, at in zip(terms, ats):
             accumulate(term, at)

time: 32.4 us -> 32.3 us (level)
  no operation moved by 1% of the time
where the time goes in v24:
time: 32.3 us; the launch traced here: 32.1 us
  blocking collectives  26.9 us (83%)
  Pallas kernels  4.3 us (13%)
  local copies, waits for them, and re-layouts  0.78 us (2%)
    all_to_all x1, blocking collectives, body(): lax.all_to_all(message, 'clus', split_axis=0, concat_axis=0, tiled=True)  15.9 us
    all_to_all x1, blocking collectives, body(): lax.all_to_all(returns, 'clus', split_axis=0, concat_axis=0, tiled=True)  11.1 us
    pallas_call x1, Pallas kernels, body(): pl.pallas_call(far_kernel, out_shape=(jax.ShapeDtypeStruct((peers, rows,...  3.1 us
    pallas_call x1, Pallas kernels, body(): pl.pallas_call(sum_kernel, out_shape=jax.ShapeDtypeStruct((clusters, nvec...  0.82 us
    unnamed x16, local copies, waits for them, and re-layouts  0.78 us

profile of v24, /device:TPU:0, one launch (start us, length us, event | category | flops | bytes accessed | tf_op | source)
XLA Modules:
  0.0 32.1 jit_solution(12156755301318243640)
XLA Ops:
  0.0 0.0 copy-start.3
  0.0 0.0 copy-start.7
  0.0 0.0 copy-start.6
  0.0 0.7 %copy-done.3 = bf16[8,8,256]{2,1,0:T(8,128)(2,1)S(1)} copy-done((bf16[8,8,256]{2,1,0:T(8,128)(2,1)S(1)}, bf16[8,8,256]{2,1,0:T(8,128)(2,1)}, u32[]{:S(2)}) %copy-start.3) | copy-done | bytes 32792
  0.8 0.0 copy-done.7
  0.8 0.0 copy-done.6
  0.8 0.0 copy-start
  0.8 0.0 copy-start.1
  0.8 0.0 copy-start.2
  0.8 0.0 copy-start.4
  0.8 0.0 copy-start.5
  0.8 0.4 %pack.1 = bf16[16,40,128]{2,1,0:T(8,128)(2,1)S(1)} custom-call(s32[2,16]{1,0:T(2,128)S(1)} %bitcast.6, s32[2,16]{1,0:T(2,128)S(1)} %bitcast.7, bf16[8,8,256]{2,1,0:T(8,128)(2,1)S(1)} %copy-done.3, f32[8,128]{1,0:T(8,128)S(1)} %pattern.1.pattern_ref), custom_call_target="tpu_custom_call" | custom-call | flops 10000000000 | bytes 163840 | tf_op jit(solution)/shard_map/pack/pallas_call | solution.py:314
  1.2 15.9 %all_to_all.10.x_ref = bf16[16,40,128]{2,1,0:T(8,128)(2,1)S(1)} all-to-all(bf16[16,40,128]{2,1,0:T(8,128)(2,1)S(1)} %pack.1), channel_id=1, replica_groups=mesh['groups'=2,'clus'=16] {'clus'}, dimensions={0} | all-to-all | bytes 327680 | tf_op jit(solution)/shard_map/all_to_all | solution.py:323
  17.1 0.0 copy-done
  17.1 0.0 copy-done.1
  17.1 0.0 copy-done.2
  17.1 0.0 copy-done.4
  17.1 0.0 copy-done.5
  17.1 3.1 %far.1 = (bf16[16,40,128]{2,1,0:T(8,128)(2,1)S(1)}, f32[64,256]{1,0:T(8,128)S(1)}, bf16[64,256]{1,0:T(8,128)(2,1)S(1)}) custom-call(s32[256]{0:T(256)S(1)} %copy-done.4, s32[256]{0:T(256)S(1)} %copy-done.5, bf16[16,40,128]{2,1,0:T(8,128)(2,1)S(1)} %all_to_all.10.x_ref, bf16[256,32,256]{2,1,0:T(8,128)(2,1)S(1)} %copy-done.1, ...), custom_call_target="tpu_custom_call" | custom-call | flops 536870912 | bytes 8388608 | tf_op jit(solution)/shard_map/far/pallas_call | solution.py:324
  20.2 11.1 %all_to_all.11.back_ref = bf16[16,40,128]{2,1,0:T(8,128)(2,1)S(1)} all-to-all(bf16[16,40,128]{2,1,0:T(8,128)(2,1)S(1)} %get-tuple-element.8), channel_id=1, replica_groups=mesh['groups'=2,'clus'=16] {'clus'}, dimensions={0} | all-to-all | bytes 327680 | tf_op jit(solution)/shard_map/all_to_all | solution.py:346
  31.3 0.8 %sum.1 = f32[8,8,256]{2,1,0:T(8,128)} custom-call(bf16[16,40,128]{2,1,0:T(8,128)(2,1)S(1)} %all_to_all.11.back_ref, f32[64,256]{1,0:T(8,128)S(1)} %get-tuple-element.9.near_out_ref, bf16[64,256]{1,0:T(8,128)(2,1)S(1)} %get-tuple-element.10.place_ref, bf16[8,3,256,256]{3,2,1,0:T(8,128)(2,1)S(1)} %copy-done), custom_call_target="tpu_custom_call" | custom-call | flops 8388608 | bytes 131072 | tf_op jit(solution)/shard_map/sum/pallas_call | solution.py:347
  (1 shorter events, 0.0 us)
Async XLA Ops:
  0.0 0.8 %copy-start.3 = (bf16[8,8,256]{2,1,0:T(8,128)(2,1)S(1)}, bf16[8,8,256]{2,1,0:T(8,128)(2,1)}, u32[]{:S(2)}) copy-start(bf16[8,8,256]{2,1,0:T(8,128)(2,1)} %src_ref.3) | copy-start | bytes 98308
  0.0 0.8 %copy-start.7 = (s32[1,16,2]{1,2,0:T(2,128)S(1)}, s32[1,16,2]{1,2,0:T(2,128)}, u32[]{:S(2)}) copy-start(s32[1,16,2]{1,2,0:T(2,128)} %param.14) | copy-start | bytes 388
  0.0 0.8 %copy-start.6 = (s32[1,16,2]{1,2,0:T(2,128)S(1)}, s32[1,16,2]{1,2,0:T(2,128)}, u32[]{:S(2)}) copy-start(s32[1,16,2]{1,2,0:T(2,128)} %param.12) | copy-start | bytes 388
  0.8 16.3 %copy-start = (bf16[8,3,256,256]{3,2,1,0:T(8,128)(2,1)S(1)}, bf16[8,3,256,256]{3,2,1,0:T(8,128)(2,1)}, u32[]{:S(2)}) copy-start(bf16[8,3,256,256]{3,2,1,0:T(8,128)(2,1)} %near_ref.3) | copy-start | bytes 9437188
  0.8 16.3 %copy-start.1 = (bf16[256,32,256]{2,1,0:T(8,128)(2,1)S(1)}, bf16[256,32,256]{2,1,0:T(8,128)(2,1)}, u32[]{:S(2)}) copy-start(bf16[256,32,256]{2,1,0:T(8,128)(2,1)} %u_ref.1) | copy-start | bytes 12582916
  0.8 16.3 %copy-start.2 = (bf16[256,32,256]{2,1,0:T(8,128)(2,1)S(1)}, bf16[256,32,256]{2,1,0:T(8,128)(2,1)}, u32[]{:S(2)}) copy-start(bf16[256,32,256]{2,1,0:T(8,128)(2,1)} %v_ref.1) | copy-start | bytes 12582916
  0.8 16.3 %copy-start.4 = (s32[256]{0:T(256)S(1)}, s32[256]{0:T(256)}, u32[]{:S(2)}) copy-start(s32[256]{0:T(256)} %slots_any.1) | copy-start | bytes 3076
  0.8 16.3 %copy-start.5 = (s32[256]{0:T(256)S(1)}, s32[256]{0:T(256)}, u32[]{:S(2)}) copy-start(s32[256]{0:T(256)} %dests_any.1) | copy-start | bytes 3076
